TPU v7x, 768 devices: a whole 4x8x12 slice. The times are simulated.
768 devices in a mesh: tile: 32 (over z_lo, x, core), bulk: 24 (over y, z_hi).
Axes of the slice: x: 4, y: 8, z: 12 (z_hi: 3, z_lo: 4; z = z_hi * 4 + z_lo), core: 2. Of those that a mesh axis runs over, the one named last changes fastest.
Arguments:
- integrals: bfloat16 [2304, 256, 768], P(('tile', 'bulk')), may hold values from -0.21875 to 0.21875
- amplitudes: bfloat16 [4, 768, 1024], P(None, 'bulk', 'tile'), may hold values from -6 to 6
- residual_in: bfloat16 [2304, 256, 1024], P(('tile', 'bulk')), may hold values from -6 to 6
- tile_irrep: int32 [2304], replicated, may hold values from 0 to 3, as said below
Outputs:
- residual: bfloat16 [2304, 256, 1024], P(('tile', 'bulk'))
Inputs may be any that keep to these rules, and one draw needn't show every extreme that they name: tile_irrep never falls along the tiles, and every irrep labels at least 72 tiles.
All inputs are finite; a program needn't handle non-finite values.
Results may differ from a plain program's by a relative error of at most 0.001.
Values may be sent and summed in bfloat16 or wider, within the bound.
No kernel may reach another device: no remote copies, remote signals or barrier semaphores. Data moves between devices by JAX's collectives and lax.ppermute only.
A program may use at most 64 MiB of HBM per device.

v0:
```python
import jax
import jax.numpy as jnp
from jax import lax
from jax.sharding import Mesh
from jax.sharding import PartitionSpec as P

BULK = ("bulk_0", "bulk_1")
TILE_BULK = ("tile", "bulk_0", "bulk_1")


def gather_axes(value, axes, dim):
    if not axes:
        return value
    nearer = lax.all_gather(value, axes[-1], axis=dim, tiled=True)
    return gather_axes(nearer, axes[:-1], dim)


def local(integrals, amplitudes, residual_in, tile_irrep):
    tile_dev = integrals.shape[0]
    row_index = lax.axis_index("tile")
    col_index = lax.axis_index(BULK)
    bulk_count = lax.axis_size(BULK)
    tile_count = lax.axis_size("tile")
    first_tile = (row_index * bulk_count + col_index) * tile_dev
    local_irrep = lax.dynamic_slice_in_dim(tile_irrep, first_tile, tile_dev, 0)
    irrep_grid = tile_irrep.reshape(tile_count, tile_dev * bulk_count)
    wanted = jnp.stack([irrep_grid[:, 0], irrep_grid[:, -1]], axis=1)
    outgoing = jnp.take(amplitudes, wanted, axis=0)
    incoming = lax.all_to_all(outgoing, "tile", split_axis=0, concat_axis=3, tiled=True)
    own_pair = lax.dynamic_index_in_dim(wanted, row_index, 0, keepdims=False)
    choose_slot = (local_irrep == own_pair[1]).astype(jnp.int32)
    picked = jnp.take(gather_axes(incoming[0], BULK, 1), choose_slot, axis=0)
    product = jnp.einsum("trc,tcp->trp", integrals, picked, preferred_element_type=jnp.float32)
    return (residual_in.astype(jnp.float32) + product).astype(jnp.bfloat16)


def solution(mesh):
    finer = Mesh(mesh.devices.reshape(mesh.shape["tile"], 8, 3), ("tile", "bulk_0", "bulk_1"))
    placed = (P(TILE_BULK, None, None), P(None, BULK, "tile"), P(TILE_BULK, None, None), P())
    return jax.shard_map(
        local, mesh=finer, in_specs=placed, out_specs=P(TILE_BULK, None, None), check_vma=False
    )
```

profile of v0, /device:TPU:1, one launch (start us, length us, event | category | flops | bytes accessed | tf_op | source)
XLA Modules:
  0.0 123.0 jit_solution(7010637814316597288)
XLA Ops:
  6.5 0.9 reshape.104
  7.4 0.2 slice_reduce_fusion.1
  7.6 0.1 copy.22
  7.7 0.1 copy.23
  7.8 0.1 copy.24
  7.9 0.1 copy.25
  8.0 0.1 reshape.107
  8.1 1.4 %gather_fusion = bf16[64,32,32]{2,1,0:T(8,128)(2,1)S(1)} fusion(bf16[4,32,32]{2,1,0:T(8,128)(2,1)} %param.5, s32[1024]{0:T(1024)S(1)} %pad_clamp_fusion.1), kind=kCustom, calls=%fused_computation | custom fusion | bytes 262400 | tf_op jit(solution)/shard_map/jit(_take)/gather | solution.py:28
  9.5 0.1 broadcast_select_fusion
  9.7 0.5 reshape.125
  10.2 21.8 %all_to_all.15 = bf16[32,2,1024]{2,1,0:T(2,128)(2,1)S(1)} all-to-all(bf16[32,2,1024]{2,1,0:T(2,128)(2,1)S(1)} %reshape.125), channel_id=1, replica_groups=mesh['tile'=32,'bulk_0'=8,'bulk_1'=3] {'tile'}, dimensions={0} | all-to-all | bytes 262144 | tf_op jit(solution)/shard_map/all_to_all | solution.py:29
  32.0 0.3 reshape.126
  32.3 0.3 copy.26
  32.6 0.5 squeeze.9
  33.2 24.0 %all_gather.6 = bf16[2,96,1024]{2,1,0:T(8,128)(2,1)} all-gather(bf16[2,32,1024]{2,1,0:T(8,128)(2,1)S(1)} %squeeze.9), channel_id=1, replica_groups=mesh['tile'=32,'bulk_0'=8,'bulk_1'=3] {'bulk_1'}, dimensions={1}, use_global_device_ids=true | all-gather | bytes 524288 | tf_op jit(solution)/shard_map/all_gather | solution.py:14
  57.1 0.0 all-gather.2.cloned.1.call-update
  57.2 0.1 constant_dynamic-slice_fusion
  57.3 0.5 slice.12
  57.8 1.7 %copy.21 = bf16[3,256,1024]{1,2,0:T(8,128)(2,1)S(1)} copy(bf16[3,256,1024]{2,1,0:T(8,128)(2,1)} %param.6) | data formatting | bytes 3145728 | tf_op args[2]
  59.5 1.4 %compare_and_fusion.1 = (pred[3]{0:T(512)(128)(4,1)S(1)}, s32[3]{0:T(128)S(1)}) fusion(s32[]{:T(128)} %bitcast, s32[2304]{0:T(1024)} %param.7, s32[]{:T(128)S(6)} %select_n.36), kind=kLoop, calls=%fused_computation.15 | loop fusion | flops 24 | bytes 35 | tf_op jit(solution)/shard_map/jit(_take)/and | solution.py:32
  61.0 42.2 %all-gather.2.cloned.1.call-done = bf16[2,768,1024]{2,1,0:T(8,128)(2,1)} async-done(((bf16[2,96,1024]{2,1,0:T(8,128)(2,1)}), bf16[2,768,1024]{2,1,0:T(8,128)(2,1)}) %all-gather.2.cloned.1.call-update) | async-done | bytes 3145744 | tf_op jit(solution)/shard_map/all_gather | solution.py:14
  103.1 5.0 %gather_fusion.1 = bf16[3,768,1024]{2,1,0:T(8,128)(2,1)} fusion(bf16[2,768,1024]{2,1,0:T(8,128)(2,1)} %all-gather.2.cloned.1.call-done, s32[1024]{0:T(1024)S(1)} %pad_clamp_fusion), kind=kCustom, calls=%fused_computation.1 | custom fusion | bytes 9437196 | tf_op jit(solution)/shard_map/jit(_take)/gather | solution.py:32
  108.2 5.4 %fusion.3 = bf16[3,256,1024]{1,2,0:T(8,128)(2,1)} fusion(bf16[3,256,1024]{1,2,0:T(8,128)(2,1)S(1)} %copy.21, bf16[3,256,768]{2,1,0:T(8,128)(2,1)S(1)} %copy-done, bf16[3,768,1024]{2,1,0:T(8,128)(2,1)} %gather_fusion.1, pred[3]{0:T(512)(128)(4,1)S(1)} %get-tuple-element.7), kind=kOutput, calls=%fused_computation.6 | convolution fusion | flops 1212678144 | bytes 9043971 | tf_op jit(solution)/shard_map/trc,tcp->trp/dot_general | solution.py:33
  113.6 2.6 %copy.28 = bf16[3,256,1024]{2,1,0:T(8,128)(2,1)} copy(bf16[3,256,1024]{1,2,0:T(8,128)(2,1)} %fusion.3) | data formatting | bytes 3145728 | tf_op jit(solution)/shard_map/convert_element_type | solution.py:34
  (8 shorter events, 0.1 us)
Async XLA Ops:
  6.5 101.6 %copy-start = (bf16[3,256,768]{2,1,0:T(8,128)(2,1)S(1)}, bf16[3,256,768]{2,1,0:T(8,128)(2,1)}, u32[]{:S(2)}) copy-start(bf16[3,256,768]{2,1,0:T(8,128)(2,1)} %param.4) | copy-start | bytes 3538948
  6.5 96.6 %all-gather.2.cloned.1.call-start = ((), (), s32[]{:S(2)}) async-start(), calls=%async_computation.1 | async-start | bytes 3538944 | tf_op jit(solution)/shard_map/all_gather | solution.py:14
Sparse Core Ops, SparseCore 0:
  57.3 45.8 all-gather.1
where the time goes:
time: 123 us
  blocking collectives  45.8 us (37%)
  waiting for transfers between devices  42.2 us (34%)
  local copies, waits for them, and re-layouts  14.5 us (12%)
  between operations  13.5 us (11%)
  matrix products  5.41 us (4%)
  other arithmetic  1.62 us (1%)
    all_gather x1, waiting for transfers between devices, gather_axes(): nearer = lax.all_gather(value, axes[-1], axis=dim, tiled=True)  42.2 us
    all_gather x1, blocking collectives, gather_axes(): nearer = lax.all_gather(value, axes[-1], axis=dim, tiled=True)  24 us
    all_to_all x1, blocking collectives, local(): lax.all_to_all(outgoing, 'tile', split_axis=0, concat_axis=3, tiled=True)  21.8 us
    dot_general x1, matrix products, local(): jnp.einsum('trc,tcp->trp', integrals, picked, preferred_element_type=jnp....  5.41 us
    gather x1, local copies, waits for them, and re-layouts, local(): picked = jnp.take(gather_axes(incoming[0], BULK, 1), choose_slot, axis=0)  5.01 us
    convert_element_type x1, local copies, waits for them, and re-layouts, local(): return (residual_in.astype(jnp.float32) + product).astype(jnp.bfloat16)  2.58 us
    unnamed x5, local copies, waits for them, and re-layouts  2.48 us
  transfers between devices with their start and end apart: 1, of which 1 were waited for; matrix products, arithmetic and copies ran while one was open for 3% of the time, Pallas kernels for 0%

commit v1 on v0

v1 whole, which is shorter than its diff:
```python
import functools

import jax
import jax.numpy as jnp
from jax import lax
from jax.experimental import pallas as pl
from jax.experimental.pallas import tpu as pltpu
from jax.sharding import Mesh
from jax.sharding import PartitionSpec as P

CHIP_CORE = ("chip", "core")
TILE_BULK = ("chip", "core", "bulk_0", "bulk_1")
BULK = ("bulk_0", "bulk_1")


def shift(value, axis, step):
    size = lax.axis_size(axis)
    return lax.ppermute(value, axis, [(i, (i + step) % size) for i in range(size)])


def half_kernel(where_ref, integrals_ref, block_ref, previous_ref, out_ref):
    product = jnp.dot(integrals_ref[0], block_ref[0], preferred_element_type=jnp.float32)
    out_ref[0] = (previous_ref[0].astype(jnp.float32) + product).astype(out_ref.dtype)


def second_kernel(where_ref, integrals_ref, block_ref, previous_ref, so_far_ref, out_ref):
    half_kernel(where_ref, integrals_ref, block_ref, previous_ref, out_ref)


def add_half(where, integrals, block, residual_in, so_far=None):
    tiles, rows, depth = integrals.shape
    half = block.shape[2]
    strip = pl.BlockSpec((1, rows, half), lambda t, w: (t, 0, w[tiles]))
    in_specs = [
        pl.BlockSpec((1, rows, depth), lambda t, w: (t, 0, 0)),
        pl.BlockSpec((1, depth, half), lambda t, w: (w[t], 0, 0)),
        strip,
    ]
    operands = [where, integrals, block, residual_in]
    aliases = {}
    if so_far is not None:
        in_specs.append(pl.BlockSpec(memory_space=pl.ANY))
        operands.append(so_far)
        aliases = {4: 0}
    return pl.pallas_call(
        half_kernel if so_far is None else second_kernel,
        grid_spec=pltpu.PrefetchScalarGridSpec(
            num_scalar_prefetch=1, grid=(tiles,), in_specs=in_specs, out_specs=strip
        ),
        out_shape=jax.ShapeDtypeStruct(residual_in.shape, residual_in.dtype),
        input_output_aliases=aliases,
        cost_estimate=pl.CostEstimate(
            flops=2 * tiles * rows * depth * half, bytes_accessed=4_000_000, transcendentals=0
        ),
        compiler_params=pltpu.CompilerParams(vmem_limit_bytes=24 * 2**20),
    )(*operands)


def select(amplitudes, labels):
    flat = amplitudes.reshape(amplitudes.shape[0], -1)
    labels = labels[..., None]
    chosen = flat[0]
    for irrep in range(1, flat.shape[0]):
        chosen = jnp.where(labels == irrep, flat[irrep], chosen)
    return chosen


def with_slots(slots, integrals, amplitudes, residual_in, first, last, where):
    depth, width = amplitudes.shape[1:]
    chips, cores = lax.axis_size("chip"), lax.axis_size("core")
    core = lax.axis_index("core")
    wanted = jnp.minimum(first[:, None] + jnp.arange(slots, dtype=jnp.int32), last[:, None])
    wanted = jnp.repeat(wanted, cores, axis=0)
    outgoing = select(amplitudes, wanted)
    incoming = lax.all_to_all(outgoing, CHIP_CORE, split_axis=0, concat_axis=0, tiled=True)
    half = chips * cores // 2
    mine = lax.dynamic_slice_in_dim(incoming, core * half, half, 0)
    mine = mine.reshape(half, slots, depth, width).transpose(1, 2, 0, 3).reshape(slots, depth, half * width)
    z_size, z = lax.axis_size("bulk_1"), lax.axis_index("bulk_1")
    group = jnp.zeros((slots, z_size, depth, half * width), mine.dtype)
    group = lax.dynamic_update_slice_in_dim(group, mine[:, None], z, 1)
    for step in range(1, z_size):
        got = shift(mine, "bulk_1", step)
        group = lax.dynamic_update_slice_in_dim(group, got[:, None], lax.rem(z - step + z_size, z_size), 1)
    group = group.reshape(slots, z_size * depth, half * width)
    y_size, y = lax.axis_size("bulk_0"), lax.axis_index("bulk_0")
    whole = jnp.zeros((slots, y_size, z_size * depth, half * width), mine.dtype)
    whole = lax.dynamic_update_slice_in_dim(whole, group[:, None], y, 1)
    up, down = group, group
    for step in range(1, y_size // 2 + 1):
        up = shift(up, "bulk_0", 1)
        whole = lax.dynamic_update_slice_in_dim(whole, up[:, None], lax.rem(y - step + y_size, y_size), 1)
        if 2 * step < y_size:
            down = shift(down, "bulk_0", -1)
            whole = lax.dynamic_update_slice_in_dim(whole, down[:, None], lax.rem(y + step, y_size), 1)
    whole = whole.reshape(slots, y_size * z_size * depth, half * width)
    other = shift(whole, "core", 1)
    out = add_half(jnp.append(where, core), integrals, whole, residual_in)
    return add_half(jnp.append(where, 1 - core), integrals, other, residual_in, out)


def local(integrals, amplitudes, residual_in, tile_irrep):
    tile_dev = integrals.shape[0]
    chips, cores = lax.axis_size("chip"), lax.axis_size("core")
    bulk_count = lax.axis_size(BULK)
    chip, core = lax.axis_index("chip"), lax.axis_index("core")
    per_chip = tile_irrep.reshape(chips, -1)
    first, last = per_chip[:, 0], per_chip[:, -1]
    first_tile = ((chip * cores + core) * bulk_count + lax.axis_index(BULK)) * tile_dev
    labels = lax.dynamic_slice_in_dim(tile_irrep, first_tile, tile_dev, 0)
    where = labels - lax.dynamic_slice_in_dim(first, chip, 1, 0)
    operands = (integrals, amplitudes, residual_in, first, last, where)
    return lax.cond(
        jnp.max(last - first) > 1,
        functools.partial(with_slots, 3),
        functools.partial(with_slots, 2),
        *operands,
    )


def solution(mesh):
    tile, bulk = mesh.shape["tile"], mesh.shape["bulk"]
    finer = Mesh(mesh.devices.reshape(tile // 2, 2, bulk // 3, 3), TILE_BULK)
    placed = (P(TILE_BULK, None, None), P(None, BULK, CHIP_CORE), P(TILE_BULK, None, None), P())
    return jax.shard_map(
        local, mesh=finer, in_specs=placed, out_specs=P(TILE_BULK, None, None), check_vma=False
    )
```

time: 123 us -> 100 us (0.81)
  starting transfers between devices: 0.01 us -> 52.9 us
  blocking collectives: 45.8 us -> 0 us
  between operations: 13.5 us -> 0.68 us
  waiting for transfers between devices: 42.2 us -> 30.4 us
  local copies, waits for them, and re-layouts: 14.5 us -> 4.73 us
  Pallas kernels: 0 us -> 7.29 us
  matrix products: 5.41 us -> 0 us
  other arithmetic: 1.62 us -> 3.13 us
    all_gather x1 -> x0, waiting for transfers between devices: 42.2 us -> none  [gather_axes(): nearer = lax.all_gather(value, axes[-1], axis=dim, tiled=True)]
    ppermute x0 -> x10, starting transfers between devices: none -> 38.9 us  [shift(): lax.ppermute(value, axis, [(i, (i + step) % size) for i in range(size)])]
    all_gather x1 -> x0, blocking collectives: 24 us -> none  [gather_axes(): nearer = lax.all_gather(value, axes[-1], axis=dim, tiled=True)]
    all_to_all x1 -> x0, blocking collectives: 21.8 us -> none  [local(): lax.all_to_all(outgoing, 'tile', split_axis=0, concat_axis=3, tiled=True)]
    ppermute x0 -> x10, waiting for transfers between devices: none -> 21.7 us  [shift(): lax.ppermute(value, axis, [(i, (i + step) % size) for i in range(size)])]
    all_to_all x0 -> x1, starting transfers between devices: none -> 14 us  [with_slots(): lax.all_to_all(outgoing, CHIP_CORE, split_axis=0, concat_axis=0, tiled=True)]
    all_to_all x0 -> x1, waiting for transfers between devices: none -> 8.62 us  [with_slots(): lax.all_to_all(outgoing, CHIP_CORE, split_axis=0, concat_axis=0, tiled=True)]
    pallas_call x0 -> x2, Pallas kernels: none -> 7.29 us  [add_half(): pl.pallas_call(half_kernel if so_far is None else second_kernel, grid_spe...]
  transfers between devices with their start and end apart: 1 -> 11, of which waited for: 1 -> 7; matrix products, arithmetic and copies ran while one was open for 3% -> 3% of each run, Pallas kernels for 0% -> 5%
where the time goes in v1:
time: 100 us; the launch traced here: 99.5 us
  starting transfers between devices  52.9 us (53%)
  waiting for transfers between devices  30.4 us (30%)
  Pallas kernels  7.29 us (7%)
  local copies, waits for them, and re-layouts  4.73 us (5%)
  other arithmetic  3.13 us (3%)
    ppermute x10, starting transfers between devices, shift(): lax.ppermute(value, axis, [(i, (i + step) % size) for i in range(size)])  38.9 us
    ppermute x10, waiting for transfers between devices, shift(): lax.ppermute(value, axis, [(i, (i + step) % size) for i in range(size)])  21.7 us
    all_to_all x1, starting transfers between devices, with_slots(): lax.all_to_all(outgoing, CHIP_CORE, split_axis=0, concat_axis=0, tiled=True)  14 us
    all_to_all x1, waiting for transfers between devices, with_slots(): lax.all_to_all(outgoing, CHIP_CORE, split_axis=0, concat_axis=0, tiled=True)  8.62 us
    pallas_call x2, Pallas kernels, add_half(): pl.pallas_call(half_kernel if so_far is None else second_kernel, grid_spe...  7.29 us
  transfers between devices with their start and end apart: 11, of which 7 were waited for; matrix products, arithmetic and copies ran while one was open for 3% of the time, Pallas kernels for 5%

profile of v1, /device:TPU:1, one launch (start us, length us, event | category | flops | bytes accessed | tf_op | source)
XLA Modules:
  0.0 99.5 jit_solution(7520177660850182809)
XLA Ops:
  0.0 0.8 reshape.129
  2.2 97.3 %conditional.1 = (bf16[3,256,1024]{2,1,0:T(8,128)(2,1)}) conditional(s32[]{:T(128)} %convert_element_type.3, (s32[2304]{0:T(1024)}, s32[16,1]{1,0:T(8,128)S(1)}, s32[16,1]{1,0:T(8,128)S(1)}, bf16[4,32,32]{2,1,0:T(8,128)(2,1)}, bf16[3,256,768]{2,1,0:T(8,128)(2,1)}, /*index=5*/bf16[3,256,1024]{2,1,0:T(8,128)(2,1)}, s32[16,1]{1,0:T(8,128)S(1)}, ...), branch_computations={%region_1.2_spmd, %region_2.3_spmd} | conditional | flops 1208254848 | bytes 47596244 | solution.py:113
  3.2 0.8 fusion.6
  4.3 0.9 broadcast_select_fusion.2
  5.2 14.0 %all-to-all-start = ((bf16[32,2,1024]{2,1,0:T(2,128)(2,1)}), bf16[32,2,1024]{2,1,0:T(2,128)(2,1)S(1)}, u32[]{:S(2)}, u32[]{:S(2)}) async-start(bf16[32,2,1024]{2,1,0:T(2,128)(2,1)} %broadcast_select_fusion.2), calls=%async_computation | async-start | bytes 262144 | tf_op jit(solution)/shard_map/cond/branch_0_fun/all_to_all | solution.py:75
  19.3 8.6 %all-to-all-done = bf16[32,2,1024]{2,1,0:T(2,128)(2,1)S(1)} async-done(((bf16[32,2,1024]{2,1,0:T(2,128)(2,1)}), bf16[32,2,1024]{2,1,0:T(2,128)(2,1)S(1)}, u32[]{:S(2)}, u32[]{:S(2)}) %all-to-all-start) | async-done | bytes 131104 | tf_op jit(solution)/shard_map/cond/branch_0_fun/all_to_all | solution.py:75
  28.8 7.6 %collective-permute-start = (bf16[2,32,512]{2,1,0:T(8,128)(2,1)S(1)}, bf16[2,32,512]{2,1,0:T(8,128)(2,1)S(1)}, u32[]{:S(2)}, u32[]{:S(2)}) collective-permute-start(bf16[2,32,512]{2,1,0:T(8,128)(2,1)S(1)} %reshape.115), channel_id=1, source_target_pairs={{0,1},{1,2},{2,0},{3,4},{4,5},{5,3},{6,7},{7,8},{8,6},{9,10},{10,1... | collective-permute-start | bytes 196616 | tf_op jit(solution)/shard_map/cond/branch_0_fun/ppermute | solution.py:18
  36.3 3.2 %collective-permute-start.1 = (bf16[2,32,512]{2,1,0:T(8,128)(2,1)S(1)}, bf16[2,32,512]{2,1,0:T(8,128)(2,1)S(1)}, u32[]{:S(2)}, u32[]{:S(2)}) collective-permute-start(bf16[2,32,512]{2,1,0:T(8,128)(2,1)S(1)} %reshape.115), channel_id=1, source_target_pairs={{0,2},{1,0},{2,1},{3,5},{4,3},{5,4},{6,8},{7,6},{8,7},{9,11},{10,9... | collective-permute-start | bytes 196616 | tf_op jit(solution)/shard_map/cond/branch_0_fun/ppermute | solution.py:18
  39.7 10.6 %collective-permute-done.1 = bf16[2,32,512]{2,1,0:T(8,128)(2,1)S(1)} collective-permute-done((bf16[2,32,512]{2,1,0:T(8,128)(2,1)S(1)}, bf16[2,32,512]{2,1,0:T(8,128)(2,1)S(1)}, u32[]{:S(2)}, u32[]{:S(2)}) %collective-permute-start.1) | collective-permute-done | bytes 65568 | tf_op jit(solution)/shard_map/cond/branch_0_fun/ppermute | solution.py:18
  50.3 3.2 %collective-permute-start.2 = (bf16[2,96,512]{2,1,0:T(8,128)(2,1)S(1)}, bf16[2,96,512]{2,1,0:T(8,128)(2,1)S(1)}, u32[]{:S(2)}, u32[]{:S(2)}) collective-permute-start(bf16[2,96,512]{2,1,0:T(8,128)(2,1)S(1)} %bitcast.127), channel_id=1, source_target_pairs={{0,3},{3,6},{6,9},{9,12},{12,15},{15,18},{18,21},{21,0},{1,4},{4,7... | collective-permute-start | bytes 589832 | tf_op jit(solution)/shard_map/cond/branch_0_fun/ppermute | solution.py:18
  53.5 3.8 %collective-permute-start.3 = (bf16[2,96,512]{2,1,0:T(8,128)(2,1)S(1)}, bf16[2,96,512]{2,1,0:T(8,128)(2,1)S(1)}, u32[]{:S(2)}, u32[]{:S(2)}) collective-permute-start(bf16[2,96,512]{2,1,0:T(8,128)(2,1)S(1)} %bitcast.128), channel_id=1, source_target_pairs={{0,21},{3,0},{6,3},{9,6},{12,9},{15,12},{18,15},{21,18},{1,22},{4,... | collective-permute-start | bytes 589832 | tf_op jit(solution)/shard_map/cond/branch_0_fun/ppermute | solution.py:18
  57.6 2.5 %collective-permute-done.2 = bf16[2,96,512]{2,1,0:T(8,128)(2,1)S(1)} collective-permute-done((bf16[2,96,512]{2,1,0:T(8,128)(2,1)S(1)}, bf16[2,96,512]{2,1,0:T(8,128)(2,1)S(1)}, u32[]{:S(2)}, u32[]{:S(2)}) %collective-permute-start.2) | collective-permute-done | bytes 196640 | tf_op jit(solution)/shard_map/cond/branch_0_fun/ppermute | solution.py:18
  60.1 1.9 %collective-permute-start.4 = (bf16[2,96,512]{2,1,0:T(8,128)(2,1)S(1)}, bf16[2,96,512]{2,1,0:T(8,128)(2,1)S(1)}, u32[]{:S(2)}, u32[]{:S(2)}) collective-permute-start(bf16[2,96,512]{2,1,0:T(8,128)(2,1)S(1)} %collective-permute-done.2), channel_id=1, source_target_pairs={{0,3},{3,6},{6,9},{9,12},{12,15},{15,18},{18,21},{21,0},{1,4},{4,7... | collective-permute-start | bytes 589832 | tf_op jit(solution)/shard_map/cond/branch_0_fun/ppermute | solution.py:18
  62.0 4.6 %collective-permute-start.5 = (bf16[2,96,512]{2,1,0:T(8,128)(2,1)S(1)}, bf16[2,96,512]{2,1,0:T(8,128)(2,1)S(1)}, u32[]{:S(2)}, u32[]{:S(2)}) collective-permute-start(bf16[2,96,512]{2,1,0:T(8,128)(2,1)S(1)} %collective-permute-done.3), channel_id=1, source_target_pairs={{0,21},{3,0},{6,3},{9,6},{12,9},{15,12},{18,15},{21,18},{1,22},{4,... | collective-permute-start | bytes 589832 | tf_op jit(solution)/shard_map/cond/branch_0_fun/ppermute | solution.py:18
  66.7 1.8 %collective-permute-done.4 = bf16[2,96,512]{2,1,0:T(8,128)(2,1)S(1)} collective-permute-done((bf16[2,96,512]{2,1,0:T(8,128)(2,1)S(1)}, bf16[2,96,512]{2,1,0:T(8,128)(2,1)S(1)}, u32[]{:S(2)}, u32[]{:S(2)}) %collective-permute-start.4) | collective-permute-done | bytes 196640 | tf_op jit(solution)/shard_map/cond/branch_0_fun/ppermute | solution.py:18
  68.5 1.9 %collective-permute-start.6 = (bf16[2,96,512]{2,1,0:T(8,128)(2,1)S(1)}, bf16[2,96,512]{2,1,0:T(8,128)(2,1)S(1)}, u32[]{:S(2)}, u32[]{:S(2)}) collective-permute-start(bf16[2,96,512]{2,1,0:T(8,128)(2,1)S(1)} %collective-permute-done.4), channel_id=1, source_target_pairs={{0,3},{3,6},{6,9},{9,12},{12,15},{15,18},{18,21},{21,0},{1,4},{4,7... | collective-permute-start | bytes 589832 | tf_op jit(solution)/shard_map/cond/branch_0_fun/ppermute | solution.py:18
  70.4 4.6 %collective-permute-start.7 = (bf16[2,96,512]{2,1,0:T(8,128)(2,1)S(1)}, bf16[2,96,512]{2,1,0:T(8,128)(2,1)S(1)}, u32[]{:S(2)}, u32[]{:S(2)}) collective-permute-start(bf16[2,96,512]{2,1,0:T(8,128)(2,1)S(1)} %collective-permute-done.5), channel_id=1, source_target_pairs={{0,21},{3,0},{6,3},{9,6},{12,9},{15,12},{18,15},{21,18},{1,22},{4,... | collective-permute-start | bytes 589832 | tf_op jit(solution)/shard_map/cond/branch_0_fun/ppermute | solution.py:18
  75.0 1.0 %collective-permute-done.6 = bf16[2,96,512]{2,1,0:T(8,128)(2,1)S(1)} collective-permute-done((bf16[2,96,512]{2,1,0:T(8,128)(2,1)S(1)}, bf16[2,96,512]{2,1,0:T(8,128)(2,1)S(1)}, u32[]{:S(2)}, u32[]{:S(2)}) %collective-permute-start.6) | collective-permute-done | bytes 196640 | tf_op jit(solution)/shard_map/cond/branch_0_fun/ppermute | solution.py:18
  76.1 1.9 %collective-permute-start.8 = (bf16[2,96,512]{2,1,0:T(8,128)(2,1)S(1)}, bf16[2,96,512]{2,1,0:T(8,128)(2,1)S(1)}, u32[]{:S(2)}, u32[]{:S(2)}) collective-permute-start(bf16[2,96,512]{2,1,0:T(8,128)(2,1)S(1)} %collective-permute-done.6), channel_id=1, source_target_pairs={{0,3},{3,6},{6,9},{9,12},{12,15},{15,18},{18,21},{21,0},{1,4},{4,7... | collective-permute-start | bytes 589832 | tf_op jit(solution)/shard_map/cond/branch_0_fun/ppermute | solution.py:18
  78.1 5.6 %collective-permute-done.8 = bf16[2,96,512]{2,1,0:T(8,128)(2,1)S(1)} collective-permute-done((bf16[2,96,512]{2,1,0:T(8,128)(2,1)S(1)}, bf16[2,96,512]{2,1,0:T(8,128)(2,1)S(1)}, u32[]{:S(2)}, u32[]{:S(2)}) %collective-permute-start.8) | collective-permute-done | bytes 196640 | tf_op jit(solution)/shard_map/cond/branch_0_fun/ppermute | solution.py:18
  83.7 6.3 %collective-permute-start.9 = (bf16[2,768,512]{2,1,0:T(8,128)(2,1)S(1)}, bf16[2,768,512]{2,1,0:T(8,128)(2,1)S(1)}, u32[]{:S(2)}, u32[]{:S(2)}) collective-permute-start(bf16[2,768,512]{2,1,0:T(8,128)(2,1)S(1)} %bitcast.120), channel_id=1, source_target_pairs={{0,24},{24,0},{1,25},{25,1},{2,26},{26,2},{3,27},{27,3},{4,28},{28... | collective-permute-start | bytes 4718600 | tf_op jit(solution)/shard_map/cond/branch_0_fun/ppermute | solution.py:18
  90.7 1.4 %dynamic-slice_subtract_fusion = s32[3]{0:T(128)S(1)} fusion(s32[2304]{0:T(1024)} %get-tuple-element.55, s32[]{:T(128)S(6)} %select_n.102, s32[]{:T(128)} %bitcast), kind=kLoop, calls=%fused_computation.22 | loop fusion | flops 3 | bytes 32 | tf_op jit(solution)/shard_map/sub | solution.py:111
  92.2 4.5 %branch_0_fun.2.so_far_ref = bf16[3,256,1024]{2,1,0:T(8,128)(2,1)} custom-call(s32[4]{0:T(128)S(1)} %get-tuple-element.218.where_ref, bf16[3,256,768]{2,1,0:T(8,128)(2,1)} %get-tuple-element.63.integrals_ref, bf16[2,768,512]{2,1,0:T(8,128)(2,1)S(1)} %bitcast.121, bf16[3,256,1024]{2,1,0:T(8,128)(2,1)} %get-tuple-element.65.previous_ref), custom_call_target="tpu_custom_call" | custom-call | flops 603979776 | bytes 4000000 | tf_op jit(solution)/shard_map/cond/branch_0_fun/pallas_call | solution.py:45
  96.7 2.8 %branch_0_fun.3 = bf16[3,256,1024]{2,1,0:T(8,128)(2,1)} custom-call(s32[4]{0:T(128)S(1)} %get-tuple-element.219.where_ref, bf16[3,256,768]{2,1,0:T(8,128)(2,1)S(1)} %copy-done.2, bf16[2,768,512]{2,1,0:T(8,128)(2,1)S(1)} %collective-permute-done.9.block_ref, bf16[3,256,1024]{2,1,0:T(8,128)(2,1)S(1)} %copy-done, ...), custom_call_target="tpu_custom_call", output_to_operand_aliasing={{}: (4, {})} | custom-call | flops 603979776 | bytes 4000000 | tf_op jit(solution)/shard_map/cond/branch_0_fun/pallas_call | solution.py:45
  (48 shorter events, 4.1 us)
Async XLA Ops:
  5.2 22.7 %all-to-all-start = ((bf16[32,2,1024]{2,1,0:T(2,128)(2,1)}), bf16[32,2,1024]{2,1,0:T(2,128)(2,1)S(1)}, u32[]{:S(2)}, u32[]{:S(2)}) async-start(bf16[32,2,1024]{2,1,0:T(2,128)(2,1)} %broadcast_select_fusion.2), calls=%async_computation | async-start | bytes 262144 | tf_op jit(solution)/shard_map/cond/branch_0_fun/all_to_all | solution.py:75
  28.8 11.0 %collective-permute-start = (bf16[2,32,512]{2,1,0:T(8,128)(2,1)S(1)}, bf16[2,32,512]{2,1,0:T(8,128)(2,1)S(1)}, u32[]{:S(2)}, u32[]{:S(2)}) collective-permute-start(bf16[2,32,512]{2,1,0:T(8,128)(2,1)S(1)} %reshape.115), channel_id=1, source_target_pairs={{0,1},{1,2},{2,0},{3,4},{4,5},{5,3},{6,7},{7,8},{8,6},{9,10},{10,1... | collective-permute-start | bytes 196616 | tf_op jit(solution)/shard_map/cond/branch_0_fun/ppermute | solution.py:18
  36.3 13.9 %collective-permute-start.1 = (bf16[2,32,512]{2,1,0:T(8,128)(2,1)S(1)}, bf16[2,32,512]{2,1,0:T(8,128)(2,1)S(1)}, u32[]{:S(2)}, u32[]{:S(2)}) collective-permute-start(bf16[2,32,512]{2,1,0:T(8,128)(2,1)S(1)} %reshape.115), channel_id=1, source_target_pairs={{0,2},{1,0},{2,1},{3,5},{4,3},{5,4},{6,8},{7,6},{8,7},{9,11},{10,9... | collective-permute-start | bytes 196616 | tf_op jit(solution)/shard_map/cond/branch_0_fun/ppermute | solution.py:18
  50.3 9.8 %collective-permute-start.2 = (bf16[2,96,512]{2,1,0:T(8,128)(2,1)S(1)}, bf16[2,96,512]{2,1,0:T(8,128)(2,1)S(1)}, u32[]{:S(2)}, u32[]{:S(2)}) collective-permute-start(bf16[2,96,512]{2,1,0:T(8,128)(2,1)S(1)} %bitcast.127), channel_id=1, source_target_pairs={{0,3},{3,6},{6,9},{9,12},{12,15},{15,18},{18,21},{21,0},{1,4},{4,7... | collective-permute-start | bytes 589832 | tf_op jit(solution)/shard_map/cond/branch_0_fun/ppermute | solution.py:18
  53.5 8.5 %collective-permute-start.3 = (bf16[2,96,512]{2,1,0:T(8,128)(2,1)S(1)}, bf16[2,96,512]{2,1,0:T(8,128)(2,1)S(1)}, u32[]{:S(2)}, u32[]{:S(2)}) collective-permute-start(bf16[2,96,512]{2,1,0:T(8,128)(2,1)S(1)} %bitcast.128), channel_id=1, source_target_pairs={{0,21},{3,0},{6,3},{9,6},{12,9},{15,12},{18,15},{21,18},{1,22},{4,... | collective-permute-start | bytes 589832 | tf_op jit(solution)/shard_map/cond/branch_0_fun/ppermute | solution.py:18
  60.1 8.4 %collective-permute-start.4 = (bf16[2,96,512]{2,1,0:T(8,128)(2,1)S(1)}, bf16[2,96,512]{2,1,0:T(8,128)(2,1)S(1)}, u32[]{:S(2)}, u32[]{:S(2)}) collective-permute-start(bf16[2,96,512]{2,1,0:T(8,128)(2,1)S(1)} %collective-permute-done.2), channel_id=1, source_target_pairs={{0,3},{3,6},{6,9},{9,12},{12,15},{15,18},{18,21},{21,0},{1,4},{4,7... | collective-permute-start | bytes 589832 | tf_op jit(solution)/shard_map/cond/branch_0_fun/ppermute | solution.py:18
  62.0 8.4 %collective-permute-start.5 = (bf16[2,96,512]{2,1,0:T(8,128)(2,1)S(1)}, bf16[2,96,512]{2,1,0:T(8,128)(2,1)S(1)}, u32[]{:S(2)}, u32[]{:S(2)}) collective-permute-start(bf16[2,96,512]{2,1,0:T(8,128)(2,1)S(1)} %collective-permute-done.3), channel_id=1, source_target_pairs={{0,21},{3,0},{6,3},{9,6},{12,9},{15,12},{18,15},{21,18},{1,22},{4,... | collective-permute-start | bytes 589832 | tf_op jit(solution)/shard_map/cond/branch_0_fun/ppermute | solution.py:18
  68.5 7.6 %collective-permute-start.6 = (bf16[2,96,512]{2,1,0:T(8,128)(2,1)S(1)}, bf16[2,96,512]{2,1,0:T(8,128)(2,1)S(1)}, u32[]{:S(2)}, u32[]{:S(2)}) collective-permute-start(bf16[2,96,512]{2,1,0:T(8,128)(2,1)S(1)} %collective-permute-done.4), channel_id=1, source_target_pairs={{0,3},{3,6},{6,9},{9,12},{12,15},{15,18},{18,21},{21,0},{1,4},{4,7... | collective-permute-start | bytes 589832 | tf_op jit(solution)/shard_map/cond/branch_0_fun/ppermute | solution.py:18
  70.4 7.6 %collective-permute-start.7 = (bf16[2,96,512]{2,1,0:T(8,128)(2,1)S(1)}, bf16[2,96,512]{2,1,0:T(8,128)(2,1)S(1)}, u32[]{:S(2)}, u32[]{:S(2)}) collective-permute-start(bf16[2,96,512]{2,1,0:T(8,128)(2,1)S(1)} %collective-permute-done.5), channel_id=1, source_target_pairs={{0,21},{3,0},{6,3},{9,6},{12,9},{15,12},{18,15},{21,18},{1,22},{4,... | collective-permute-start | bytes 589832 | tf_op jit(solution)/shard_map/cond/branch_0_fun/ppermute | solution.py:18
  76.1 7.6 %collective-permute-start.8 = (bf16[2,96,512]{2,1,0:T(8,128)(2,1)S(1)}, bf16[2,96,512]{2,1,0:T(8,128)(2,1)S(1)}, u32[]{:S(2)}, u32[]{:S(2)}) collective-permute-start(bf16[2,96,512]{2,1,0:T(8,128)(2,1)S(1)} %collective-permute-done.6), channel_id=1, source_target_pairs={{0,3},{3,6},{6,9},{9,12},{12,15},{15,18},{18,21},{21,0},{1,4},{4,7... | collective-permute-start | bytes 589832 | tf_op jit(solution)/shard_map/cond/branch_0_fun/ppermute | solution.py:18
  83.7 13.0 %collective-permute-start.9 = (bf16[2,768,512]{2,1,0:T(8,128)(2,1)S(1)}, bf16[2,768,512]{2,1,0:T(8,128)(2,1)S(1)}, u32[]{:S(2)}, u32[]{:S(2)}) collective-permute-start(bf16[2,768,512]{2,1,0:T(8,128)(2,1)S(1)} %bitcast.120), channel_id=1, source_target_pairs={{0,24},{24,0},{1,25},{25,1},{2,26},{26,2},{3,27},{27,3},{4,28},{28... | collective-permute-start | bytes 4718600 | tf_op jit(solution)/shard_map/cond/branch_0_fun/ppermute | solution.py:18
  92.2 4.5 %copy-start = (bf16[3,256,1024]{2,1,0:T(8,128)(2,1)S(1)}, bf16[3,256,1024]{2,1,0:T(8,128)(2,1)}, u32[]{:S(2)}) copy-start(bf16[3,256,1024]{2,1,0:T(8,128)(2,1)} %get-tuple-element.65.previous_ref) | copy-start | bytes 4718596 | tf_op jit(solution)/shard_map/cond
  92.2 4.5 %copy-start.2 = (bf16[3,256,768]{2,1,0:T(8,128)(2,1)S(1)}, bf16[3,256,768]{2,1,0:T(8,128)(2,1)}, u32[]{:S(2)}) copy-start(bf16[3,256,768]{2,1,0:T(8,128)(2,1)} %get-tuple-element.63.integrals_ref) | copy-start | bytes 3538948 | tf_op jit(solution)/shard_map/cond

commit v2 on v0

v2 whole, which is shorter than its diff:
```python
import functools

import jax
import jax.numpy as jnp
from jax import lax
from jax.experimental import pallas as pl
from jax.experimental.pallas import tpu as pltpu
from jax.sharding import Mesh
from jax.sharding import PartitionSpec as P

CHIP_CORE = ("chip", "core")
TILE_BULK = ("chip", "core", "bulk_0", "bulk_1")
BULK = ("bulk_0", "bulk_1")
VMEM = pl.BlockSpec(memory_space=pltpu.VMEM)
SMEM = pl.BlockSpec(memory_space=pltpu.SMEM)


def shift(value, axis, step):
    size = lax.axis_size(axis)
    return lax.ppermute(value, axis, [(i, (i + step) % size) for i in range(size)])


def choose_kernel(slots, chips, tiles, bulk_0, bulk_1, labels_ref, packed_ref, outgoing_ref, where_ref):
    per_chip = labels_ref.shape[0] // chips
    rows = packed_ref.shape[1]
    most = jnp.int32(0)
    for chip in range(chips):
        first, last = labels_ref[chip * per_chip], labels_ref[(chip + 1) * per_chip - 1]
        most = jnp.maximum(most, last - first)
        for slot in range(slots):
            block = packed_ref[jnp.minimum(first + slot, last)]
            for core in range(2):
                outgoing_ref[2 * chip + core, pl.ds(slot * rows, rows), :] = block
    own = lax.axis_index("chip")
    row = own * 2 + lax.axis_index("core")
    column = lax.axis_index("bulk_0") * bulk_1 + lax.axis_index("bulk_1")
    first_tile = (row * (bulk_0 * bulk_1) + column) * tiles
    for t in range(tiles):
        where_ref[t] = labels_ref[first_tile + t] - labels_ref[own * per_chip]
    where_ref[tiles] = most + 1


def choose(slots, labels, packed, tiles):
    chips = lax.axis_size("chip")
    rows, lanes = packed.shape[1:]
    body = functools.partial(
        choose_kernel, slots, chips, tiles, lax.axis_size("bulk_0"), lax.axis_size("bulk_1")
    )
    return pl.pallas_call(
        body,
        in_specs=[SMEM, VMEM],
        out_specs=(VMEM, SMEM),
        out_shape=(
            jax.ShapeDtypeStruct((2 * chips, slots * rows, lanes), packed.dtype),
            jax.ShapeDtypeStruct((tiles + 1,), jnp.int32),
        ),
    )(labels, packed)


def ladder_kernel(where_ref, integrals_ref, own_ref, other_ref, previous_ref, out_ref, strip_ref, sems):
    tiles = integrals_ref.shape[0]
    half = own_ref.shape[2]
    core = lax.axis_index("core")
    chunk = 256
    copies = []
    for t in range(tiles):
        slot = where_ref[t]
        for block_ref, side in ((own_ref, core), (other_ref, 1 - core)):
            for begin in range(0, half, chunk):
                columns = pl.ds(pl.multiple_of(side * half + begin, chunk), chunk)
                product = jnp.dot(
                    integrals_ref[t], block_ref[slot, :, begin : begin + chunk], preferred_element_type=jnp.float32
                )
                total = previous_ref[t, :, columns].astype(jnp.float32) + product
                strip_ref[t, :, columns] = total.astype(strip_ref.dtype)
        copies.append(pltpu.make_async_copy(strip_ref.at[t], out_ref.at[t], sems.at[t]))
        copies[-1].start()
    for copy in copies:
        copy.wait()


def ladder(where, integrals, own, other, residual_in):
    tiles, rows, depth = integrals.shape
    return pl.pallas_call(
        ladder_kernel,
        in_specs=[SMEM, VMEM, VMEM, VMEM, VMEM],
        out_specs=pl.BlockSpec(memory_space=pl.ANY),
        out_shape=jax.ShapeDtypeStruct(residual_in.shape, residual_in.dtype),
        scratch_shapes=[
            pltpu.VMEM(residual_in.shape, residual_in.dtype),
            pltpu.SemaphoreType.DMA((tiles,)),
        ],
        compiler_params=pltpu.CompilerParams(vmem_limit_bytes=24 * 2**20),
    )(where, integrals, own, other, residual_in)


def with_slots(slots, outgoing, where, integrals, residual_in, depth, width):
    chips = lax.axis_size("chip")
    core = lax.axis_index("core")
    incoming = lax.all_to_all(outgoing, CHIP_CORE, split_axis=0, concat_axis=0, tiled=True)
    half = chips
    mine = lax.dynamic_slice_in_dim(incoming, core * half, half, 0)
    parts = incoming.shape[2] // width
    mine = mine.reshape(half, slots, depth // parts, parts, width).transpose(1, 2, 3, 0, 4)
    mine = mine.reshape(slots, depth, half * width)
    z_size, z = lax.axis_size("bulk_1"), lax.axis_index("bulk_1")
    group = jnp.zeros((slots, z_size, depth, half * width), mine.dtype)
    group = lax.dynamic_update_slice_in_dim(group, mine[:, None], z, 1)
    for step in range(1, z_size):
        got = shift(mine, "bulk_1", step)
        group = lax.dynamic_update_slice_in_dim(group, got[:, None], lax.rem(z - step + z_size, z_size), 1)
    group = group.reshape(slots, z_size * depth, half * width)
    y_size, y = lax.axis_size("bulk_0"), lax.axis_index("bulk_0")
    whole = jnp.zeros((slots, y_size, z_size * depth, half * width), mine.dtype)
    whole = lax.dynamic_update_slice_in_dim(whole, group[:, None], y, 1)
    up, down = group, group
    for step in range(1, y_size // 2):
        up = shift(up, "bulk_0", 1)
        whole = lax.dynamic_update_slice_in_dim(whole, up[:, None], lax.rem(y - step + y_size, y_size), 1)
        down = shift(down, "bulk_0", -1)
        whole = lax.dynamic_update_slice_in_dim(whole, down[:, None], lax.rem(y + step, y_size), 1)
    up = shift(up, "bulk_0", 1)
    far = lax.rem(y + y_size // 2, y_size)
    other = shift(whole, "core", 1)
    whole = lax.dynamic_update_slice_in_dim(whole, up[:, None], far, 1)
    other = lax.dynamic_update_slice_in_dim(other, shift(up, "core", 1)[:, None], far, 1)
    flat = (slots, y_size * z_size * depth, half * width)
    return ladder(where, integrals, whole.reshape(flat), other.reshape(flat), residual_in)


def local(integrals, amplitudes, residual_in, tile_irrep):
    tiles = integrals.shape[0]
    irreps, depth, width = amplitudes.shape
    parts = 128 // width
    packed = amplitudes.reshape(irreps, depth // parts, parts * width)
    outgoing, where = choose(2, tile_irrep, packed, tiles)

    def two():
        return with_slots(2, outgoing, where, integrals, residual_in, depth, width)

    def three():
        return with_slots(3, *choose(3, tile_irrep, packed, tiles), integrals, residual_in, depth, width)

    return lax.cond(where[tiles] > 2, three, two)


def solution(mesh):
    tile, bulk = mesh.shape["tile"], mesh.shape["bulk"]
    finer = Mesh(mesh.devices.reshape(tile // 2, 2, bulk // 3, 3), TILE_BULK)
    placed = (P(TILE_BULK, None, None), P(None, BULK, CHIP_CORE), P(TILE_BULK, None, None), P())
    return jax.shard_map(
        local, mesh=finer, in_specs=placed, out_specs=P(TILE_BULK, None, None), check_vma=False
    )
```

time: 123 us -> 99.9 us (0.81)
  starting transfers between devices: 0.01 us -> 54.7 us
  blocking collectives: 45.8 us -> 0 us
  between operations: 13.5 us -> 0.67 us
  local copies, waits for them, and re-layouts: 14.5 us -> 2.59 us
  waiting for transfers between devices: 42.2 us -> 35.5 us
  Pallas kernels: 0 us -> 5.56 us
  matrix products: 5.41 us -> 0 us
  other arithmetic: 1.62 us -> 0 us
    all_gather x1 -> x0, waiting for transfers between devices: 42.2 us -> none  [gather_axes(): nearer = lax.all_gather(value, axes[-1], axis=dim, tiled=True)]
    ppermute x0 -> x11, starting transfers between devices: none -> 40.6 us  [shift(): lax.ppermute(value, axis, [(i, (i + step) % size) for i in range(size)])]
    ppermute x0 -> x11, waiting for transfers between devices: none -> 26.8 us  [shift(): lax.ppermute(value, axis, [(i, (i + step) % size) for i in range(size)])]
    all_gather x1 -> x0, blocking collectives: 24 us -> none  [gather_axes(): nearer = lax.all_gather(value, axes[-1], axis=dim, tiled=True)]
    all_to_all x1 -> x0, blocking collectives: 21.8 us -> none  [local(): lax.all_to_all(outgoing, 'tile', split_axis=0, concat_axis=3, tiled=True)]
    all_to_all x0 -> x1, starting transfers between devices: none -> 14 us  [with_slots(): lax.all_to_all(outgoing, CHIP_CORE, split_axis=0, concat_axis=0, tiled=True)]
    all_to_all x0 -> x1, waiting for transfers between devices: none -> 8.62 us  [with_slots(): lax.all_to_all(outgoing, CHIP_CORE, split_axis=0, concat_axis=0, tiled=True)]
    gather x2 -> x0, local copies, waits for them, and re-layouts: 6.42 us -> none  [the longest x1 5.01 us: local(): picked = jnp.take(gather_axes(incoming[0], BULK, 1), choose_slot, axis=0)]
  transfers between devices with their start and end apart: 1 -> 12, of which waited for: 1 -> 9; matrix products, arithmetic and copies ran while one was open for 3% -> 0% of each run, Pallas kernels for 0% -> 0%
where the time goes in v2:
time: 99.9 us; the launch traced here: 99.3 us
  starting transfers between devices  54.7 us (55%)
  waiting for transfers between devices  35.5 us (36%)
  Pallas kernels  5.56 us (6%)
  local copies, waits for them, and re-layouts  2.59 us (3%)
    ppermute x11, starting transfers between devices, shift(): lax.ppermute(value, axis, [(i, (i + step) % size) for i in range(size)])  40.6 us
    ppermute x11, waiting for transfers between devices, shift(): lax.ppermute(value, axis, [(i, (i + step) % size) for i in range(size)])  26.8 us
    all_to_all x1, starting transfers between devices, with_slots(): lax.all_to_all(outgoing, CHIP_CORE, split_axis=0, concat_axis=0, tiled=True)  14 us
    all_to_all x1, waiting for transfers between devices, with_slots(): lax.all_to_all(outgoing, CHIP_CORE, split_axis=0, concat_axis=0, tiled=True)  8.62 us
    pallas_call x1, Pallas kernels, ladder(): pl.pallas_call(ladder_kernel, in_specs=[SMEM, VMEM, VMEM, VMEM, VMEM], ou...  4.03 us
  transfers between devices with their start and end apart: 12, of which 9 were waited for; matrix products, arithmetic and copies ran while one was open for 0% of the time, Pallas kernels for 0%

profile of v2, /device:TPU:1, one launch (start us, length us, event | category | flops | bytes accessed | tf_op | source)
XLA Modules:
  0.0 99.3 jit_solution(16963739595778528222)
XLA Ops:
  0.0 0.8 reshape.49.packed_ref
  0.9 1.5 %shard_map.48 = (bf16[32,16,128]{2,1,0:T(8,128)(2,1)}, s32[4]{0:T(128)S(1)}) custom-call(s32[2304]{0:T(1024)} %labels_ref.1, bf16[4,8,128]{2,1,0:T(8,128)(2,1)S(1)} %reshape.49.packed_ref), custom_call_target="tpu_custom_call" | custom-call | tf_op jit(solution)/shard_map/pallas_call | solution.py:49
  3.6 95.7 %conditional.1 = (bf16[3,256,1024]{2,1,0:T(8,128)(2,1)}) conditional(s32[]{:T(128)} %bitcast.68, (bf16[32,16,128]{2,1,0:T(8,128)(2,1)}, s32[4]{0:T(128)S(1)}, bf16[3,256,768]{2,1,0:T(8,128)(2,1)}, bf16[3,256,1024]{2,1,0:T(8,128)(2,1)}) %tuple.11, (s32[2304]{0:T(1024)}, bf16[4,8,128]{2,1,0:T(8,128)(2,1)S(1)}, bf16[3,256,768]{2,1,0:T(8,128)(2,1)}, ...), branch_computations={%region_0.0_spmd, %region_1.0_spmd} | conditional | flops 98 | bytes 34506424 | solution.py:144
  3.6 14.0 %all-to-all-start = ((bf16[32,16,128]{2,1,0:T(8,128)(2,1)}), bf16[32,16,128]{2,1,0:T(8,128)(2,1)S(1)}, u32[]{:S(2)}, u32[]{:S(2)}) async-start(bf16[32,16,128]{2,1,0:T(8,128)(2,1)} %get-tuple-element.26), calls=%async_computation | async-start | bytes 262144 | tf_op jit(solution)/shard_map/cond/branch_0_fun/all_to_all | solution.py:100
  17.7 8.6 %all-to-all-done = bf16[32,16,128]{2,1,0:T(8,128)(2,1)S(1)} async-done(((bf16[32,16,128]{2,1,0:T(8,128)(2,1)}), bf16[32,16,128]{2,1,0:T(8,128)(2,1)S(1)}, u32[]{:S(2)}, u32[]{:S(2)}) %all-to-all-start) | async-done | bytes 131104 | tf_op jit(solution)/shard_map/cond/branch_0_fun/all_to_all | solution.py:100
  27.1 7.6 %collective-permute-start = (bf16[2,32,512]{2,1,0:T(8,128)(2,1)S(1)}, bf16[2,32,512]{2,1,0:T(8,128)(2,1)S(1)}, u32[]{:S(2)}, u32[]{:S(2)}) collective-permute-start(bf16[2,32,512]{2,1,0:T(8,128)(2,1)S(1)} %reshape.36), channel_id=1, source_target_pairs={{0,1},{1,2},{2,0},{3,4},{4,5},{5,3},{6,7},{7,8},{8,6},{9,10},{10,1... | collective-permute-start | bytes 196616 | tf_op jit(solution)/shard_map/cond/branch_0_fun/ppermute | solution.py:20
  34.7 3.2 %collective-permute-start.1 = (bf16[2,32,512]{2,1,0:T(8,128)(2,1)S(1)}, bf16[2,32,512]{2,1,0:T(8,128)(2,1)S(1)}, u32[]{:S(2)}, u32[]{:S(2)}) collective-permute-start(bf16[2,32,512]{2,1,0:T(8,128)(2,1)S(1)} %reshape.36), channel_id=1, source_target_pairs={{0,2},{1,0},{2,1},{3,5},{4,3},{5,4},{6,8},{7,6},{8,7},{9,11},{10,9... | collective-permute-start | bytes 196616 | tf_op jit(solution)/shard_map/cond/branch_0_fun/ppermute | solution.py:20
  38.1 10.6 %collective-permute-done.1 = bf16[2,32,512]{2,1,0:T(8,128)(2,1)S(1)} collective-permute-done((bf16[2,32,512]{2,1,0:T(8,128)(2,1)S(1)}, bf16[2,32,512]{2,1,0:T(8,128)(2,1)S(1)}, u32[]{:S(2)}, u32[]{:S(2)}) %collective-permute-start.1) | collective-permute-done | bytes 65568 | tf_op jit(solution)/shard_map/cond/branch_0_fun/ppermute | solution.py:20
  48.7 3.2 %collective-permute-start.2 = (bf16[2,96,512]{2,1,0:T(8,128)(2,1)S(1)}, bf16[2,96,512]{2,1,0:T(8,128)(2,1)S(1)}, u32[]{:S(2)}, u32[]{:S(2)}) collective-permute-start(bf16[2,96,512]{2,1,0:T(8,128)(2,1)S(1)} %bitcast.111), channel_id=1, source_target_pairs={{0,3},{3,6},{6,9},{9,12},{12,15},{15,18},{18,21},{21,0},{1,4},{4,7... | collective-permute-start | bytes 589832 | tf_op jit(solution)/shard_map/cond/branch_0_fun/ppermute | solution.py:20
  51.9 3.8 %collective-permute-start.3 = (bf16[2,96,512]{2,1,0:T(8,128)(2,1)S(1)}, bf16[2,96,512]{2,1,0:T(8,128)(2,1)S(1)}, u32[]{:S(2)}, u32[]{:S(2)}) collective-permute-start(bf16[2,96,512]{2,1,0:T(8,128)(2,1)S(1)} %bitcast.112), channel_id=1, source_target_pairs={{0,21},{3,0},{6,3},{9,6},{12,9},{15,12},{18,15},{21,18},{1,22},{4,... | collective-permute-start | bytes 589832 | tf_op jit(solution)/shard_map/cond/branch_0_fun/ppermute | solution.py:20
  56.0 2.6 %collective-permute-done.2 = bf16[2,96,512]{2,1,0:T(8,128)(2,1)S(1)} collective-permute-done((bf16[2,96,512]{2,1,0:T(8,128)(2,1)S(1)}, bf16[2,96,512]{2,1,0:T(8,128)(2,1)S(1)}, u32[]{:S(2)}, u32[]{:S(2)}) %collective-permute-start.2) | collective-permute-done | bytes 196640 | tf_op jit(solution)/shard_map/cond/branch_0_fun/ppermute | solution.py:20
  58.5 1.9 %collective-permute-start.4 = (bf16[2,96,512]{2,1,0:T(8,128)(2,1)S(1)}, bf16[2,96,512]{2,1,0:T(8,128)(2,1)S(1)}, u32[]{:S(2)}, u32[]{:S(2)}) collective-permute-start(bf16[2,96,512]{2,1,0:T(8,128)(2,1)S(1)} %collective-permute-done.2), channel_id=1, source_target_pairs={{0,3},{3,6},{6,9},{9,12},{12,15},{15,18},{18,21},{21,0},{1,4},{4,7... | collective-permute-start | bytes 589832 | tf_op jit(solution)/shard_map/cond/branch_0_fun/ppermute | solution.py:20
  60.4 4.6 %collective-permute-start.5 = (bf16[2,96,512]{2,1,0:T(8,128)(2,1)S(1)}, bf16[2,96,512]{2,1,0:T(8,128)(2,1)S(1)}, u32[]{:S(2)}, u32[]{:S(2)}) collective-permute-start(bf16[2,96,512]{2,1,0:T(8,128)(2,1)S(1)} %collective-permute-done.3), channel_id=1, source_target_pairs={{0,21},{3,0},{6,3},{9,6},{12,9},{15,12},{18,15},{21,18},{1,22},{4,... | collective-permute-start | bytes 589832 | tf_op jit(solution)/shard_map/cond/branch_0_fun/ppermute | solution.py:20
  65.1 1.8 %collective-permute-done.4 = bf16[2,96,512]{2,1,0:T(8,128)(2,1)S(1)} collective-permute-done((bf16[2,96,512]{2,1,0:T(8,128)(2,1)S(1)}, bf16[2,96,512]{2,1,0:T(8,128)(2,1)S(1)}, u32[]{:S(2)}, u32[]{:S(2)}) %collective-permute-start.4) | collective-permute-done | bytes 196640 | tf_op jit(solution)/shard_map/cond/branch_0_fun/ppermute | solution.py:20
  66.9 1.9 %collective-permute-start.6 = (bf16[2,96,512]{2,1,0:T(8,128)(2,1)S(1)}, bf16[2,96,512]{2,1,0:T(8,128)(2,1)S(1)}, u32[]{:S(2)}, u32[]{:S(2)}) collective-permute-start(bf16[2,96,512]{2,1,0:T(8,128)(2,1)S(1)} %collective-permute-done.4), channel_id=1, source_target_pairs={{0,3},{3,6},{6,9},{9,12},{12,15},{15,18},{18,21},{21,0},{1,4},{4,7... | collective-permute-start | bytes 589832 | tf_op jit(solution)/shard_map/cond/branch_0_fun/ppermute | solution.py:20
  68.8 4.6 %collective-permute-start.7 = (bf16[2,96,512]{2,1,0:T(8,128)(2,1)S(1)}, bf16[2,96,512]{2,1,0:T(8,128)(2,1)S(1)}, u32[]{:S(2)}, u32[]{:S(2)}) collective-permute-start(bf16[2,96,512]{2,1,0:T(8,128)(2,1)S(1)} %collective-permute-done.5), channel_id=1, source_target_pairs={{0,21},{3,0},{6,3},{9,6},{12,9},{15,12},{18,15},{21,18},{1,22},{4,... | collective-permute-start | bytes 589832 | tf_op jit(solution)/shard_map/cond/branch_0_fun/ppermute | solution.py:20
  73.4 1.0 %collective-permute-done.6 = bf16[2,96,512]{2,1,0:T(8,128)(2,1)S(1)} collective-permute-done((bf16[2,96,512]{2,1,0:T(8,128)(2,1)S(1)}, bf16[2,96,512]{2,1,0:T(8,128)(2,1)S(1)}, u32[]{:S(2)}, u32[]{:S(2)}) %collective-permute-start.6) | collective-permute-done | bytes 196640 | tf_op jit(solution)/shard_map/cond/branch_0_fun/ppermute | solution.py:20
  74.5 1.5 %collective-permute-done.7 = bf16[2,96,512]{2,1,0:T(8,128)(2,1)S(1)} collective-permute-done((bf16[2,96,512]{2,1,0:T(8,128)(2,1)S(1)}, bf16[2,96,512]{2,1,0:T(8,128)(2,1)S(1)}, u32[]{:S(2)}, u32[]{:S(2)}) %collective-permute-start.7) | collective-permute-done | bytes 196640 | tf_op jit(solution)/shard_map/cond/branch_0_fun/ppermute | solution.py:20
  76.0 5.1 %collective-permute-start.9 = (bf16[2,8,96,512]{3,2,1,0:T(8,128)(2,1)S(1)}, bf16[2,8,96,512]{3,2,1,0:T(8,128)(2,1)S(1)}, u32[]{:S(2)}, u32[]{:S(2)}) collective-permute-start(bf16[2,8,96,512]{3,2,1,0:T(8,128)(2,1)S(1)} %bitcast_dynamic-update-slice_fusion.1), channel_id=1, source_target_pairs={{0,24},{24,0},{1,25},{25,1},{2,26},{26,2},{3,27},{27,3},{4,28},{28... | collective-permute-start | bytes 4718600 | tf_op jit(solution)/shard_map/cond/branch_0_fun/ppermute | solution.py:20
  81.1 2.3 %collective-permute-start.8 = (bf16[2,96,512]{2,1,0:T(8,128)(2,1)S(1)}, bf16[2,96,512]{2,1,0:T(8,128)(2,1)S(1)}, u32[]{:S(2)}, u32[]{:S(2)}) collective-permute-start(bf16[2,96,512]{2,1,0:T(8,128)(2,1)S(1)} %collective-permute-done.6), channel_id=1, source_target_pairs={{0,3},{3,6},{6,9},{9,12},{12,15},{15,18},{18,21},{21,0},{1,4},{4,7... | collective-permute-start | bytes 589832 | tf_op jit(solution)/shard_map/cond/branch_0_fun/ppermute | solution.py:20
  83.4 8.3 %collective-permute-done.8 = bf16[2,96,512]{2,1,0:T(8,128)(2,1)S(1)} collective-permute-done((bf16[2,96,512]{2,1,0:T(8,128)(2,1)S(1)}, bf16[2,96,512]{2,1,0:T(8,128)(2,1)S(1)}, u32[]{:S(2)}, u32[]{:S(2)}) %collective-permute-start.8) | collective-permute-done | bytes 196640 | tf_op jit(solution)/shard_map/cond/branch_0_fun/ppermute | solution.py:20
  91.7 2.5 %collective-permute-start.10 = (bf16[2,96,512]{2,1,0:T(8,128)(2,1)S(1)}, bf16[2,96,512]{2,1,0:T(8,128)(2,1)S(1)}, u32[]{:S(2)}, u32[]{:S(2)}) collective-permute-start(bf16[2,96,512]{2,1,0:T(8,128)(2,1)S(1)} %collective-permute-done.8), channel_id=1, source_target_pairs={{0,24},{24,0},{1,25},{25,1},{2,26},{26,2},{3,27},{27,3},{4,28},{28... | collective-permute-start | bytes 589832 | tf_op jit(solution)/shard_map/cond/branch_0_fun/ppermute | solution.py:20
  94.2 1.0 %collective-permute-done.10 = bf16[2,96,512]{2,1,0:T(8,128)(2,1)S(1)} collective-permute-done((bf16[2,96,512]{2,1,0:T(8,128)(2,1)S(1)}, bf16[2,96,512]{2,1,0:T(8,128)(2,1)S(1)}, u32[]{:S(2)}, u32[]{:S(2)}) %collective-permute-start.10) | collective-permute-done | bytes 196640 | tf_op jit(solution)/shard_map/cond/branch_0_fun/ppermute | solution.py:20
  95.2 4.0 %branch_0_fun.1 = bf16[3,256,1024]{2,1,0:T(8,128)(2,1)} custom-call(s32[4]{0:T(128)S(1)} %get-tuple-element.24.where_ref, bf16[3,256,768]{2,1,0:T(8,128)(2,1)} %get-tuple-element.25.integrals_ref, bf16[2,768,512]{2,1,0:T(8,128)(2,1)S(1)} %bitcast.104, bf16[2,768,512]{2,1,0:T(8,128)(2,1)S(1)} %bitcast.105, bf16[3,256,1024]{2,1,0:T(8,128)(2,1)} %get-tuple-element.27.previous_ref), custom_call_target="tpu_custom_call" | custom-call | tf_op jit(solution)/shard_map/cond/branch_0_fun/pallas_call | solution.py:84
  (24 shorter events, 1.9 us)
Async XLA Ops:
  3.6 22.7 %all-to-all-start = ((bf16[32,16,128]{2,1,0:T(8,128)(2,1)}), bf16[32,16,128]{2,1,0:T(8,128)(2,1)S(1)}, u32[]{:S(2)}, u32[]{:S(2)}) async-start(bf16[32,16,128]{2,1,0:T(8,128)(2,1)} %get-tuple-element.26), calls=%async_computation | async-start | bytes 262144 | tf_op jit(solution)/shard_map/cond/branch_0_fun/all_to_all | solution.py:100
  27.1 11.0 %collective-permute-start = (bf16[2,32,512]{2,1,0:T(8,128)(2,1)S(1)}, bf16[2,32,512]{2,1,0:T(8,128)(2,1)S(1)}, u32[]{:S(2)}, u32[]{:S(2)}) collective-permute-start(bf16[2,32,512]{2,1,0:T(8,128)(2,1)S(1)} %reshape.36), channel_id=1, source_target_pairs={{0,1},{1,2},{2,0},{3,4},{4,5},{5,3},{6,7},{7,8},{8,6},{9,10},{10,1... | collective-permute-start | bytes 196616 | tf_op jit(solution)/shard_map/cond/branch_0_fun/ppermute | solution.py:20
  34.7 13.9 %collective-permute-start.1 = (bf16[2,32,512]{2,1,0:T(8,128)(2,1)S(1)}, bf16[2,32,512]{2,1,0:T(8,128)(2,1)S(1)}, u32[]{:S(2)}, u32[]{:S(2)}) collective-permute-start(bf16[2,32,512]{2,1,0:T(8,128)(2,1)S(1)} %reshape.36), channel_id=1, source_target_pairs={{0,2},{1,0},{2,1},{3,5},{4,3},{5,4},{6,8},{7,6},{8,7},{9,11},{10,9... | collective-permute-start | bytes 196616 | tf_op jit(solution)/shard_map/cond/branch_0_fun/ppermute | solution.py:20
  48.7 9.8 %collective-permute-start.2 = (bf16[2,96,512]{2,1,0:T(8,128)(2,1)S(1)}, bf16[2,96,512]{2,1,0:T(8,128)(2,1)S(1)}, u32[]{:S(2)}, u32[]{:S(2)}) collective-permute-start(bf16[2,96,512]{2,1,0:T(8,128)(2,1)S(1)} %bitcast.111), channel_id=1, source_target_pairs={{0,3},{3,6},{6,9},{9,12},{12,15},{15,18},{18,21},{21,0},{1,4},{4,7... | collective-permute-start | bytes 589832 | tf_op jit(solution)/shard_map/cond/branch_0_fun/ppermute | solution.py:20
  51.9 8.5 %collective-permute-start.3 = (bf16[2,96,512]{2,1,0:T(8,128)(2,1)S(1)}, bf16[2,96,512]{2,1,0:T(8,128)(2,1)S(1)}, u32[]{:S(2)}, u32[]{:S(2)}) collective-permute-start(bf16[2,96,512]{2,1,0:T(8,128)(2,1)S(1)} %bitcast.112), channel_id=1, source_target_pairs={{0,21},{3,0},{6,3},{9,6},{12,9},{15,12},{18,15},{21,18},{1,22},{4,... | collective-permute-start | bytes 589832 | tf_op jit(solution)/shard_map/cond/branch_0_fun/ppermute | solution.py:20
  58.5 8.4 %collective-permute-start.4 = (bf16[2,96,512]{2,1,0:T(8,128)(2,1)S(1)}, bf16[2,96,512]{2,1,0:T(8,128)(2,1)S(1)}, u32[]{:S(2)}, u32[]{:S(2)}) collective-permute-start(bf16[2,96,512]{2,1,0:T(8,128)(2,1)S(1)} %collective-permute-done.2), channel_id=1, source_target_pairs={{0,3},{3,6},{6,9},{9,12},{12,15},{15,18},{18,21},{21,0},{1,4},{4,7... | collective-permute-start | bytes 589832 | tf_op jit(solution)/shard_map/cond/branch_0_fun/ppermute | solution.py:20
  60.4 8.4 %collective-permute-start.5 = (bf16[2,96,512]{2,1,0:T(8,128)(2,1)S(1)}, bf16[2,96,512]{2,1,0:T(8,128)(2,1)S(1)}, u32[]{:S(2)}, u32[]{:S(2)}) collective-permute-start(bf16[2,96,512]{2,1,0:T(8,128)(2,1)S(1)} %collective-permute-done.3), channel_id=1, source_target_pairs={{0,21},{3,0},{6,3},{9,6},{12,9},{15,12},{18,15},{21,18},{1,22},{4,... | collective-permute-start | bytes 589832 | tf_op jit(solution)/shard_map/cond/branch_0_fun/ppermute | solution.py:20
  66.9 7.6 %collective-permute-start.6 = (bf16[2,96,512]{2,1,0:T(8,128)(2,1)S(1)}, bf16[2,96,512]{2,1,0:T(8,128)(2,1)S(1)}, u32[]{:S(2)}, u32[]{:S(2)}) collective-permute-start(bf16[2,96,512]{2,1,0:T(8,128)(2,1)S(1)} %collective-permute-done.4), channel_id=1, source_target_pairs={{0,3},{3,6},{6,9},{9,12},{12,15},{15,18},{18,21},{21,0},{1,4},{4,7... | collective-permute-start | bytes 589832 | tf_op jit(solution)/shard_map/cond/branch_0_fun/ppermute | solution.py:20
  68.8 7.2 %collective-permute-start.7 = (bf16[2,96,512]{2,1,0:T(8,128)(2,1)S(1)}, bf16[2,96,512]{2,1,0:T(8,128)(2,1)S(1)}, u32[]{:S(2)}, u32[]{:S(2)}) collective-permute-start(bf16[2,96,512]{2,1,0:T(8,128)(2,1)S(1)} %collective-permute-done.5), channel_id=1, source_target_pairs={{0,21},{3,0},{6,3},{9,6},{12,9},{15,12},{18,15},{21,18},{1,22},{4,... | collective-permute-start | bytes 589832 | tf_op jit(solution)/shard_map/cond/branch_0_fun/ppermute | solution.py:20
  76.0 18.2 %collective-permute-start.9 = (bf16[2,8,96,512]{3,2,1,0:T(8,128)(2,1)S(1)}, bf16[2,8,96,512]{3,2,1,0:T(8,128)(2,1)S(1)}, u32[]{:S(2)}, u32[]{:S(2)}) collective-permute-start(bf16[2,8,96,512]{3,2,1,0:T(8,128)(2,1)S(1)} %bitcast_dynamic-update-slice_fusion.1), channel_id=1, source_target_pairs={{0,24},{24,0},{1,25},{25,1},{2,26},{26,2},{3,27},{27,3},{4,28},{28... | collective-permute-start | bytes 4718600 | tf_op jit(solution)/shard_map/cond/branch_0_fun/ppermute | solution.py:20
  81.1 10.6 %collective-permute-start.8 = (bf16[2,96,512]{2,1,0:T(8,128)(2,1)S(1)}, bf16[2,96,512]{2,1,0:T(8,128)(2,1)S(1)}, u32[]{:S(2)}, u32[]{:S(2)}) collective-permute-start(bf16[2,96,512]{2,1,0:T(8,128)(2,1)S(1)} %collective-permute-done.6), channel_id=1, source_target_pairs={{0,3},{3,6},{6,9},{9,12},{12,15},{15,18},{18,21},{21,0},{1,4},{4,7... | collective-permute-start | bytes 589832 | tf_op jit(solution)/shard_map/cond/branch_0_fun/ppermute | solution.py:20
  91.7 3.5 %collective-permute-start.10 = (bf16[2,96,512]{2,1,0:T(8,128)(2,1)S(1)}, bf16[2,96,512]{2,1,0:T(8,128)(2,1)S(1)}, u32[]{:S(2)}, u32[]{:S(2)}) collective-permute-start(bf16[2,96,512]{2,1,0:T(8,128)(2,1)S(1)} %collective-permute-done.8), channel_id=1, source_target_pairs={{0,24},{24,0},{1,25},{25,1},{2,26},{26,2},{3,27},{27,3},{4,28},{28... | collective-permute-start | bytes 589832 | tf_op jit(solution)/shard_map/cond/branch_0_fun/ppermute | solution.py:20

commit v3 on v2

v3 whole, which is shorter than its diff:
```python
import functools

import jax
import jax.numpy as jnp
from jax import lax
from jax.experimental import pallas as pl
from jax.experimental.pallas import tpu as pltpu
from jax.sharding import Mesh
from jax.sharding import PartitionSpec as P

CHIP_CORE = ("chip", "core")
TILE_BULK = ("chip", "core", "bulk_0", "bulk_1")
BULK = ("bulk_0", "bulk_1")
VMEM = pl.BlockSpec(memory_space=pltpu.VMEM)
SMEM = pl.BlockSpec(memory_space=pltpu.SMEM)


def shift(value, axis, step):
    size = lax.axis_size(axis)
    return lax.ppermute(value, axis, [(i, (i + step) % size) for i in range(size)])


def choose_kernel(slots, chips, tiles, bulk_0, bulk_1, labels_ref, amplitudes_ref, outgoing_ref, where_ref, packed_ref):
    per_chip = labels_ref.shape[0] // chips
    irreps, rows, lanes = packed_ref.shape
    for irrep in range(irreps):
        block = amplitudes_ref[irrep].astype(jnp.float32)
        pieces = [block[begin : begin + rows] for begin in range(0, block.shape[0], rows)]
        packed_ref[irrep] = jnp.concatenate(pieces, axis=1)
    most = jnp.int32(0)
    for chip in range(chips):
        first, last = labels_ref[chip * per_chip], labels_ref[(chip + 1) * per_chip - 1]
        most = jnp.maximum(most, last - first)
        chosen = [packed_ref[jnp.minimum(first + slot, last)] for slot in range(slots)]
        chosen = jnp.concatenate(chosen, axis=0).astype(outgoing_ref.dtype)
        for core in range(2):
            outgoing_ref[2 * chip + core] = chosen
    own = lax.axis_index("chip")
    row = own * 2 + lax.axis_index("core")
    column = lax.axis_index("bulk_0") * bulk_1 + lax.axis_index("bulk_1")
    first_tile = (row * (bulk_0 * bulk_1) + column) * tiles
    for t in range(tiles):
        where_ref[t] = labels_ref[first_tile + t] - labels_ref[own * per_chip]
    where_ref[tiles] = most + 1


def choose(slots, labels, amplitudes, tiles):
    chips = lax.axis_size("chip")
    irreps, depth, width = amplitudes.shape
    lanes = 128
    rows = depth * width // lanes
    body = functools.partial(
        choose_kernel, slots, chips, tiles, lax.axis_size("bulk_0"), lax.axis_size("bulk_1")
    )
    return pl.pallas_call(
        body,
        in_specs=[SMEM, VMEM],
        out_specs=(VMEM, SMEM),
        out_shape=(
            jax.ShapeDtypeStruct((2 * chips, slots * rows, lanes), amplitudes.dtype),
            jax.ShapeDtypeStruct((tiles + 1,), jnp.int32),
        ),
        scratch_shapes=[pltpu.VMEM((irreps, rows, lanes), jnp.float32)],
    )(labels, amplitudes)


def begin_kernel(other, where_ref, integrals_ref, block_ref, previous_ref, out_ref):
    tiles = integrals_ref.shape[0]
    half = block_ref.shape[2]
    core = lax.axis_index("core")
    side = 1 - core if other else core
    chunk = 256
    for t in range(tiles):
        slot = where_ref[t]
        for begin in range(0, half, chunk):
            columns = pl.ds(pl.multiple_of(side * half + begin, chunk), chunk)
            product = jnp.dot(
                integrals_ref[t], block_ref[slot, :, begin : begin + chunk], preferred_element_type=jnp.float32
            )
            out_ref[t, :, begin : begin + chunk] = previous_ref[t, :, columns].astype(jnp.float32) + product


def begin_half(other, where, integrals, block, residual_in):
    tiles, rows, depth = integrals.shape
    half = block.shape[2]
    return pl.pallas_call(
        functools.partial(begin_kernel, other),
        in_specs=[SMEM, VMEM, VMEM, VMEM],
        out_specs=VMEM,
        out_shape=jax.ShapeDtypeStruct((tiles, rows, half), jnp.float32),
        cost_estimate=pl.CostEstimate(
            flops=2 * tiles * rows * depth * half, bytes_accessed=4_000_000, transcendentals=0
        ),
        compiler_params=pltpu.CompilerParams(vmem_limit_bytes=24 * 2**20),
    )(where, integrals, block, residual_in)


def finish_kernel(where_ref, strip_ref, own_ref, other_ref, own_sum_ref, other_sum_ref, out_ref, rows_ref, sems):
    tiles, _, half = own_sum_ref.shape
    core = lax.axis_index("core")
    copies = []
    for t in range(tiles):
        slot = where_ref[t]
        for block_ref, sum_ref, side in ((own_ref, own_sum_ref, core), (other_ref, other_sum_ref, 1 - core)):
            columns = pl.ds(pl.multiple_of(side * half, half), half)
            product = jnp.dot(strip_ref[t], block_ref[slot], preferred_element_type=jnp.float32)
            rows_ref[t, :, columns] = (sum_ref[t] + product).astype(rows_ref.dtype)
        copies.append(pltpu.make_async_copy(rows_ref.at[t], out_ref.at[t], sems.at[t]))
        copies[-1].start()
    for copy in copies:
        copy.wait()


def finish(where, strip, own, other, own_sum, other_sum, like):
    tiles = like.shape[0]
    return pl.pallas_call(
        finish_kernel,
        in_specs=[SMEM] + [VMEM] * 5,
        out_specs=pl.BlockSpec(memory_space=pl.ANY),
        out_shape=jax.ShapeDtypeStruct(like.shape, like.dtype),
        scratch_shapes=[pltpu.VMEM(like.shape, like.dtype), pltpu.SemaphoreType.DMA((tiles,))],
        compiler_params=pltpu.CompilerParams(vmem_limit_bytes=24 * 2**20),
    )(where, strip, own, other, own_sum, other_sum)


def with_slots(slots, incoming, where, integrals, residual_in, depth, width):
    half = lax.axis_size("chip")
    core = lax.axis_index("core")
    mine = lax.dynamic_slice_in_dim(incoming, core * half, half, 0)
    parts = incoming.shape[2] // width
    mine = mine.reshape(half, slots, depth // parts, parts, width).transpose(1, 3, 2, 0, 4)
    mine = mine.reshape(slots, depth, half * width)
    z_size, z = lax.axis_size("bulk_1"), lax.axis_index("bulk_1")
    group = jnp.zeros((slots, z_size, depth, half * width), mine.dtype)
    group = lax.dynamic_update_slice_in_dim(group, mine[:, None], z, 1)
    for step in range(1, z_size):
        got = shift(mine, "bulk_1", step)
        group = lax.dynamic_update_slice_in_dim(group, got[:, None], lax.rem(z - step + z_size, z_size), 1)
    group = group.reshape(slots, z_size * depth, half * width)
    y_size, y = lax.axis_size("bulk_0"), lax.axis_index("bulk_0")
    whole = jnp.zeros((slots, y_size, z_size * depth, half * width), mine.dtype)
    whole = lax.dynamic_update_slice_in_dim(whole, group[:, None], y, 1)
    up, down = group, group
    for step in range(1, y_size // 2):
        up = shift(up, "bulk_0", 1)
        whole = lax.dynamic_update_slice_in_dim(whole, up[:, None], lax.rem(y - step + y_size, y_size), 1)
        down = shift(down, "bulk_0", -1)
        whole = lax.dynamic_update_slice_in_dim(whole, down[:, None], lax.rem(y + step, y_size), 1)
    whole = whole.reshape(slots, y_size * z_size * depth, half * width)
    up = shift(up, "bulk_0", 1)
    own_sum = begin_half(False, where, integrals, whole, residual_in)
    up, own_sum = lax.optimization_barrier((up, own_sum))
    other_sum = begin_half(True, where, integrals, shift(whole, "core", 1), residual_in)
    far = lax.rem(y + y_size // 2, y_size)
    strip = lax.dynamic_slice_in_dim(integrals, far * (z_size * depth), z_size * depth, 2)
    return finish(where, strip, up, shift(up, "core", 1), own_sum, other_sum, residual_in)


def local(integrals, amplitudes, residual_in, tile_irrep):
    tiles = integrals.shape[0]
    _, depth, width = amplitudes.shape

    def spread(outgoing):
        return lax.all_to_all(outgoing, CHIP_CORE, split_axis=0, concat_axis=0, tiled=True)

    outgoing, where = choose(2, tile_irrep, amplitudes, tiles)
    incoming = spread(outgoing)

    def two():
        return with_slots(2, incoming, where, integrals, residual_in, depth, width)

    def three():
        wider = spread(choose(3, tile_irrep, amplitudes, tiles)[0])
        return with_slots(3, wider, where, integrals, residual_in, depth, width)

    return lax.cond(where[tiles] > 2, three, two)


def solution(mesh):
    tile, bulk = mesh.shape["tile"], mesh.shape["bulk"]
    finer = Mesh(mesh.devices.reshape(tile // 2, 2, bulk // 3, 3), TILE_BULK)
    placed = (P(TILE_BULK, None, None), P(None, BULK, CHIP_CORE), P(TILE_BULK, None, None), P())
    return jax.shard_map(
        local, mesh=finer, in_specs=placed, out_specs=P(TILE_BULK, None, None), check_vma=False
    )
```

time: 99.9 us -> 99 us (level)
  waiting for transfers between devices: 35.5 us -> 31.6 us
  Pallas kernels: 5.56 us -> 7.93 us
    ppermute x11, waiting for transfers between devices: 26.8 us -> 24.3 us  [shift(): lax.ppermute(value, axis, [(i, (i + step) % size) for i in range(size)])]
    pallas_call x1 -> x3, Pallas kernels: 4.03 us -> 6.35 us  [the longest x2 4.36 us: begin_half(): pl.pallas_call(functools.partial(begin_kernel, other), in_specs=[SMEM, VM...]
    all_to_all x1, waiting for transfers between devices: 8.62 us -> 7.33 us  [spread(): lax.all_to_all(outgoing, CHIP_CORE, split_axis=0, concat_axis=0, tiled=True)]
    dynamic_slice x0 -> x1, local copies, waits for them, and re-layouts: none -> 1.12 us  [with_slots(): lax.dynamic_slice_in_dim(integrals, far * (z_size * depth), z_size * dept...]
  transfers between devices with their start and end apart: 12 -> 12, of which waited for: 9 -> 7; matrix products, arithmetic and copies ran while one was open for 0% -> 2% of each run, Pallas kernels for 0% -> 4%
where the time goes in v3:
time: 99 us; the launch traced here: 98.4 us
  starting transfers between devices  54.8 us (55%)
  waiting for transfers between devices  31.6 us (32%)
  Pallas kernels  7.93 us (8%)
  local copies, waits for them, and re-layouts  3.01 us (3%)
    ppermute x11, starting transfers between devices, shift(): lax.ppermute(value, axis, [(i, (i + step) % size) for i in range(size)])  40.7 us
    ppermute x11, waiting for transfers between devices, shift(): lax.ppermute(value, axis, [(i, (i + step) % size) for i in range(size)])  24.3 us
    all_to_all x1, starting transfers between devices, spread(): lax.all_to_all(outgoing, CHIP_CORE, split_axis=0, concat_axis=0, tiled=True)  14 us
    all_to_all x1, waiting for transfers between devices, spread(): lax.all_to_all(outgoing, CHIP_CORE, split_axis=0, concat_axis=0, tiled=True)  7.33 us
    pallas_call x2, Pallas kernels, begin_half(): pl.pallas_call(functools.partial(begin_kernel, other), in_specs=[SMEM, VM...  4.36 us
    pallas_call x1, Pallas kernels, finish(): pl.pallas_call(finish_kernel, in_specs=[SMEM] + [VMEM] * 5, out_specs=pl....  1.98 us
  transfers between devices with their start and end apart: 12, of which 7 were waited for; matrix products, arithmetic and copies ran while one was open for 2% of the time, Pallas kernels for 4%

profile of v3, /device:TPU:1, one launch (start us, length us, event | category | flops | bytes accessed | tf_op | source)
XLA Modules:
  0.0 98.4 jit_solution(75839683970201064)
XLA Ops:
  0.0 1.6 %shard_map.48 = (bf16[32,16,128]{2,1,0:T(8,128)(2,1)}, s32[4]{0:T(128)S(1)}) custom-call(s32[2304]{0:T(1024)} %labels_ref.1, bf16[4,32,32]{2,1,0:T(8,128)(2,1)} %amplitudes_ref.1), custom_call_target="tpu_custom_call" | custom-call | tf_op jit(solution)/shard_map/pallas_call | solution.py:55
  1.6 14.0 %all-to-all-start.1 = ((bf16[32,16,128]{2,1,0:T(8,128)(2,1)}), bf16[32,16,128]{2,1,0:T(8,128)(2,1)S(1)}, u32[]{:S(2)}, u32[]{:S(2)}) async-start(bf16[32,16,128]{2,1,0:T(8,128)(2,1)} %get-tuple-element.43), calls=%async_computation.1 | async-start | bytes 262144 | tf_op jit(solution)/shard_map/all_to_all | solution.py:164
  17.0 7.3 %all-to-all-done.1 = bf16[32,16,128]{2,1,0:T(8,128)(2,1)S(1)} async-done(((bf16[32,16,128]{2,1,0:T(8,128)(2,1)}), bf16[32,16,128]{2,1,0:T(8,128)(2,1)S(1)}, u32[]{:S(2)}, u32[]{:S(2)}) %all-to-all-start.1) | async-done | bytes 131104 | tf_op jit(solution)/shard_map/all_to_all | solution.py:164
  24.3 74.1 %conditional.1 = (bf16[3,256,1024]{2,1,0:T(8,128)(2,1)}) conditional(s32[]{:T(128)} %bitcast.42, (bf16[3,256,768]{2,1,0:T(8,128)(2,1)}, bf16[32,16,128]{2,1,0:T(8,128)(2,1)S(1)}, s32[4]{0:T(128)S(1)}, bf16[3,256,1024]{2,1,0:T(8,128)(2,1)}) %tuple.13, (bf16[3,256,768]{2,1,0:T(8,128)(2,1)}, s32[2304]{0:T(1024)}, bf16[4,32,32]{2,1,0:T(8,128)(2,1)}, ...), branch_computations={%region_0.0_spmd, %region_1.0_spmd} | conditional | flops 1207959680 | bytes 65214632 | solution.py:176
  24.9 7.6 %collective-permute-start = (bf16[2,32,512]{2,1,0:T(8,128)(2,1)S(1)}, bf16[2,32,512]{2,1,0:T(8,128)(2,1)S(1)}, u32[]{:S(2)}, u32[]{:S(2)}) collective-permute-start(bf16[2,32,512]{2,1,0:T(8,128)(2,1)S(1)} %reshape.30), channel_id=1, source_target_pairs={{0,1},{1,2},{2,0},{3,4},{4,5},{5,3},{6,7},{7,8},{8,6},{9,10},{10,1... | collective-permute-start | bytes 196616 | tf_op jit(solution)/shard_map/cond/branch_0_fun/ppermute | solution.py:20
  32.5 3.2 %collective-permute-start.1 = (bf16[2,32,512]{2,1,0:T(8,128)(2,1)S(1)}, bf16[2,32,512]{2,1,0:T(8,128)(2,1)S(1)}, u32[]{:S(2)}, u32[]{:S(2)}) collective-permute-start(bf16[2,32,512]{2,1,0:T(8,128)(2,1)S(1)} %reshape.30), channel_id=1, source_target_pairs={{0,2},{1,0},{2,1},{3,5},{4,3},{5,4},{6,8},{7,6},{8,7},{9,11},{10,9... | collective-permute-start | bytes 196616 | tf_op jit(solution)/shard_map/cond/branch_0_fun/ppermute | solution.py:20
  36.0 10.4 %collective-permute-done.1 = bf16[2,32,512]{2,1,0:T(8,128)(2,1)S(1)} collective-permute-done((bf16[2,32,512]{2,1,0:T(8,128)(2,1)S(1)}, bf16[2,32,512]{2,1,0:T(8,128)(2,1)S(1)}, u32[]{:S(2)}, u32[]{:S(2)}) %collective-permute-start.1) | collective-permute-done | bytes 65568 | tf_op jit(solution)/shard_map/cond/branch_0_fun/ppermute | solution.py:20
  46.4 3.2 %collective-permute-start.2 = (bf16[2,96,512]{2,1,0:T(8,128)(2,1)S(1)}, bf16[2,96,512]{2,1,0:T(8,128)(2,1)S(1)}, u32[]{:S(2)}, u32[]{:S(2)}) collective-permute-start(bf16[2,96,512]{2,1,0:T(8,128)(2,1)S(1)} %bitcast.78), channel_id=1, source_target_pairs={{0,3},{3,6},{6,9},{9,12},{12,15},{15,18},{18,21},{21,0},{1,4},{4,7... | collective-permute-start | bytes 589832 | tf_op jit(solution)/shard_map/cond/branch_0_fun/ppermute | solution.py:20
  49.6 3.8 %collective-permute-start.6 = (bf16[2,96,512]{2,1,0:T(8,128)(2,1)S(1)}, bf16[2,96,512]{2,1,0:T(8,128)(2,1)S(1)}, u32[]{:S(2)}, u32[]{:S(2)}) collective-permute-start(bf16[2,96,512]{2,1,0:T(8,128)(2,1)S(1)} %bitcast.79), channel_id=1, source_target_pairs={{0,21},{3,0},{6,3},{9,6},{12,9},{15,12},{18,15},{21,18},{1,22},{4,... | collective-permute-start | bytes 589832 | tf_op jit(solution)/shard_map/cond/branch_0_fun/ppermute | solution.py:20
  53.7 2.6 %collective-permute-done.2 = bf16[2,96,512]{2,1,0:T(8,128)(2,1)S(1)} collective-permute-done((bf16[2,96,512]{2,1,0:T(8,128)(2,1)S(1)}, bf16[2,96,512]{2,1,0:T(8,128)(2,1)S(1)}, u32[]{:S(2)}, u32[]{:S(2)}) %collective-permute-start.2) | collective-permute-done | bytes 196640 | tf_op jit(solution)/shard_map/cond/branch_0_fun/ppermute | solution.py:20
  56.2 1.9 %collective-permute-start.3 = (bf16[2,96,512]{2,1,0:T(8,128)(2,1)S(1)}, bf16[2,96,512]{2,1,0:T(8,128)(2,1)S(1)}, u32[]{:S(2)}, u32[]{:S(2)}) collective-permute-start(bf16[2,96,512]{2,1,0:T(8,128)(2,1)S(1)} %collective-permute-done.2), channel_id=1, source_target_pairs={{0,3},{3,6},{6,9},{9,12},{12,15},{15,18},{18,21},{21,0},{1,4},{4,7... | collective-permute-start | bytes 589832 | tf_op jit(solution)/shard_map/cond/branch_0_fun/ppermute | solution.py:20
  58.2 4.6 %collective-permute-start.7 = (bf16[2,96,512]{2,1,0:T(8,128)(2,1)S(1)}, bf16[2,96,512]{2,1,0:T(8,128)(2,1)S(1)}, u32[]{:S(2)}, u32[]{:S(2)}) collective-permute-start(bf16[2,96,512]{2,1,0:T(8,128)(2,1)S(1)} %collective-permute-done.6), channel_id=1, source_target_pairs={{0,21},{3,0},{6,3},{9,6},{12,9},{15,12},{18,15},{21,18},{1,22},{4,... | collective-permute-start | bytes 589832 | tf_op jit(solution)/shard_map/cond/branch_0_fun/ppermute | solution.py:20
  62.8 1.8 %collective-permute-done.3 = bf16[2,96,512]{2,1,0:T(8,128)(2,1)S(1)} collective-permute-done((bf16[2,96,512]{2,1,0:T(8,128)(2,1)S(1)}, bf16[2,96,512]{2,1,0:T(8,128)(2,1)S(1)}, u32[]{:S(2)}, u32[]{:S(2)}) %collective-permute-start.3) | collective-permute-done | bytes 196640 | tf_op jit(solution)/shard_map/cond/branch_0_fun/ppermute | solution.py:20
  64.6 1.9 %collective-permute-start.4 = (bf16[2,96,512]{2,1,0:T(8,128)(2,1)S(1)}, bf16[2,96,512]{2,1,0:T(8,128)(2,1)S(1)}, u32[]{:S(2)}, u32[]{:S(2)}) collective-permute-start(bf16[2,96,512]{2,1,0:T(8,128)(2,1)S(1)} %collective-permute-done.3), channel_id=1, source_target_pairs={{0,3},{3,6},{6,9},{9,12},{12,15},{15,18},{18,21},{21,0},{1,4},{4,7... | collective-permute-start | bytes 589832 | tf_op jit(solution)/shard_map/cond/branch_0_fun/ppermute | solution.py:20
  66.7 4.7 %collective-permute-start.8 = (bf16[2,96,512]{2,1,0:T(8,128)(2,1)S(1)}, bf16[2,96,512]{2,1,0:T(8,128)(2,1)S(1)}, u32[]{:S(2)}, u32[]{:S(2)}) collective-permute-start(bf16[2,96,512]{2,1,0:T(8,128)(2,1)S(1)} %collective-permute-done.7), channel_id=1, source_target_pairs={{0,21},{3,0},{6,3},{9,6},{12,9},{15,12},{18,15},{21,18},{1,22},{4,... | collective-permute-start | bytes 589832 | tf_op jit(solution)/shard_map/cond/branch_0_fun/ppermute | solution.py:20
  72.2 1.8 %collective-permute-done.8 = bf16[2,96,512]{2,1,0:T(8,128)(2,1)S(1)} collective-permute-done((bf16[2,96,512]{2,1,0:T(8,128)(2,1)S(1)}, bf16[2,96,512]{2,1,0:T(8,128)(2,1)S(1)}, u32[]{:S(2)}, u32[]{:S(2)}) %collective-permute-start.8) | collective-permute-done | bytes 196640 | tf_op jit(solution)/shard_map/cond/branch_0_fun/ppermute | solution.py:20
  74.0 5.1 %collective-permute-start.10 = (bf16[2,768,512]{2,1,0:T(8,128)(2,1)S(1)}, bf16[2,768,512]{2,1,0:T(8,128)(2,1)}, u32[]{:S(2)}, u32[]{:S(2)}) collective-permute-start(bf16[2,768,512]{2,1,0:T(8,128)(2,1)S(1)} %bitcast.71), channel_id=1, source_target_pairs={{0,24},{24,0},{1,25},{25,1},{2,26},{26,2},{3,27},{27,3},{4,28},{28... | collective-permute-start | bytes 4718600 | tf_op jit(solution)/shard_map/cond/branch_0_fun/ppermute | solution.py:20
  79.1 2.3 %collective-permute-start.5 = (bf16[2,96,512]{2,1,0:T(8,128)(2,1)S(1)}, bf16[2,96,512]{2,1,0:T(8,128)(2,1)S(1)}, u32[]{:S(2)}, u32[]{:S(2)}) collective-permute-start(bf16[2,96,512]{2,1,0:T(8,128)(2,1)S(1)} %collective-permute-done.4), channel_id=1, source_target_pairs={{0,3},{3,6},{6,9},{9,12},{12,15},{15,18},{18,21},{21,0},{1,4},{4,7... | collective-permute-start | bytes 589832 | tf_op jit(solution)/shard_map/cond/branch_0_fun/ppermute | solution.py:20
  81.4 1.3 %branch_0_fun.3.own_sum_ref = f32[3,256,512]{2,1,0:T(8,128)S(1)} custom-call(s32[4]{0:T(128)S(1)} %get-tuple-element.26.where_ref, bf16[3,256,768]{2,1,0:T(8,128)(2,1)S(1)} %copy-done.4, bf16[2,768,512]{2,1,0:T(8,128)(2,1)S(1)} %bitcast.72, bf16[3,256,1024]{2,1,0:T(8,128)(2,1)S(1)} %copy-done.2), custom_call_target="tpu_custom_call" | custom-call | flops 603979776 | bytes 4000000 | tf_op jit(solution)/shard_map/cond/branch_0_fun/pallas_call | solution.py:86
  82.8 6.9 %collective-permute-done.5.own_ref = bf16[2,96,512]{2,1,0:T(8,128)(2,1)S(1)} collective-permute-done((bf16[2,96,512]{2,1,0:T(8,128)(2,1)S(1)}, bf16[2,96,512]{2,1,0:T(8,128)(2,1)S(1)}, u32[]{:S(2)}, u32[]{:S(2)}) %collective-permute-start.5) | collective-permute-done | bytes 196640 | tf_op jit(solution)/shard_map/cond/branch_0_fun/ppermute | solution.py:20
  89.7 2.5 %collective-permute-start.9 = (bf16[2,96,512]{2,1,0:T(8,128)(2,1)S(1)}, bf16[2,96,512]{2,1,0:T(8,128)(2,1)S(1)}, u32[]{:S(2)}, u32[]{:S(2)}) collective-permute-start(bf16[2,96,512]{2,1,0:T(8,128)(2,1)S(1)} %collective-permute-done.5.own_ref), channel_id=1, source_target_pairs={{0,24},{24,0},{1,25},{25,1},{2,26},{26,2},{3,27},{27,3},{4,28},{28... | collective-permute-start | bytes 589832 | tf_op jit(solution)/shard_map/cond/branch_0_fun/ppermute | solution.py:20
  92.2 1.1 %constant_dynamic-slice_fusion.1.strip_ref = bf16[3,256,96]{2,1,0:T(8,128)(2,1)S(1)} fusion(bf16[3,256,768]{2,1,0:T(8,128)(2,1)} %get-tuple-element.27.integrals_ref, s32[]{:T(128)S(6)} %select_n.48), kind=kLoop, calls=%fused_computation.11 | loop fusion | bytes 294916 | tf_op jit(solution)/shard_map/cond/branch_0_fun/dynamic_slice | solution.py:155
  93.4 3.0 %branch_0_fun.4.other_sum_ref = f32[3,256,512]{2,1,0:T(8,128)S(1)} custom-call(s32[4]{0:T(128)S(1)} %get-tuple-element.26.where_ref, bf16[3,256,768]{2,1,0:T(8,128)(2,1)} %get-tuple-element.27.integrals_ref, bf16[2,768,512]{2,1,0:T(8,128)(2,1)} %collective-permute-done.10.block_ref, bf16[3,256,1024]{2,1,0:T(8,128)(2,1)} %get-tuple-element.29.previous_ref), custom_call_target="tpu_custom_call" | custom-call | flops 603979776 | bytes 4000000 | tf_op jit(solution)/shard_map/cond/branch_0_fun/pallas_call | solution.py:86
  96.4 2.0 %branch_0_fun.5 = bf16[3,256,1024]{2,1,0:T(8,128)(2,1)} custom-call(s32[4]{0:T(128)S(1)} %get-tuple-element.26.where_ref, bf16[3,256,96]{2,1,0:T(8,128)(2,1)S(1)} %constant_dynamic-slice_fusion.1.strip_ref, bf16[2,96,512]{2,1,0:T(8,128)(2,1)S(1)} %collective-permute-done.5.own_ref, bf16[2,96,512]{2,1,0:T(8,128)(2,1)S(1)} %collective-permute-done.9.other_ref, ...), custom_call_target="tpu_custom_call" | custom-call | tf_op jit(solution)/shard_map/cond/branch_0_fun/pallas_call | solution.py:116
  (29 shorter events, 2.7 us)
Async XLA Ops:
  1.6 22.7 %all-to-all-start.1 = ((bf16[32,16,128]{2,1,0:T(8,128)(2,1)}), bf16[32,16,128]{2,1,0:T(8,128)(2,1)S(1)}, u32[]{:S(2)}, u32[]{:S(2)}) async-start(bf16[32,16,128]{2,1,0:T(8,128)(2,1)} %get-tuple-element.43), calls=%async_computation.1 | async-start | bytes 262144 | tf_op jit(solution)/shard_map/all_to_all | solution.py:164
  24.9 11.1 %collective-permute-start = (bf16[2,32,512]{2,1,0:T(8,128)(2,1)S(1)}, bf16[2,32,512]{2,1,0:T(8,128)(2,1)S(1)}, u32[]{:S(2)}, u32[]{:S(2)}) collective-permute-start(bf16[2,32,512]{2,1,0:T(8,128)(2,1)S(1)} %reshape.30), channel_id=1, source_target_pairs={{0,1},{1,2},{2,0},{3,4},{4,5},{5,3},{6,7},{7,8},{8,6},{9,10},{10,1... | collective-permute-start | bytes 196616 | tf_op jit(solution)/shard_map/cond/branch_0_fun/ppermute | solution.py:20
  32.5 13.9 %collective-permute-start.1 = (bf16[2,32,512]{2,1,0:T(8,128)(2,1)S(1)}, bf16[2,32,512]{2,1,0:T(8,128)(2,1)S(1)}, u32[]{:S(2)}, u32[]{:S(2)}) collective-permute-start(bf16[2,32,512]{2,1,0:T(8,128)(2,1)S(1)} %reshape.30), channel_id=1, source_target_pairs={{0,2},{1,0},{2,1},{3,5},{4,3},{5,4},{6,8},{7,6},{8,7},{9,11},{10,9... | collective-permute-start | bytes 196616 | tf_op jit(solution)/shard_map/cond/branch_0_fun/ppermute | solution.py:20
  46.4 9.8 %collective-permute-start.2 = (bf16[2,96,512]{2,1,0:T(8,128)(2,1)S(1)}, bf16[2,96,512]{2,1,0:T(8,128)(2,1)S(1)}, u32[]{:S(2)}, u32[]{:S(2)}) collective-permute-start(bf16[2,96,512]{2,1,0:T(8,128)(2,1)S(1)} %bitcast.78), channel_id=1, source_target_pairs={{0,3},{3,6},{6,9},{9,12},{12,15},{15,18},{18,21},{21,0},{1,4},{4,7... | collective-permute-start | bytes 589832 | tf_op jit(solution)/shard_map/cond/branch_0_fun/ppermute | solution.py:20
  49.6 8.5 %collective-permute-start.6 = (bf16[2,96,512]{2,1,0:T(8,128)(2,1)S(1)}, bf16[2,96,512]{2,1,0:T(8,128)(2,1)S(1)}, u32[]{:S(2)}, u32[]{:S(2)}) collective-permute-start(bf16[2,96,512]{2,1,0:T(8,128)(2,1)S(1)} %bitcast.79), channel_id=1, source_target_pairs={{0,21},{3,0},{6,3},{9,6},{12,9},{15,12},{18,15},{21,18},{1,22},{4,... | collective-permute-start | bytes 589832 | tf_op jit(solution)/shard_map/cond/branch_0_fun/ppermute | solution.py:20
  56.2 8.4 %collective-permute-start.3 = (bf16[2,96,512]{2,1,0:T(8,128)(2,1)S(1)}, bf16[2,96,512]{2,1,0:T(8,128)(2,1)S(1)}, u32[]{:S(2)}, u32[]{:S(2)}) collective-permute-start(bf16[2,96,512]{2,1,0:T(8,128)(2,1)S(1)} %collective-permute-done.2), channel_id=1, source_target_pairs={{0,3},{3,6},{6,9},{9,12},{12,15},{15,18},{18,21},{21,0},{1,4},{4,7... | collective-permute-start | bytes 589832 | tf_op jit(solution)/shard_map/cond/branch_0_fun/ppermute | solution.py:20
  58.2 8.4 %collective-permute-start.7 = (bf16[2,96,512]{2,1,0:T(8,128)(2,1)S(1)}, bf16[2,96,512]{2,1,0:T(8,128)(2,1)S(1)}, u32[]{:S(2)}, u32[]{:S(2)}) collective-permute-start(bf16[2,96,512]{2,1,0:T(8,128)(2,1)S(1)} %collective-permute-done.6), channel_id=1, source_target_pairs={{0,21},{3,0},{6,3},{9,6},{12,9},{15,12},{18,15},{21,18},{1,22},{4,... | collective-permute-start | bytes 589832 | tf_op jit(solution)/shard_map/cond/branch_0_fun/ppermute | solution.py:20
  64.6 7.6 %collective-permute-start.4 = (bf16[2,96,512]{2,1,0:T(8,128)(2,1)S(1)}, bf16[2,96,512]{2,1,0:T(8,128)(2,1)S(1)}, u32[]{:S(2)}, u32[]{:S(2)}) collective-permute-start(bf16[2,96,512]{2,1,0:T(8,128)(2,1)S(1)} %collective-permute-done.3), channel_id=1, source_target_pairs={{0,3},{3,6},{6,9},{9,12},{12,15},{15,18},{18,21},{21,0},{1,4},{4,7... | collective-permute-start | bytes 589832 | tf_op jit(solution)/shard_map/cond/branch_0_fun/ppermute | solution.py:20
  66.6 14.9 %copy-start.2 = (bf16[3,256,1024]{2,1,0:T(8,128)(2,1)S(1)}, bf16[3,256,1024]{2,1,0:T(8,128)(2,1)}, u32[]{:S(2)}) copy-start(bf16[3,256,1024]{2,1,0:T(8,128)(2,1)} %get-tuple-element.29.previous_ref) | copy-start | bytes 4718596 | tf_op jit(solution)/shard_map/cond
  66.6 14.9 %copy-start.4 = (bf16[3,256,768]{2,1,0:T(8,128)(2,1)S(1)}, bf16[3,256,768]{2,1,0:T(8,128)(2,1)}, u32[]{:S(2)}) copy-start(bf16[3,256,768]{2,1,0:T(8,128)(2,1)} %get-tuple-element.27.integrals_ref) | copy-start | bytes 3538948 | tf_op jit(solution)/shard_map/cond
  66.7 7.3 %collective-permute-start.8 = (bf16[2,96,512]{2,1,0:T(8,128)(2,1)S(1)}, bf16[2,96,512]{2,1,0:T(8,128)(2,1)S(1)}, u32[]{:S(2)}, u32[]{:S(2)}) collective-permute-start(bf16[2,96,512]{2,1,0:T(8,128)(2,1)S(1)} %collective-permute-done.7), channel_id=1, source_target_pairs={{0,21},{3,0},{6,3},{9,6},{12,9},{15,12},{18,15},{21,18},{1,22},{4,... | collective-permute-start | bytes 589832 | tf_op jit(solution)/shard_map/cond/branch_0_fun/ppermute | solution.py:20
  74.0 19.3 %collective-permute-start.10 = (bf16[2,768,512]{2,1,0:T(8,128)(2,1)S(1)}, bf16[2,768,512]{2,1,0:T(8,128)(2,1)}, u32[]{:S(2)}, u32[]{:S(2)}) collective-permute-start(bf16[2,768,512]{2,1,0:T(8,128)(2,1)S(1)} %bitcast.71), channel_id=1, source_target_pairs={{0,24},{24,0},{1,25},{25,1},{2,26},{26,2},{3,27},{27,3},{4,28},{28... | collective-permute-start | bytes 4718600 | tf_op jit(solution)/shard_map/cond/branch_0_fun/ppermute | solution.py:20
  79.1 10.6 %collective-permute-start.5 = (bf16[2,96,512]{2,1,0:T(8,128)(2,1)S(1)}, bf16[2,96,512]{2,1,0:T(8,128)(2,1)S(1)}, u32[]{:S(2)}, u32[]{:S(2)}) collective-permute-start(bf16[2,96,512]{2,1,0:T(8,128)(2,1)S(1)} %collective-permute-done.4), channel_id=1, source_target_pairs={{0,3},{3,6},{6,9},{9,12},{12,15},{15,18},{18,21},{21,0},{1,4},{4,7... | collective-permute-start | bytes 589832 | tf_op jit(solution)/shard_map/cond/branch_0_fun/ppermute | solution.py:20
  89.7 6.7 %collective-permute-start.9 = (bf16[2,96,512]{2,1,0:T(8,128)(2,1)S(1)}, bf16[2,96,512]{2,1,0:T(8,128)(2,1)S(1)}, u32[]{:S(2)}, u32[]{:S(2)}) collective-permute-start(bf16[2,96,512]{2,1,0:T(8,128)(2,1)S(1)} %collective-permute-done.5.own_ref), channel_id=1, source_target_pairs={{0,24},{24,0},{1,25},{25,1},{2,26},{26,2},{3,27},{27,3},{4,28},{28... | collective-permute-start | bytes 589832 | tf_op jit(solution)/shard_map/cond/branch_0_fun/ppermute | solution.py:20

commit v4 on v3

--- a/solution.py
+++ b/solution.py
@@ -13,6 +13,7 @@
 BULK = ("bulk_0", "bulk_1")
 VMEM = pl.BlockSpec(memory_space=pltpu.VMEM)
 SMEM = pl.BlockSpec(memory_space=pltpu.SMEM)
+ANY = pl.BlockSpec(memory_space=pl.ANY)
 
 
 def shift(value, axis, step):
@@ -64,30 +65,60 @@
     )(labels, amplitudes)
 
 
-def begin_kernel(other, where_ref, integrals_ref, block_ref, previous_ref, out_ref):
-    tiles = integrals_ref.shape[0]
-    half = block_ref.shape[2]
-    core = lax.axis_index("core")
-    side = 1 - core if other else core
+def half_kernel(where_ref, integrals_ref, block_ref, previous_ref, side, begin, strip_ref, out_ref, sems):
+    tiles, _, half = strip_ref.shape
     chunk = 256
+    copies = []
     for t in range(tiles):
         slot = where_ref[t]
-        for begin in range(0, half, chunk):
-            columns = pl.ds(pl.multiple_of(side * half + begin, chunk), chunk)
+        for offset in range(0, half, chunk):
+            columns = pl.ds(pl.multiple_of(begin + offset, chunk), chunk)
             product = jnp.dot(
-                integrals_ref[t], block_ref[slot, :, begin : begin + chunk], preferred_element_type=jnp.float32
+                integrals_ref[t], block_ref[slot, :, offset : offset + chunk], preferred_element_type=jnp.float32
             )
-            out_ref[t, :, begin : begin + chunk] = previous_ref[t, :, columns].astype(jnp.float32) + product
-
-
-def begin_half(other, where, integrals, block, residual_in):
+            total = previous_ref[t, :, columns].astype(jnp.float32) + product
+            strip_ref[t, :, offset : offset + chunk] = total.astype(strip_ref.dtype)
+        target = out_ref.at[t, :, pl.ds(pl.multiple_of(side * half, half), half)]
+        copies.append(pltpu.make_async_copy(strip_ref.at[t], target, sems.at[t]))
+        copies[-1].start()
+    return copies
+
+
+def own_kernel(
+    where_ref, integrals_ref, block_ref, previous_ref, out_ref, kept_integrals_ref, kept_previous_ref, strip_ref, sems
+):
+    half = block_ref.shape[2]
+    side = lax.axis_index("core")
+    copies = half_kernel(where_ref, integrals_ref, block_ref, previous_ref, side, side * half, strip_ref, out_ref, sems)
+    kept_integrals_ref[...] = integrals_ref[...]
+    kept_previous_ref[...] = previous_ref[:, :, pl.ds(pl.multiple_of((1 - side) * half, half), half)]
+    for copy in copies:
+        copy.wait()
+
+
+def other_kernel(where_ref, integrals_ref, block_ref, previous_ref, so_far_ref, out_ref, strip_ref, sems):
+    side = 1 - lax.axis_index("core")
+    for copy in half_kernel(where_ref, integrals_ref, block_ref, previous_ref, side, 0, strip_ref, out_ref, sems):
+        copy.wait()
+
+
+def scratch(tiles, rows, half, dtype):
+    return [pltpu.VMEM((tiles, rows, half), dtype), pltpu.SemaphoreType.DMA((tiles,))]
+
+
+def own_half(where, integrals, block, residual_in):
     tiles, rows, depth = integrals.shape
     half = block.shape[2]
     return pl.pallas_call(
-        functools.partial(begin_kernel, other),
+        own_kernel,
         in_specs=[SMEM, VMEM, VMEM, VMEM],
-        out_specs=VMEM,
-        out_shape=jax.ShapeDtypeStruct((tiles, rows, half), jnp.float32),
+        out_specs=(ANY, VMEM, VMEM),
+        out_shape=(
+            jax.ShapeDtypeStruct(residual_in.shape, residual_in.dtype),
+            jax.ShapeDtypeStruct(integrals.shape, integrals.dtype),
+            jax.ShapeDtypeStruct((tiles, rows, half), residual_in.dtype),
+        ),
+        scratch_shapes=scratch(tiles, rows, half, residual_in.dtype),
         cost_estimate=pl.CostEstimate(
             flops=2 * tiles * rows * depth * half, bytes_accessed=4_000_000, transcendentals=0
         ),
@@ -95,32 +126,20 @@
     )(where, integrals, block, residual_in)
 
 
-def finish_kernel(where_ref, strip_ref, own_ref, other_ref, own_sum_ref, other_sum_ref, out_ref, rows_ref, sems):
-    tiles, _, half = own_sum_ref.shape
-    core = lax.axis_index("core")
-    copies = []
-    for t in range(tiles):
-        slot = where_ref[t]
-        for block_ref, sum_ref, side in ((own_ref, own_sum_ref, core), (other_ref, other_sum_ref, 1 - core)):
-            columns = pl.ds(pl.multiple_of(side * half, half), half)
-            product = jnp.dot(strip_ref[t], block_ref[slot], preferred_element_type=jnp.float32)
-            rows_ref[t, :, columns] = (sum_ref[t] + product).astype(rows_ref.dtype)
-        copies.append(pltpu.make_async_copy(rows_ref.at[t], out_ref.at[t], sems.at[t]))
-        copies[-1].start()
-    for copy in copies:
-        copy.wait()
-
-
-def finish(where, strip, own, other, own_sum, other_sum, like):
-    tiles = like.shape[0]
+def other_half(where, integrals, block, previous, so_far):
     return pl.pallas_call(
-        finish_kernel,
-        in_specs=[SMEM] + [VMEM] * 5,
-        out_specs=pl.BlockSpec(memory_space=pl.ANY),
-        out_shape=jax.ShapeDtypeStruct(like.shape, like.dtype),
-        scratch_shapes=[pltpu.VMEM(like.shape, like.dtype), pltpu.SemaphoreType.DMA((tiles,))],
+        other_kernel,
+        in_specs=[SMEM, VMEM, VMEM, VMEM, ANY],
+        out_specs=ANY,
+        out_shape=jax.ShapeDtypeStruct(so_far.shape, so_far.dtype),
+        scratch_shapes=scratch(*previous.shape, so_far.dtype),
+        input_output_aliases={4: 0},
         compiler_params=pltpu.CompilerParams(vmem_limit_bytes=24 * 2**20),
-    )(where, strip, own, other, own_sum, other_sum)
+    )(where, integrals, block, previous, so_far)
+
+
+def put(whole, block, at):
+    return lax.dynamic_update_slice_in_dim(whole, block[:, None], lax.rem(at + whole.shape[1], whole.shape[1]), 1)
 
 
 def with_slots(slots, incoming, where, integrals, residual_in, depth, width):
@@ -139,21 +158,18 @@
     group = group.reshape(slots, z_size * depth, half * width)
     y_size, y = lax.axis_size("bulk_0"), lax.axis_index("bulk_0")
     whole = jnp.zeros((slots, y_size, z_size * depth, half * width), mine.dtype)
-    whole = lax.dynamic_update_slice_in_dim(whole, group[:, None], y, 1)
+    whole = put(whole, group, y)
     up, down = group, group
-    for step in range(1, y_size // 2):
-        up = shift(up, "bulk_0", 1)
-        whole = lax.dynamic_update_slice_in_dim(whole, up[:, None], lax.rem(y - step + y_size, y_size), 1)
-        down = shift(down, "bulk_0", -1)
-        whole = lax.dynamic_update_slice_in_dim(whole, down[:, None], lax.rem(y + step, y_size), 1)
-    whole = whole.reshape(slots, y_size * z_size * depth, half * width)
-    up = shift(up, "bulk_0", 1)
-    own_sum = begin_half(False, where, integrals, whole, residual_in)
-    up, own_sum = lax.optimization_barrier((up, own_sum))
-    other_sum = begin_half(True, where, integrals, shift(whole, "core", 1), residual_in)
-    far = lax.rem(y + y_size // 2, y_size)
-    strip = lax.dynamic_slice_in_dim(integrals, far * (z_size * depth), z_size * depth, 2)
-    return finish(where, strip, up, shift(up, "core", 1), own_sum, other_sum, residual_in)
+    for step in range(1, y_size // 2 - 1):
+        up, down = shift(up, "bulk_0", 1), shift(down, "bulk_0", -1)
+        whole = put(put(whole, up, y - step), down, y + step)
+    last = y_size // 2 - 1
+    up, far, down = shift(up, "bulk_0", 1), shift(up, "bulk_0", 2), shift(down, "bulk_0", -1)
+    whole = put(put(put(whole, up, y - last), down, y + last), far, y + last + 1)
+    other = shift(whole, "core", 1)
+    flat = (slots, y_size * z_size * depth, half * width)
+    out, integrals, previous = own_half(where, integrals, whole.reshape(flat), residual_in)
+    return other_half(where, integrals, other.reshape(flat), previous, out)
 
 
 def local(integrals, amplitudes, residual_in, tile_irrep):

time: 99 us -> 93.7 us (0.946)
  starting transfers between devices: 54.8 us -> 51.7 us
  Pallas kernels: 7.93 us -> 5.72 us
  waiting for transfers between devices: 31.6 us -> 33 us
  local copies, waits for them, and re-layouts: 3.01 us -> 1.78 us
    ppermute x11 -> x10, starting transfers between devices: 40.7 us -> 37.6 us  [shift(): lax.ppermute(value, axis, [(i, (i + step) % size) for i in range(size)])]
    pallas_call x3 -> x2, Pallas kernels: 6.35 us -> 4.14 us  [the longest x1 2.09 us: own_half(): pl.pallas_call(own_kernel, in_specs=[SMEM, VMEM, VMEM, VMEM], out_specs=(...]
    ppermute x11 -> x10, waiting for transfers between devices: 24.3 us -> 25.5 us  [shift(): lax.ppermute(value, axis, [(i, (i + step) % size) for i in range(size)])]
    dynamic_slice x1 -> x0, local copies, waits for them, and re-layouts: 1.12 us -> none  [with_slots(): lax.dynamic_slice_in_dim(integrals, far * (z_size * depth), z_size * dept...]
  transfers between devices with their start and end apart: 12 -> 11, of which waited for: 7 -> 6; matrix products, arithmetic and copies ran while one was open for 2% -> 1% of each run, Pallas kernels for 4% -> 2%
where the time goes in v4:
time: 93.7 us; the launch traced here: 93.2 us
  starting transfers between devices  51.7 us (55%)
  waiting for transfers between devices  33 us (35%)
  Pallas kernels  5.72 us (6%)
  local copies, waits for them, and re-layouts  1.78 us (2%)
    ppermute x10, starting transfers between devices, shift(): lax.ppermute(value, axis, [(i, (i + step) % size) for i in range(size)])  37.6 us
    ppermute x10, waiting for transfers between devices, shift(): lax.ppermute(value, axis, [(i, (i + step) % size) for i in range(size)])  25.5 us
    all_to_all x1, starting transfers between devices, spread(): lax.all_to_all(outgoing, CHIP_CORE, split_axis=0, concat_axis=0, tiled=True)  14 us
    all_to_all x1, waiting for transfers between devices, spread(): lax.all_to_all(outgoing, CHIP_CORE, split_axis=0, concat_axis=0, tiled=True)  7.43 us
    pallas_call x1, Pallas kernels, own_half(): pl.pallas_call(own_kernel, in_specs=[SMEM, VMEM, VMEM, VMEM], out_specs=(...  2.09 us
    pallas_call x1, Pallas kernels, other_half(): pl.pallas_call(other_kernel, in_specs=[SMEM, VMEM, VMEM, VMEM, ANY], out_...  2.05 us
  transfers between devices with their start and end apart: 11, of which 6 were waited for; matrix products, arithmetic and copies ran while one was open for 1% of the time, Pallas kernels for 2%

profile of v4, /device:TPU:1, one launch (start us, length us, event | category | flops | bytes accessed | tf_op | source)
XLA Modules:
  0.0 93.2 jit_solution(4531018304096321419)
XLA Ops:
  0.0 1.6 %shard_map.48 = (bf16[32,16,128]{2,1,0:T(8,128)(2,1)}, s32[4]{0:T(128)S(1)}) custom-call(s32[2304]{0:T(1024)} %labels_ref.1, bf16[4,32,32]{2,1,0:T(8,128)(2,1)} %amplitudes_ref.1), custom_call_target="tpu_custom_call" | custom-call | tf_op jit(solution)/shard_map/pallas_call | solution.py:56
  1.6 14.0 %all-to-all-start.1 = ((bf16[32,16,128]{2,1,0:T(8,128)(2,1)}), bf16[32,16,128]{2,1,0:T(8,128)(2,1)S(1)}, u32[]{:S(2)}, u32[]{:S(2)}) async-start(bf16[32,16,128]{2,1,0:T(8,128)(2,1)} %get-tuple-element.45), calls=%async_computation.1 | async-start | bytes 262144 | tf_op jit(solution)/shard_map/all_to_all | solution.py:180
  15.6 0.6 slice.3
  16.9 7.4 %all-to-all-done.1 = bf16[32,16,128]{2,1,0:T(8,128)(2,1)S(1)} async-done(((bf16[32,16,128]{2,1,0:T(8,128)(2,1)}), bf16[32,16,128]{2,1,0:T(8,128)(2,1)S(1)}, u32[]{:S(2)}, u32[]{:S(2)}) %all-to-all-start.1) | async-done | bytes 131104 | tf_op jit(solution)/shard_map/all_to_all | solution.py:180
  24.3 68.9 %conditional.1 = (bf16[3,256,1024]{2,1,0:T(8,128)(2,1)}) conditional(s32[]{:T(128)} %bitcast.62, (bf16[32,16,128]{2,1,0:T(8,128)(2,1)S(1)}, s32[4]{0:T(128)S(1)}, bf16[3,256,768]{2,1,0:T(8,128)(2,1)}, bf16[3,256,1024]{2,1,0:T(8,128)(2,1)}) %tuple.11, (s32[2304]{0:T(1024)}, bf16[4,32,32]{2,1,0:T(8,128)(2,1)}, s32[4]{0:T(128)S(1)}, ...), branch_computations={%region_0.0_spmd, %region_1.0_spmd} | conditional | flops 603979904 | bytes 43028372 | solution.py:192
  24.6 0.2 reshape.34
  24.9 8.8 %collective-permute-start.1 = (bf16[2,32,512]{2,1,0:T(8,128)(2,1)S(1)}, bf16[2,32,512]{2,1,0:T(8,128)(2,1)S(1)}, u32[]{:S(2)}, u32[]{:S(2)}) collective-permute-start(bf16[2,32,512]{2,1,0:T(8,128)(2,1)S(1)} %reshape.34), channel_id=1, source_target_pairs={{0,2},{1,0},{2,1},{3,5},{4,3},{5,4},{6,8},{7,6},{8,7},{9,11},{10,9... | collective-permute-start | bytes 196616 | tf_op jit(solution)/shard_map/cond/branch_0_fun/ppermute | solution.py:21
  33.7 1.9 %collective-permute-start = (bf16[2,32,512]{2,1,0:T(8,128)(2,1)S(1)}, bf16[2,32,512]{2,1,0:T(8,128)(2,1)S(1)}, u32[]{:S(2)}, u32[]{:S(2)}) collective-permute-start(bf16[2,32,512]{2,1,0:T(8,128)(2,1)S(1)} %reshape.34), channel_id=1, source_target_pairs={{0,1},{1,2},{2,0},{3,4},{4,5},{5,3},{6,7},{7,8},{8,6},{9,10},{10,1... | collective-permute-start | bytes 196616 | tf_op jit(solution)/shard_map/cond/branch_0_fun/ppermute | solution.py:21
  35.6 0.2 reshape.33
  35.9 10.0 %collective-permute-done = bf16[2,32,512]{2,1,0:T(8,128)(2,1)S(1)} collective-permute-done((bf16[2,32,512]{2,1,0:T(8,128)(2,1)S(1)}, bf16[2,32,512]{2,1,0:T(8,128)(2,1)S(1)}, u32[]{:S(2)}, u32[]{:S(2)}) %collective-permute-start) | collective-permute-done | bytes 65568 | tf_op jit(solution)/shard_map/cond/branch_0_fun/ppermute | solution.py:21
  46.0 5.1 %collective-permute-start.3 = (bf16[2,96,512]{2,1,0:T(8,128)(2,1)S(1)}, bf16[2,96,512]{2,1,0:T(8,128)(2,1)S(1)}, u32[]{:S(2)}, u32[]{:S(2)}) collective-permute-start(bf16[2,96,512]{2,1,0:T(8,128)(2,1)S(1)} %bitcast.104), channel_id=1, source_target_pairs={{0,21},{3,0},{6,3},{9,6},{12,9},{15,12},{18,15},{21,18},{1,22},{4,... | collective-permute-start | bytes 589832 | tf_op jit(solution)/shard_map/cond/branch_0_fun/ppermute | solution.py:21
  51.1 1.9 %collective-permute-start.2 = (bf16[2,96,512]{2,1,0:T(8,128)(2,1)S(1)}, bf16[2,96,512]{2,1,0:T(8,128)(2,1)S(1)}, u32[]{:S(2)}, u32[]{:S(2)}) collective-permute-start(bf16[2,96,512]{2,1,0:T(8,128)(2,1)S(1)} %bitcast.105), channel_id=1, source_target_pairs={{0,3},{3,6},{6,9},{9,12},{12,15},{15,18},{18,21},{21,0},{1,4},{4,7... | collective-permute-start | bytes 589832 | tf_op jit(solution)/shard_map/cond/branch_0_fun/ppermute | solution.py:21
  53.3 1.6 %collective-permute-done.3 = bf16[2,96,512]{2,1,0:T(8,128)(2,1)S(1)} collective-permute-done((bf16[2,96,512]{2,1,0:T(8,128)(2,1)S(1)}, bf16[2,96,512]{2,1,0:T(8,128)(2,1)S(1)}, u32[]{:S(2)}, u32[]{:S(2)}) %collective-permute-start.3) | collective-permute-done | bytes 196640 | tf_op jit(solution)/shard_map/cond/branch_0_fun/ppermute | solution.py:21
  54.8 5.3 %collective-permute-start.5 = (bf16[2,96,512]{2,1,0:T(8,128)(2,1)S(1)}, bf16[2,96,512]{2,1,0:T(8,128)(2,1)S(1)}, u32[]{:S(2)}, u32[]{:S(2)}) collective-permute-start(bf16[2,96,512]{2,1,0:T(8,128)(2,1)S(1)} %collective-permute-done.3), channel_id=1, source_target_pairs={{0,21},{3,0},{6,3},{9,6},{12,9},{15,12},{18,15},{21,18},{1,22},{4,... | collective-permute-start | bytes 589832 | tf_op jit(solution)/shard_map/cond/branch_0_fun/ppermute | solution.py:21
  60.2 1.9 %collective-permute-start.4 = (bf16[2,96,512]{2,1,0:T(8,128)(2,1)S(1)}, bf16[2,96,512]{2,1,0:T(8,128)(2,1)S(1)}, u32[]{:S(2)}, u32[]{:S(2)}) collective-permute-start(bf16[2,96,512]{2,1,0:T(8,128)(2,1)S(1)} %collective-permute-done.2), channel_id=1, source_target_pairs={{0,3},{3,6},{6,9},{9,12},{12,15},{15,18},{18,21},{21,0},{1,4},{4,7... | collective-permute-start | bytes 589832 | tf_op jit(solution)/shard_map/cond/branch_0_fun/ppermute | solution.py:21
  62.2 5.6 %collective-permute-done.4 = bf16[2,96,512]{2,1,0:T(8,128)(2,1)S(1)} collective-permute-done((bf16[2,96,512]{2,1,0:T(8,128)(2,1)S(1)}, bf16[2,96,512]{2,1,0:T(8,128)(2,1)S(1)}, u32[]{:S(2)}, u32[]{:S(2)}) %collective-permute-start.4) | collective-permute-done | bytes 196640 | tf_op jit(solution)/shard_map/cond/branch_0_fun/ppermute | solution.py:21
  67.8 1.9 %collective-permute-start.8 = (bf16[2,96,512]{2,1,0:T(8,128)(2,1)S(1)}, bf16[2,96,512]{2,1,0:T(8,128)(2,1)S(1)}, u32[]{:S(2)}, u32[]{:S(2)}) collective-permute-start(bf16[2,96,512]{2,1,0:T(8,128)(2,1)S(1)} %collective-permute-done.4), channel_id=1, source_target_pairs={{0,6},{3,9},{6,12},{9,15},{12,18},{15,21},{18,0},{21,3},{1,7},{4,1... | collective-permute-start | bytes 589832 | tf_op jit(solution)/shard_map/cond/branch_0_fun/ppermute | solution.py:21
  69.7 1.9 %collective-permute-start.6 = (bf16[2,96,512]{2,1,0:T(8,128)(2,1)S(1)}, bf16[2,96,512]{2,1,0:T(8,128)(2,1)S(1)}, u32[]{:S(2)}, u32[]{:S(2)}) collective-permute-start(bf16[2,96,512]{2,1,0:T(8,128)(2,1)S(1)} %collective-permute-done.4), channel_id=1, source_target_pairs={{0,3},{3,6},{6,9},{9,12},{12,15},{15,18},{18,21},{21,0},{1,4},{4,7... | collective-permute-start | bytes 589832 | tf_op jit(solution)/shard_map/cond/branch_0_fun/ppermute | solution.py:21
  71.7 4.6 %collective-permute-start.7 = (bf16[2,96,512]{2,1,0:T(8,128)(2,1)S(1)}, bf16[2,96,512]{2,1,0:T(8,128)(2,1)S(1)}, u32[]{:S(2)}, u32[]{:S(2)}) collective-permute-start(bf16[2,96,512]{2,1,0:T(8,128)(2,1)S(1)} %collective-permute-done.5), channel_id=1, source_target_pairs={{0,21},{3,0},{6,3},{9,6},{12,9},{15,12},{18,15},{21,18},{1,22},{4,... | collective-permute-start | bytes 589832 | tf_op jit(solution)/shard_map/cond/branch_0_fun/ppermute | solution.py:21
  76.3 7.4 %collective-permute-done.6 = bf16[2,96,512]{2,1,0:T(8,128)(2,1)S(1)} collective-permute-done((bf16[2,96,512]{2,1,0:T(8,128)(2,1)S(1)}, bf16[2,96,512]{2,1,0:T(8,128)(2,1)S(1)}, u32[]{:S(2)}, u32[]{:S(2)}) %collective-permute-start.6) | collective-permute-done | bytes 196640 | tf_op jit(solution)/shard_map/cond/branch_0_fun/ppermute | solution.py:21
  83.8 4.3 %collective-permute-start.9 = (bf16[2,8,96,512]{3,2,1,0:T(8,128)(2,1)S(1)}, bf16[2,8,96,512]{3,2,1,0:T(8,128)(2,1)S(1)}, u32[]{:S(2)}, u32[]{:S(2)}) collective-permute-start(bf16[2,8,96,512]{3,2,1,0:T(8,128)(2,1)S(1)} %bitcast_dynamic-update-slice_fusion.6), channel_id=1, source_target_pairs={{0,24},{24,0},{1,25},{25,1},{2,26},{26,2},{3,27},{27,3},{4,28},{28... | collective-permute-start | bytes 4718600 | tf_op jit(solution)/shard_map/cond/branch_0_fun/ppermute | solution.py:21
  88.1 2.1 %branch_0_fun.2 = (bf16[3,256,1024]{2,1,0:T(8,128)(2,1)}, bf16[3,256,768]{2,1,0:T(8,128)(2,1)S(1)}, bf16[3,256,512]{2,1,0:T(8,128)(2,1)S(1)}) custom-call(s32[4]{0:T(128)S(1)} %get-tuple-element.26.where_ref, bf16[3,256,768]{2,1,0:T(8,128)(2,1)S(1)} %copy-done.2, bf16[2,768,512]{2,1,0:T(8,128)(2,1)S(1)} %bitcast.96, bf16[3,256,1024]{2,1,0:T(8,128)(2,1)S(1)} %copy-done), custom_call_target="tpu_custom_call" | custom-call | flops 603979776 | bytes 4000000 | tf_op jit(solution)/shard_map/cond/branch_0_fun/pallas_call | solution.py:112
  90.2 0.9 collective-permute-done.9
  91.1 2.0 %branch_0_fun.3 = bf16[3,256,1024]{2,1,0:T(8,128)(2,1)} custom-call(s32[4]{0:T(128)S(1)} %get-tuple-element.26.where_ref, bf16[3,256,768]{2,1,0:T(8,128)(2,1)S(1)} %get-tuple-element.30.integrals_ref, bf16[2,768,512]{2,1,0:T(8,128)(2,1)S(1)} %bitcast.98, bf16[3,256,512]{2,1,0:T(8,128)(2,1)S(1)} %get-tuple-element.31.previous_ref, ...), custom_call_target="tpu_custom_call", output_to_operand_aliasing={{}: (4, {})} | custom-call | tf_op jit(solution)/shard_map/cond/branch_0_fun/pallas_call | solution.py:130
  (25 shorter events, 0.7 us)
Async XLA Ops:
  1.6 22.7 %all-to-all-start.1 = ((bf16[32,16,128]{2,1,0:T(8,128)(2,1)}), bf16[32,16,128]{2,1,0:T(8,128)(2,1)S(1)}, u32[]{:S(2)}, u32[]{:S(2)}) async-start(bf16[32,16,128]{2,1,0:T(8,128)(2,1)} %get-tuple-element.45), calls=%async_computation.1 | async-start | bytes 262144 | tf_op jit(solution)/shard_map/all_to_all | solution.py:180
  24.9 21.1 %collective-permute-start.1 = (bf16[2,32,512]{2,1,0:T(8,128)(2,1)S(1)}, bf16[2,32,512]{2,1,0:T(8,128)(2,1)S(1)}, u32[]{:S(2)}, u32[]{:S(2)}) collective-permute-start(bf16[2,32,512]{2,1,0:T(8,128)(2,1)S(1)} %reshape.34), channel_id=1, source_target_pairs={{0,2},{1,0},{2,1},{3,5},{4,3},{5,4},{6,8},{7,6},{8,7},{9,11},{10,9... | collective-permute-start | bytes 196616 | tf_op jit(solution)/shard_map/cond/branch_0_fun/ppermute | solution.py:21
  33.7 12.3 %collective-permute-start = (bf16[2,32,512]{2,1,0:T(8,128)(2,1)S(1)}, bf16[2,32,512]{2,1,0:T(8,128)(2,1)S(1)}, u32[]{:S(2)}, u32[]{:S(2)}) collective-permute-start(bf16[2,32,512]{2,1,0:T(8,128)(2,1)S(1)} %reshape.34), channel_id=1, source_target_pairs={{0,1},{1,2},{2,0},{3,4},{4,5},{5,3},{6,7},{7,8},{8,6},{9,10},{10,1... | collective-permute-start | bytes 196616 | tf_op jit(solution)/shard_map/cond/branch_0_fun/ppermute | solution.py:21
  46.0 8.8 %collective-permute-start.3 = (bf16[2,96,512]{2,1,0:T(8,128)(2,1)S(1)}, bf16[2,96,512]{2,1,0:T(8,128)(2,1)S(1)}, u32[]{:S(2)}, u32[]{:S(2)}) collective-permute-start(bf16[2,96,512]{2,1,0:T(8,128)(2,1)S(1)} %bitcast.104), channel_id=1, source_target_pairs={{0,21},{3,0},{6,3},{9,6},{12,9},{15,12},{18,15},{21,18},{1,22},{4,... | collective-permute-start | bytes 589832 | tf_op jit(solution)/shard_map/cond/branch_0_fun/ppermute | solution.py:21
  51.1 9.1 %collective-permute-start.2 = (bf16[2,96,512]{2,1,0:T(8,128)(2,1)S(1)}, bf16[2,96,512]{2,1,0:T(8,128)(2,1)S(1)}, u32[]{:S(2)}, u32[]{:S(2)}) collective-permute-start(bf16[2,96,512]{2,1,0:T(8,128)(2,1)S(1)} %bitcast.105), channel_id=1, source_target_pairs={{0,3},{3,6},{6,9},{9,12},{12,15},{15,18},{18,21},{21,0},{1,4},{4,7... | collective-permute-start | bytes 589832 | tf_op jit(solution)/shard_map/cond/branch_0_fun/ppermute | solution.py:21
  53.2 34.8 %copy-start = (bf16[3,256,1024]{2,1,0:T(8,128)(2,1)S(1)}, bf16[3,256,1024]{2,1,0:T(8,128)(2,1)}, u32[]{:S(2)}) copy-start(bf16[3,256,1024]{2,1,0:T(8,128)(2,1)} %get-tuple-element.29.previous_ref) | copy-start | bytes 4718596 | tf_op jit(solution)/shard_map/cond
  53.3 34.8 %copy-start.2 = (bf16[3,256,768]{2,1,0:T(8,128)(2,1)S(1)}, bf16[3,256,768]{2,1,0:T(8,128)(2,1)}, u32[]{:S(2)}) copy-start(bf16[3,256,768]{2,1,0:T(8,128)(2,1)} %get-tuple-element.27.integrals_ref) | copy-start | bytes 3538948 | tf_op jit(solution)/shard_map/cond
  54.8 16.8 %collective-permute-start.5 = (bf16[2,96,512]{2,1,0:T(8,128)(2,1)S(1)}, bf16[2,96,512]{2,1,0:T(8,128)(2,1)S(1)}, u32[]{:S(2)}, u32[]{:S(2)}) collective-permute-start(bf16[2,96,512]{2,1,0:T(8,128)(2,1)S(1)} %collective-permute-done.3), channel_id=1, source_target_pairs={{0,21},{3,0},{6,3},{9,6},{12,9},{15,12},{18,15},{21,18},{1,22},{4,... | collective-permute-start | bytes 589832 | tf_op jit(solution)/shard_map/cond/branch_0_fun/ppermute | solution.py:21
  60.2 7.6 %collective-permute-start.4 = (bf16[2,96,512]{2,1,0:T(8,128)(2,1)S(1)}, bf16[2,96,512]{2,1,0:T(8,128)(2,1)S(1)}, u32[]{:S(2)}, u32[]{:S(2)}) collective-permute-start(bf16[2,96,512]{2,1,0:T(8,128)(2,1)S(1)} %collective-permute-done.2), channel_id=1, source_target_pairs={{0,3},{3,6},{6,9},{9,12},{12,15},{15,18},{18,21},{21,0},{1,4},{4,7... | collective-permute-start | bytes 589832 | tf_op jit(solution)/shard_map/cond/branch_0_fun/ppermute | solution.py:21
  67.8 16.0 %collective-permute-start.8 = (bf16[2,96,512]{2,1,0:T(8,128)(2,1)S(1)}, bf16[2,96,512]{2,1,0:T(8,128)(2,1)S(1)}, u32[]{:S(2)}, u32[]{:S(2)}) collective-permute-start(bf16[2,96,512]{2,1,0:T(8,128)(2,1)S(1)} %collective-permute-done.4), channel_id=1, source_target_pairs={{0,6},{3,9},{6,12},{9,15},{12,18},{15,21},{18,0},{21,3},{1,7},{4,1... | collective-permute-start | bytes 589832 | tf_op jit(solution)/shard_map/cond/branch_0_fun/ppermute | solution.py:21
  69.7 14.0 %collective-permute-start.6 = (bf16[2,96,512]{2,1,0:T(8,128)(2,1)S(1)}, bf16[2,96,512]{2,1,0:T(8,128)(2,1)S(1)}, u32[]{:S(2)}, u32[]{:S(2)}) collective-permute-start(bf16[2,96,512]{2,1,0:T(8,128)(2,1)S(1)} %collective-permute-done.4), channel_id=1, source_target_pairs={{0,3},{3,6},{6,9},{9,12},{12,15},{15,18},{18,21},{21,0},{1,4},{4,7... | collective-permute-start | bytes 589832 | tf_op jit(solution)/shard_map/cond/branch_0_fun/ppermute | solution.py:21
  71.7 12.1 %collective-permute-start.7 = (bf16[2,96,512]{2,1,0:T(8,128)(2,1)S(1)}, bf16[2,96,512]{2,1,0:T(8,128)(2,1)S(1)}, u32[]{:S(2)}, u32[]{:S(2)}) collective-permute-start(bf16[2,96,512]{2,1,0:T(8,128)(2,1)S(1)} %collective-permute-done.5), channel_id=1, source_target_pairs={{0,21},{3,0},{6,3},{9,6},{12,9},{15,12},{18,15},{21,18},{1,22},{4,... | collective-permute-start | bytes 589832 | tf_op jit(solution)/shard_map/cond/branch_0_fun/ppermute | solution.py:21
  83.8 7.3 %collective-permute-start.9 = (bf16[2,8,96,512]{3,2,1,0:T(8,128)(2,1)S(1)}, bf16[2,8,96,512]{3,2,1,0:T(8,128)(2,1)S(1)}, u32[]{:S(2)}, u32[]{:S(2)}) collective-permute-start(bf16[2,8,96,512]{3,2,1,0:T(8,128)(2,1)S(1)} %bitcast_dynamic-update-slice_fusion.6), channel_id=1, source_target_pairs={{0,24},{24,0},{1,25},{25,1},{2,26},{26,2},{3,27},{27,3},{4,28},{28... | collective-permute-start | bytes 4718600 | tf_op jit(solution)/shard_map/cond/branch_0_fun/ppermute | solution.py:21

commit v5 on v4

--- a/solution.py
+++ b/solution.py
@@ -164,7 +164,7 @@
         up, down = shift(up, "bulk_0", 1), shift(down, "bulk_0", -1)
         whole = put(put(whole, up, y - step), down, y + step)
     last = y_size // 2 - 1
-    up, far, down = shift(up, "bulk_0", 1), shift(up, "bulk_0", 2), shift(down, "bulk_0", -1)
+    far, up, down = shift(down, "bulk_0", -2), shift(up, "bulk_0", 1), shift(down, "bulk_0", -1)
     whole = put(put(put(whole, up, y - last), down, y + last), far, y + last + 1)
     other = shift(whole, "core", 1)
     flat = (slots, y_size * z_size * depth, half * width)

time: 93.7 us -> 90 us (0.961)
  waiting for transfers between devices: 33 us -> 28.7 us
    ppermute x10, waiting for transfers between devices: 25.5 us -> 21.2 us  [shift(): lax.ppermute(value, axis, [(i, (i + step) % size) for i in range(size)])]
  transfers between devices with their start and end apart: 11 -> 11, of which waited for: 6 -> 7; matrix products, arithmetic and copies ran while one was open for 1% -> 1% of each run, Pallas kernels for 2% -> 2%
where the time goes in v5:
time: 90 us; the launch traced here: 89.5 us
  starting transfers between devices  52.3 us (58%)
  waiting for transfers between devices  28.7 us (32%)
  Pallas kernels  5.72 us (6%)
  local copies, waits for them, and re-layouts  1.77 us (2%)
    ppermute x10, starting transfers between devices, shift(): lax.ppermute(value, axis, [(i, (i + step) % size) for i in range(size)])  38.3 us
    ppermute x10, waiting for transfers between devices, shift(): lax.ppermute(value, axis, [(i, (i + step) % size) for i in range(size)])  21.2 us
    all_to_all x1, starting transfers between devices, spread(): lax.all_to_all(outgoing, CHIP_CORE, split_axis=0, concat_axis=0, tiled=True)  14 us
    all_to_all x1, waiting for transfers between devices, spread(): lax.all_to_all(outgoing, CHIP_CORE, split_axis=0, concat_axis=0, tiled=True)  7.43 us
    pallas_call x1, Pallas kernels, own_half(): pl.pallas_call(own_kernel, in_specs=[SMEM, VMEM, VMEM, VMEM], out_specs=(...  2.1 us
    pallas_call x1, Pallas kernels, other_half(): pl.pallas_call(other_kernel, in_specs=[SMEM, VMEM, VMEM, VMEM, ANY], out_...  2.05 us
  transfers between devices with their start and end apart: 11, of which 7 were waited for; matrix products, arithmetic and copies ran while one was open for 1% of the time, Pallas kernels for 2%

profile of v5, /device:TPU:1, one launch (start us, length us, event | category | flops | bytes accessed | tf_op | source)
XLA Modules:
  0.0 89.5 jit_solution(5195428837960323179)
XLA Ops:
  0.0 1.6 %shard_map.48 = (bf16[32,16,128]{2,1,0:T(8,128)(2,1)}, s32[4]{0:T(128)S(1)}) custom-call(s32[2304]{0:T(1024)} %labels_ref.1, bf16[4,32,32]{2,1,0:T(8,128)(2,1)} %amplitudes_ref.1), custom_call_target="tpu_custom_call" | custom-call | tf_op jit(solution)/shard_map/pallas_call | solution.py:56
  1.6 14.0 %all-to-all-start.1 = ((bf16[32,16,128]{2,1,0:T(8,128)(2,1)}), bf16[32,16,128]{2,1,0:T(8,128)(2,1)S(1)}, u32[]{:S(2)}, u32[]{:S(2)}) async-start(bf16[32,16,128]{2,1,0:T(8,128)(2,1)} %get-tuple-element.45), calls=%async_computation.1 | async-start | bytes 262144 | tf_op jit(solution)/shard_map/all_to_all | solution.py:180
  15.6 0.6 slice.3
  16.9 7.4 %all-to-all-done.1 = bf16[32,16,128]{2,1,0:T(8,128)(2,1)S(1)} async-done(((bf16[32,16,128]{2,1,0:T(8,128)(2,1)}), bf16[32,16,128]{2,1,0:T(8,128)(2,1)S(1)}, u32[]{:S(2)}, u32[]{:S(2)}) %all-to-all-start.1) | async-done | bytes 131104 | tf_op jit(solution)/shard_map/all_to_all | solution.py:180
  24.3 65.2 %conditional.1 = (bf16[3,256,1024]{2,1,0:T(8,128)(2,1)}) conditional(s32[]{:T(128)} %bitcast.62, (bf16[32,16,128]{2,1,0:T(8,128)(2,1)S(1)}, s32[4]{0:T(128)S(1)}, bf16[3,256,768]{2,1,0:T(8,128)(2,1)}, bf16[3,256,1024]{2,1,0:T(8,128)(2,1)}) %tuple.11, (s32[2304]{0:T(1024)}, bf16[4,32,32]{2,1,0:T(8,128)(2,1)}, s32[4]{0:T(128)S(1)}, ...), branch_computations={%region_0.0_spmd, %region_1.0_spmd} | conditional | flops 603979904 | bytes 43028372 | solution.py:192
  24.6 0.2 reshape.34
  24.9 8.8 %collective-permute-start.1 = (bf16[2,32,512]{2,1,0:T(8,128)(2,1)S(1)}, bf16[2,32,512]{2,1,0:T(8,128)(2,1)S(1)}, u32[]{:S(2)}, u32[]{:S(2)}) collective-permute-start(bf16[2,32,512]{2,1,0:T(8,128)(2,1)S(1)} %reshape.34), channel_id=1, source_target_pairs={{0,2},{1,0},{2,1},{3,5},{4,3},{5,4},{6,8},{7,6},{8,7},{9,11},{10,9... | collective-permute-start | bytes 196616 | tf_op jit(solution)/shard_map/cond/branch_0_fun/ppermute | solution.py:21
  33.7 1.9 %collective-permute-start = (bf16[2,32,512]{2,1,0:T(8,128)(2,1)S(1)}, bf16[2,32,512]{2,1,0:T(8,128)(2,1)S(1)}, u32[]{:S(2)}, u32[]{:S(2)}) collective-permute-start(bf16[2,32,512]{2,1,0:T(8,128)(2,1)S(1)} %reshape.34), channel_id=1, source_target_pairs={{0,1},{1,2},{2,0},{3,4},{4,5},{5,3},{6,7},{7,8},{8,6},{9,10},{10,1... | collective-permute-start | bytes 196616 | tf_op jit(solution)/shard_map/cond/branch_0_fun/ppermute | solution.py:21
  35.9 10.0 %collective-permute-done = bf16[2,32,512]{2,1,0:T(8,128)(2,1)S(1)} collective-permute-done((bf16[2,32,512]{2,1,0:T(8,128)(2,1)S(1)}, bf16[2,32,512]{2,1,0:T(8,128)(2,1)S(1)}, u32[]{:S(2)}, u32[]{:S(2)}) %collective-permute-start) | collective-permute-done | bytes 65568 | tf_op jit(solution)/shard_map/cond/branch_0_fun/ppermute | solution.py:21
  46.0 5.1 %collective-permute-start.3 = (bf16[2,96,512]{2,1,0:T(8,128)(2,1)S(1)}, bf16[2,96,512]{2,1,0:T(8,128)(2,1)S(1)}, u32[]{:S(2)}, u32[]{:S(2)}) collective-permute-start(bf16[2,96,512]{2,1,0:T(8,128)(2,1)S(1)} %bitcast.104), channel_id=1, source_target_pairs={{0,21},{3,0},{6,3},{9,6},{12,9},{15,12},{18,15},{21,18},{1,22},{4,... | collective-permute-start | bytes 589832 | tf_op jit(solution)/shard_map/cond/branch_0_fun/ppermute | solution.py:21
  51.1 1.9 %collective-permute-start.2 = (bf16[2,96,512]{2,1,0:T(8,128)(2,1)S(1)}, bf16[2,96,512]{2,1,0:T(8,128)(2,1)S(1)}, u32[]{:S(2)}, u32[]{:S(2)}) collective-permute-start(bf16[2,96,512]{2,1,0:T(8,128)(2,1)S(1)} %bitcast.105), channel_id=1, source_target_pairs={{0,3},{3,6},{6,9},{9,12},{12,15},{15,18},{18,21},{21,0},{1,4},{4,7... | collective-permute-start | bytes 589832 | tf_op jit(solution)/shard_map/cond/branch_0_fun/ppermute | solution.py:21
  53.3 1.6 %collective-permute-done.3 = bf16[2,96,512]{2,1,0:T(8,128)(2,1)S(1)} collective-permute-done((bf16[2,96,512]{2,1,0:T(8,128)(2,1)S(1)}, bf16[2,96,512]{2,1,0:T(8,128)(2,1)S(1)}, u32[]{:S(2)}, u32[]{:S(2)}) %collective-permute-start.3) | collective-permute-done | bytes 196640 | tf_op jit(solution)/shard_map/cond/branch_0_fun/ppermute | solution.py:21
  54.8 5.3 %collective-permute-start.5 = (bf16[2,96,512]{2,1,0:T(8,128)(2,1)S(1)}, bf16[2,96,512]{2,1,0:T(8,128)(2,1)S(1)}, u32[]{:S(2)}, u32[]{:S(2)}) collective-permute-start(bf16[2,96,512]{2,1,0:T(8,128)(2,1)S(1)} %collective-permute-done.3), channel_id=1, source_target_pairs={{0,21},{3,0},{6,3},{9,6},{12,9},{15,12},{18,15},{21,18},{1,22},{4,... | collective-permute-start | bytes 589832 | tf_op jit(solution)/shard_map/cond/branch_0_fun/ppermute | solution.py:21
  60.2 1.9 %collective-permute-start.4 = (bf16[2,96,512]{2,1,0:T(8,128)(2,1)S(1)}, bf16[2,96,512]{2,1,0:T(8,128)(2,1)S(1)}, u32[]{:S(2)}, u32[]{:S(2)}) collective-permute-start(bf16[2,96,512]{2,1,0:T(8,128)(2,1)S(1)} %collective-permute-done.2), channel_id=1, source_target_pairs={{0,3},{3,6},{6,9},{9,12},{12,15},{15,18},{18,21},{21,0},{1,4},{4,7... | collective-permute-start | bytes 589832 | tf_op jit(solution)/shard_map/cond/branch_0_fun/ppermute | solution.py:21
  62.2 0.8 collective-permute-done.5
  63.0 4.0 %collective-permute-start.8 = (bf16[2,96,512]{2,1,0:T(8,128)(2,1)S(1)}, bf16[2,96,512]{2,1,0:T(8,128)(2,1)S(1)}, u32[]{:S(2)}, u32[]{:S(2)}) collective-permute-start(bf16[2,96,512]{2,1,0:T(8,128)(2,1)S(1)} %collective-permute-done.5), channel_id=1, source_target_pairs={{0,18},{3,21},{6,0},{9,3},{12,6},{15,9},{18,12},{21,15},{1,19},{4,... | collective-permute-start | bytes 589832 | tf_op jit(solution)/shard_map/cond/branch_0_fun/ppermute | solution.py:21
  67.0 3.2 %collective-permute-start.7 = (bf16[2,96,512]{2,1,0:T(8,128)(2,1)S(1)}, bf16[2,96,512]{2,1,0:T(8,128)(2,1)S(1)}, u32[]{:S(2)}, u32[]{:S(2)}) collective-permute-start(bf16[2,96,512]{2,1,0:T(8,128)(2,1)S(1)} %collective-permute-done.5), channel_id=1, source_target_pairs={{0,21},{3,0},{6,3},{9,6},{12,9},{15,12},{18,15},{21,18},{1,22},{4,... | collective-permute-start | bytes 589832 | tf_op jit(solution)/shard_map/cond/branch_0_fun/ppermute | solution.py:21
  70.2 3.1 %collective-permute-start.6 = (bf16[2,96,512]{2,1,0:T(8,128)(2,1)S(1)}, bf16[2,96,512]{2,1,0:T(8,128)(2,1)S(1)}, u32[]{:S(2)}, u32[]{:S(2)}) collective-permute-start(bf16[2,96,512]{2,1,0:T(8,128)(2,1)S(1)} %collective-permute-done.4), channel_id=1, source_target_pairs={{0,3},{3,6},{6,9},{9,12},{12,15},{15,18},{18,21},{21,0},{1,4},{4,7... | collective-permute-start | bytes 589832 | tf_op jit(solution)/shard_map/cond/branch_0_fun/ppermute | solution.py:21
  73.4 4.5 %collective-permute-done.6 = bf16[2,96,512]{2,1,0:T(8,128)(2,1)S(1)} collective-permute-done((bf16[2,96,512]{2,1,0:T(8,128)(2,1)S(1)}, bf16[2,96,512]{2,1,0:T(8,128)(2,1)S(1)}, u32[]{:S(2)}, u32[]{:S(2)}) %collective-permute-start.6) | collective-permute-done | bytes 196640 | tf_op jit(solution)/shard_map/cond/branch_0_fun/ppermute | solution.py:21
  77.9 3.5 %collective-permute-done.7 = bf16[2,96,512]{2,1,0:T(8,128)(2,1)S(1)} collective-permute-done((bf16[2,96,512]{2,1,0:T(8,128)(2,1)S(1)}, bf16[2,96,512]{2,1,0:T(8,128)(2,1)S(1)}, u32[]{:S(2)}, u32[]{:S(2)}) %collective-permute-start.7) | collective-permute-done | bytes 196640 | tf_op jit(solution)/shard_map/cond/branch_0_fun/ppermute | solution.py:21
  81.4 3.0 %collective-permute-start.9 = (bf16[2,8,96,512]{3,2,1,0:T(8,128)(2,1)S(1)}, bf16[2,8,96,512]{3,2,1,0:T(8,128)(2,1)S(1)}, u32[]{:S(2)}, u32[]{:S(2)}) collective-permute-start(bf16[2,8,96,512]{3,2,1,0:T(8,128)(2,1)S(1)} %bitcast_dynamic-update-slice_fusion.6), channel_id=1, source_target_pairs={{0,24},{24,0},{1,25},{25,1},{2,26},{26,2},{3,27},{27,3},{4,28},{28... | collective-permute-start | bytes 4718600 | tf_op jit(solution)/shard_map/cond/branch_0_fun/ppermute | solution.py:21
  84.4 2.1 %branch_0_fun.2 = (bf16[3,256,1024]{2,1,0:T(8,128)(2,1)}, bf16[3,256,768]{2,1,0:T(8,128)(2,1)S(1)}, bf16[3,256,512]{2,1,0:T(8,128)(2,1)S(1)}) custom-call(s32[4]{0:T(128)S(1)} %get-tuple-element.26.where_ref, bf16[3,256,768]{2,1,0:T(8,128)(2,1)S(1)} %copy-done.2, bf16[2,768,512]{2,1,0:T(8,128)(2,1)S(1)} %bitcast.96, bf16[3,256,1024]{2,1,0:T(8,128)(2,1)S(1)} %copy-done), custom_call_target="tpu_custom_call" | custom-call | flops 603979776 | bytes 4000000 | tf_op jit(solution)/shard_map/cond/branch_0_fun/pallas_call | solution.py:112
  86.5 0.9 collective-permute-done.9
  87.4 2.0 %branch_0_fun.3 = bf16[3,256,1024]{2,1,0:T(8,128)(2,1)} custom-call(s32[4]{0:T(128)S(1)} %get-tuple-element.26.where_ref, bf16[3,256,768]{2,1,0:T(8,128)(2,1)S(1)} %get-tuple-element.30.integrals_ref, bf16[2,768,512]{2,1,0:T(8,128)(2,1)S(1)} %bitcast.98, bf16[3,256,512]{2,1,0:T(8,128)(2,1)S(1)} %get-tuple-element.31.previous_ref, ...), custom_call_target="tpu_custom_call", output_to_operand_aliasing={{}: (4, {})} | custom-call | tf_op jit(solution)/shard_map/cond/branch_0_fun/pallas_call | solution.py:130
  (25 shorter events, 0.9 us)
Async XLA Ops:
  1.6 22.7 %all-to-all-start.1 = ((bf16[32,16,128]{2,1,0:T(8,128)(2,1)}), bf16[32,16,128]{2,1,0:T(8,128)(2,1)S(1)}, u32[]{:S(2)}, u32[]{:S(2)}) async-start(bf16[32,16,128]{2,1,0:T(8,128)(2,1)} %get-tuple-element.45), calls=%async_computation.1 | async-start | bytes 262144 | tf_op jit(solution)/shard_map/all_to_all | solution.py:180
  24.9 21.1 %collective-permute-start.1 = (bf16[2,32,512]{2,1,0:T(8,128)(2,1)S(1)}, bf16[2,32,512]{2,1,0:T(8,128)(2,1)S(1)}, u32[]{:S(2)}, u32[]{:S(2)}) collective-permute-start(bf16[2,32,512]{2,1,0:T(8,128)(2,1)S(1)} %reshape.34), channel_id=1, source_target_pairs={{0,2},{1,0},{2,1},{3,5},{4,3},{5,4},{6,8},{7,6},{8,7},{9,11},{10,9... | collective-permute-start | bytes 196616 | tf_op jit(solution)/shard_map/cond/branch_0_fun/ppermute | solution.py:21
  33.7 12.3 %collective-permute-start = (bf16[2,32,512]{2,1,0:T(8,128)(2,1)S(1)}, bf16[2,32,512]{2,1,0:T(8,128)(2,1)S(1)}, u32[]{:S(2)}, u32[]{:S(2)}) collective-permute-start(bf16[2,32,512]{2,1,0:T(8,128)(2,1)S(1)} %reshape.34), channel_id=1, source_target_pairs={{0,1},{1,2},{2,0},{3,4},{4,5},{5,3},{6,7},{7,8},{8,6},{9,10},{10,1... | collective-permute-start | bytes 196616 | tf_op jit(solution)/shard_map/cond/branch_0_fun/ppermute | solution.py:21
  46.0 8.8 %collective-permute-start.3 = (bf16[2,96,512]{2,1,0:T(8,128)(2,1)S(1)}, bf16[2,96,512]{2,1,0:T(8,128)(2,1)S(1)}, u32[]{:S(2)}, u32[]{:S(2)}) collective-permute-start(bf16[2,96,512]{2,1,0:T(8,128)(2,1)S(1)} %bitcast.104), channel_id=1, source_target_pairs={{0,21},{3,0},{6,3},{9,6},{12,9},{15,12},{18,15},{21,18},{1,22},{4,... | collective-permute-start | bytes 589832 | tf_op jit(solution)/shard_map/cond/branch_0_fun/ppermute | solution.py:21
  51.1 9.1 %collective-permute-start.2 = (bf16[2,96,512]{2,1,0:T(8,128)(2,1)S(1)}, bf16[2,96,512]{2,1,0:T(8,128)(2,1)S(1)}, u32[]{:S(2)}, u32[]{:S(2)}) collective-permute-start(bf16[2,96,512]{2,1,0:T(8,128)(2,1)S(1)} %bitcast.105), channel_id=1, source_target_pairs={{0,3},{3,6},{6,9},{9,12},{12,15},{15,18},{18,21},{21,0},{1,4},{4,7... | collective-permute-start | bytes 589832 | tf_op jit(solution)/shard_map/cond/branch_0_fun/ppermute | solution.py:21
  53.2 31.2 %copy-start = (bf16[3,256,1024]{2,1,0:T(8,128)(2,1)S(1)}, bf16[3,256,1024]{2,1,0:T(8,128)(2,1)}, u32[]{:S(2)}) copy-start(bf16[3,256,1024]{2,1,0:T(8,128)(2,1)} %get-tuple-element.29.previous_ref) | copy-start | bytes 4718596 | tf_op jit(solution)/shard_map/cond
  53.3 31.2 %copy-start.2 = (bf16[3,256,768]{2,1,0:T(8,128)(2,1)S(1)}, bf16[3,256,768]{2,1,0:T(8,128)(2,1)}, u32[]{:S(2)}) copy-start(bf16[3,256,768]{2,1,0:T(8,128)(2,1)} %get-tuple-element.27.integrals_ref) | copy-start | bytes 3538948 | tf_op jit(solution)/shard_map/cond
  54.8 8.1 %collective-permute-start.5 = (bf16[2,96,512]{2,1,0:T(8,128)(2,1)S(1)}, bf16[2,96,512]{2,1,0:T(8,128)(2,1)S(1)}, u32[]{:S(2)}, u32[]{:S(2)}) collective-permute-start(bf16[2,96,512]{2,1,0:T(8,128)(2,1)S(1)} %collective-permute-done.3), channel_id=1, source_target_pairs={{0,21},{3,0},{6,3},{9,6},{12,9},{15,12},{18,15},{21,18},{1,22},{4,... | collective-permute-start | bytes 589832 | tf_op jit(solution)/shard_map/cond/branch_0_fun/ppermute | solution.py:21
  60.2 10.1 %collective-permute-start.4 = (bf16[2,96,512]{2,1,0:T(8,128)(2,1)S(1)}, bf16[2,96,512]{2,1,0:T(8,128)(2,1)S(1)}, u32[]{:S(2)}, u32[]{:S(2)}) collective-permute-start(bf16[2,96,512]{2,1,0:T(8,128)(2,1)S(1)} %collective-permute-done.2), channel_id=1, source_target_pairs={{0,3},{3,6},{6,9},{9,12},{12,15},{15,18},{18,21},{21,0},{1,4},{4,7... | collective-permute-start | bytes 589832 | tf_op jit(solution)/shard_map/cond/branch_0_fun/ppermute | solution.py:21
  63.0 18.4 %collective-permute-start.8 = (bf16[2,96,512]{2,1,0:T(8,128)(2,1)S(1)}, bf16[2,96,512]{2,1,0:T(8,128)(2,1)S(1)}, u32[]{:S(2)}, u32[]{:S(2)}) collective-permute-start(bf16[2,96,512]{2,1,0:T(8,128)(2,1)S(1)} %collective-permute-done.5), channel_id=1, source_target_pairs={{0,18},{3,21},{6,0},{9,3},{12,6},{15,9},{18,12},{21,15},{1,19},{4,... | collective-permute-start | bytes 589832 | tf_op jit(solution)/shard_map/cond/branch_0_fun/ppermute | solution.py:21
  67.0 14.4 %collective-permute-start.7 = (bf16[2,96,512]{2,1,0:T(8,128)(2,1)S(1)}, bf16[2,96,512]{2,1,0:T(8,128)(2,1)S(1)}, u32[]{:S(2)}, u32[]{:S(2)}) collective-permute-start(bf16[2,96,512]{2,1,0:T(8,128)(2,1)S(1)} %collective-permute-done.5), channel_id=1, source_target_pairs={{0,21},{3,0},{6,3},{9,6},{12,9},{15,12},{18,15},{21,18},{1,22},{4,... | collective-permute-start | bytes 589832 | tf_op jit(solution)/shard_map/cond/branch_0_fun/ppermute | solution.py:21
  70.2 7.6 %collective-permute-start.6 = (bf16[2,96,512]{2,1,0:T(8,128)(2,1)S(1)}, bf16[2,96,512]{2,1,0:T(8,128)(2,1)S(1)}, u32[]{:S(2)}, u32[]{:S(2)}) collective-permute-start(bf16[2,96,512]{2,1,0:T(8,128)(2,1)S(1)} %collective-permute-done.4), channel_id=1, source_target_pairs={{0,3},{3,6},{6,9},{9,12},{12,15},{15,18},{18,21},{21,0},{1,4},{4,7... | collective-permute-start | bytes 589832 | tf_op jit(solution)/shard_map/cond/branch_0_fun/ppermute | solution.py:21
  81.4 6.0 %collective-permute-start.9 = (bf16[2,8,96,512]{3,2,1,0:T(8,128)(2,1)S(1)}, bf16[2,8,96,512]{3,2,1,0:T(8,128)(2,1)S(1)}, u32[]{:S(2)}, u32[]{:S(2)}) collective-permute-start(bf16[2,8,96,512]{3,2,1,0:T(8,128)(2,1)S(1)} %bitcast_dynamic-update-slice_fusion.6), channel_id=1, source_target_pairs={{0,24},{24,0},{1,25},{25,1},{2,26},{26,2},{3,27},{27,3},{4,28},{28... | collective-permute-start | bytes 4718600 | tf_op jit(solution)/shard_map/cond/branch_0_fun/ppermute | solution.py:21

commit v6 on v5

--- a/solution.py
+++ b/solution.py
@@ -145,16 +145,20 @@
 def with_slots(slots, incoming, where, integrals, residual_in, depth, width):
     half = lax.axis_size("chip")
     core = lax.axis_index("core")
-    mine = lax.dynamic_slice_in_dim(incoming, core * half, half, 0)
     parts = incoming.shape[2] // width
-    mine = mine.reshape(half, slots, depth // parts, parts, width).transpose(1, 3, 2, 0, 4)
-    mine = mine.reshape(slots, depth, half * width)
+    every = incoming.reshape(2, half, slots, depth // parts, parts, width).transpose(0, 2, 4, 3, 1, 5)
+    every = every.reshape(2, slots, depth, half * width)
+    mine = lax.dynamic_index_in_dim(every, core, 0, keepdims=False)
     z_size, z = lax.axis_size("bulk_1"), lax.axis_index("bulk_1")
+    ways = [(c, i, (i + 1 - 2 * c) % z_size) for c in range(2) for i in range(z_size)]
+    same = [(c * z_size + i, c * z_size + to) for c, i, to in ways]
+    across = [(c * z_size + i, (1 - c) * z_size + to) for c, i, to in ways]
+    near = lax.ppermute(mine, ("core", "bulk_1"), same)
+    theirs = lax.dynamic_index_in_dim(every, 1 - core, 0, keepdims=False)
+    opposite = lax.ppermute(theirs, ("core", "bulk_1"), across)
     group = jnp.zeros((slots, z_size, depth, half * width), mine.dtype)
-    group = lax.dynamic_update_slice_in_dim(group, mine[:, None], z, 1)
-    for step in range(1, z_size):
-        got = shift(mine, "bulk_1", step)
-        group = lax.dynamic_update_slice_in_dim(group, got[:, None], lax.rem(z - step + z_size, z_size), 1)
+    way = 1 - 2 * core
+    group = put(put(put(group, mine, z), near, z - way), opposite, z + way)
     group = group.reshape(slots, z_size * depth, half * width)
     y_size, y = lax.axis_size("bulk_0"), lax.axis_index("bulk_0")
     whole = jnp.zeros((slots, y_size, z_size * depth, half * width), mine.dtype)

time: 90 us -> 89.6 us (level)
  waiting for transfers between devices: 28.7 us -> 26.4 us
  starting transfers between devices: 52.3 us -> 53.9 us
    ppermute x0 -> x2, starting transfers between devices: none -> 12.5 us  [the longest x1 9.09 us: with_slots(): opposite = lax.ppermute(theirs, ('core', 'bulk_1'), across)]
    ppermute x10 -> x8, starting transfers between devices: 38.3 us -> 27.4 us  [shift(): lax.ppermute(value, axis, [(i, (i + step) % size) for i in range(size)])]
    ppermute x10 -> x8, waiting for transfers between devices: 21.2 us -> 12.8 us  [shift(): lax.ppermute(value, axis, [(i, (i + step) % size) for i in range(size)])]
    ppermute x0 -> x2, waiting for transfers between devices: none -> 6.26 us  [the longest x1 6.26 us: with_slots(): near = lax.ppermute(mine, ('core', 'bulk_1'), same)]
where the time goes in v6:
time: 89.6 us; the launch traced here: 89.1 us
  starting transfers between devices  53.9 us (60%)
  waiting for transfers between devices  26.4 us (29%)
  Pallas kernels  5.72 us (6%)
  local copies, waits for them, and re-layouts  2.06 us (2%)
    ppermute x8, starting transfers between devices, shift(): lax.ppermute(value, axis, [(i, (i + step) % size) for i in range(size)])  27.4 us
    all_to_all x1, starting transfers between devices, spread(): lax.all_to_all(outgoing, CHIP_CORE, split_axis=0, concat_axis=0, tiled=True)  14 us
    ppermute x8, waiting for transfers between devices, shift(): lax.ppermute(value, axis, [(i, (i + step) % size) for i in range(size)])  12.8 us
    ppermute x1, starting transfers between devices, with_slots(): opposite = lax.ppermute(theirs, ('core', 'bulk_1'), across)  9.09 us
    all_to_all x1, waiting for transfers between devices, spread(): lax.all_to_all(outgoing, CHIP_CORE, split_axis=0, concat_axis=0, tiled=True)  7.33 us
    ppermute x1, waiting for transfers between devices, with_slots(): near = lax.ppermute(mine, ('core', 'bulk_1'), same)  6.26 us
    ppermute x1, starting transfers between devices, with_slots(): near = lax.ppermute(mine, ('core', 'bulk_1'), same)  3.36 us
    pallas_call x1, Pallas kernels, own_half(): pl.pallas_call(own_kernel, in_specs=[SMEM, VMEM, VMEM, VMEM], out_specs=(...  2.09 us
  transfers between devices with their start and end apart: 11, of which 7 were waited for; matrix products, arithmetic and copies ran while one was open for 1% of the time, Pallas kernels for 2%

profile of v6, /device:TPU:1, one launch (start us, length us, event | category | flops | bytes accessed | tf_op | source)
XLA Modules:
  0.0 89.1 jit_solution(13565787200030359259)
XLA Ops:
  0.0 1.6 %shard_map.48 = (bf16[32,16,128]{2,1,0:T(8,128)(2,1)}, s32[4]{0:T(128)S(1)}) custom-call(s32[2304]{0:T(1024)} %labels_ref.1, bf16[4,32,32]{2,1,0:T(8,128)(2,1)} %amplitudes_ref.1), custom_call_target="tpu_custom_call" | custom-call | tf_op jit(solution)/shard_map/pallas_call | solution.py:56
  1.6 14.0 %all-to-all-start.1 = ((bf16[32,16,128]{2,1,0:T(8,128)(2,1)}), bf16[32,16,128]{2,1,0:T(8,128)(2,1)S(1)}, u32[]{:S(2)}, u32[]{:S(2)}) async-start(bf16[32,16,128]{2,1,0:T(8,128)(2,1)} %get-tuple-element.45), calls=%async_computation.1 | async-start | bytes 262144 | tf_op jit(solution)/shard_map/all_to_all | solution.py:184
  15.6 0.6 slice.3
  17.0 7.3 %all-to-all-done.1 = bf16[32,16,128]{2,1,0:T(8,128)(2,1)S(1)} async-done(((bf16[32,16,128]{2,1,0:T(8,128)(2,1)}), bf16[32,16,128]{2,1,0:T(8,128)(2,1)S(1)}, u32[]{:S(2)}, u32[]{:S(2)}) %all-to-all-start.1) | async-done | bytes 131104 | tf_op jit(solution)/shard_map/all_to_all | solution.py:184
  24.3 64.8 %conditional.1 = (bf16[3,256,1024]{2,1,0:T(8,128)(2,1)}) conditional(s32[]{:T(128)} %bitcast.58, (bf16[32,16,128]{2,1,0:T(8,128)(2,1)S(1)}, s32[4]{0:T(128)S(1)}, bf16[3,256,768]{2,1,0:T(8,128)(2,1)}, bf16[3,256,1024]{2,1,0:T(8,128)(2,1)}) %tuple.11, (s32[2304]{0:T(1024)}, bf16[4,32,32]{2,1,0:T(8,128)(2,1)}, s32[4]{0:T(128)S(1)}, ...), branch_computations={%region_0.1_spmd, %region_1.2_spmd} | conditional | flops 603979904 | bytes 43618308 | solution.py:196
  24.9 0.4 reshape.31
  25.4 9.1 %collective-permute-start.1 = (bf16[2,32,512]{2,1,0:T(8,128)(2,1)S(1)}, bf16[2,32,512]{2,1,0:T(8,128)(2,1)S(1)}, u32[]{:S(2)}, u32[]{:S(2)}) collective-permute-start(bf16[2,32,512]{2,1,0:T(8,128)(2,1)S(1)} %get-tuple-element.47), channel_id=1, source_target_pairs={{0,25},{1,26},{2,24},{24,2},{25,0},{26,1},{3,28},{4,29},{5,27},{27... | collective-permute-start | bytes 196616 | tf_op jit(solution)/shard_map/cond/branch_0_fun/ppermute | solution.py:158
  34.5 3.4 %collective-permute-start = (bf16[2,32,512]{2,1,0:T(8,128)(2,1)S(1)}, bf16[2,32,512]{2,1,0:T(8,128)(2,1)S(1)}, u32[]{:S(2)}, u32[]{:S(2)}) collective-permute-start(bf16[2,32,512]{2,1,0:T(8,128)(2,1)S(1)} %get-tuple-element.48), channel_id=1, source_target_pairs={{0,1},{1,2},{2,0},{24,26},{25,24},{26,25},{3,4},{4,5},{5,3},{27,29... | collective-permute-start | bytes 196616 | tf_op jit(solution)/shard_map/cond/branch_0_fun/ppermute | solution.py:156
  37.9 6.3 %collective-permute-done = bf16[2,32,512]{2,1,0:T(8,128)(2,1)S(1)} collective-permute-done((bf16[2,32,512]{2,1,0:T(8,128)(2,1)S(1)}, bf16[2,32,512]{2,1,0:T(8,128)(2,1)S(1)}, u32[]{:S(2)}, u32[]{:S(2)}) %collective-permute-start) | collective-permute-done | bytes 65568 | tf_op jit(solution)/shard_map/cond/branch_0_fun/ppermute | solution.py:156
  44.2 5.1 %collective-permute-start.3 = (bf16[2,96,512]{2,1,0:T(8,128)(2,1)S(1)}, bf16[2,96,512]{2,1,0:T(8,128)(2,1)S(1)}, u32[]{:S(2)}, u32[]{:S(2)}) collective-permute-start(bf16[2,96,512]{2,1,0:T(8,128)(2,1)S(1)} %bitcast.104), channel_id=1, source_target_pairs={{0,21},{3,0},{6,3},{9,6},{12,9},{15,12},{18,15},{21,18},{1,22},{4,... | collective-permute-start | bytes 589832 | tf_op jit(solution)/shard_map/cond/branch_0_fun/ppermute | solution.py:21
  49.3 1.9 %collective-permute-start.2 = (bf16[2,96,512]{2,1,0:T(8,128)(2,1)S(1)}, bf16[2,96,512]{2,1,0:T(8,128)(2,1)S(1)}, u32[]{:S(2)}, u32[]{:S(2)}) collective-permute-start(bf16[2,96,512]{2,1,0:T(8,128)(2,1)S(1)} %bitcast.105), channel_id=1, source_target_pairs={{0,3},{3,6},{6,9},{9,12},{12,15},{15,18},{18,21},{21,0},{1,4},{4,7... | collective-permute-start | bytes 589832 | tf_op jit(solution)/shard_map/cond/branch_0_fun/ppermute | solution.py:21
  51.5 2.2 %collective-permute-done.3 = bf16[2,96,512]{2,1,0:T(8,128)(2,1)S(1)} collective-permute-done((bf16[2,96,512]{2,1,0:T(8,128)(2,1)S(1)}, bf16[2,96,512]{2,1,0:T(8,128)(2,1)S(1)}, u32[]{:S(2)}, u32[]{:S(2)}) %collective-permute-start.3) | collective-permute-done | bytes 196640 | tf_op jit(solution)/shard_map/cond/branch_0_fun/ppermute | solution.py:21
  53.7 5.3 %collective-permute-start.5 = (bf16[2,96,512]{2,1,0:T(8,128)(2,1)S(1)}, bf16[2,96,512]{2,1,0:T(8,128)(2,1)S(1)}, u32[]{:S(2)}, u32[]{:S(2)}) collective-permute-start(bf16[2,96,512]{2,1,0:T(8,128)(2,1)S(1)} %collective-permute-done.3), channel_id=1, source_target_pairs={{0,21},{3,0},{6,3},{9,6},{12,9},{15,12},{18,15},{21,18},{1,22},{4,... | collective-permute-start | bytes 589832 | tf_op jit(solution)/shard_map/cond/branch_0_fun/ppermute | solution.py:21
  59.1 1.9 %collective-permute-start.4 = (bf16[2,96,512]{2,1,0:T(8,128)(2,1)S(1)}, bf16[2,96,512]{2,1,0:T(8,128)(2,1)S(1)}, u32[]{:S(2)}, u32[]{:S(2)}) collective-permute-start(bf16[2,96,512]{2,1,0:T(8,128)(2,1)S(1)} %collective-permute-done.2), channel_id=1, source_target_pairs={{0,3},{3,6},{6,9},{9,12},{12,15},{15,18},{18,21},{21,0},{1,4},{4,7... | collective-permute-start | bytes 589832 | tf_op jit(solution)/shard_map/cond/branch_0_fun/ppermute | solution.py:21
  61.1 1.5 %collective-permute-done.5 = bf16[2,96,512]{2,1,0:T(8,128)(2,1)S(1)} collective-permute-done((bf16[2,96,512]{2,1,0:T(8,128)(2,1)S(1)}, bf16[2,96,512]{2,1,0:T(8,128)(2,1)S(1)}, u32[]{:S(2)}, u32[]{:S(2)}) %collective-permute-start.5) | collective-permute-done | bytes 196640 | tf_op jit(solution)/shard_map/cond/branch_0_fun/ppermute | solution.py:21
  62.6 4.0 %collective-permute-start.8 = (bf16[2,96,512]{2,1,0:T(8,128)(2,1)S(1)}, bf16[2,96,512]{2,1,0:T(8,128)(2,1)S(1)}, u32[]{:S(2)}, u32[]{:S(2)}) collective-permute-start(bf16[2,96,512]{2,1,0:T(8,128)(2,1)S(1)} %collective-permute-done.5), channel_id=1, source_target_pairs={{0,18},{3,21},{6,0},{9,3},{12,6},{15,9},{18,12},{21,15},{1,19},{4,... | collective-permute-start | bytes 589832 | tf_op jit(solution)/shard_map/cond/branch_0_fun/ppermute | solution.py:21
  66.6 3.2 %collective-permute-start.7 = (bf16[2,96,512]{2,1,0:T(8,128)(2,1)S(1)}, bf16[2,96,512]{2,1,0:T(8,128)(2,1)S(1)}, u32[]{:S(2)}, u32[]{:S(2)}) collective-permute-start(bf16[2,96,512]{2,1,0:T(8,128)(2,1)S(1)} %collective-permute-done.5), channel_id=1, source_target_pairs={{0,21},{3,0},{6,3},{9,6},{12,9},{15,12},{18,15},{21,18},{1,22},{4,... | collective-permute-start | bytes 589832 | tf_op jit(solution)/shard_map/cond/branch_0_fun/ppermute | solution.py:21
  69.8 3.1 %collective-permute-start.6 = (bf16[2,96,512]{2,1,0:T(8,128)(2,1)S(1)}, bf16[2,96,512]{2,1,0:T(8,128)(2,1)S(1)}, u32[]{:S(2)}, u32[]{:S(2)}) collective-permute-start(bf16[2,96,512]{2,1,0:T(8,128)(2,1)S(1)} %collective-permute-done.4), channel_id=1, source_target_pairs={{0,3},{3,6},{6,9},{9,12},{12,15},{15,18},{18,21},{21,0},{1,4},{4,7... | collective-permute-start | bytes 589832 | tf_op jit(solution)/shard_map/cond/branch_0_fun/ppermute | solution.py:21
  73.0 4.5 %collective-permute-done.6 = bf16[2,96,512]{2,1,0:T(8,128)(2,1)S(1)} collective-permute-done((bf16[2,96,512]{2,1,0:T(8,128)(2,1)S(1)}, bf16[2,96,512]{2,1,0:T(8,128)(2,1)S(1)}, u32[]{:S(2)}, u32[]{:S(2)}) %collective-permute-start.6) | collective-permute-done | bytes 196640 | tf_op jit(solution)/shard_map/cond/branch_0_fun/ppermute | solution.py:21
  77.5 3.7 %collective-permute-done.7 = bf16[2,96,512]{2,1,0:T(8,128)(2,1)S(1)} collective-permute-done((bf16[2,96,512]{2,1,0:T(8,128)(2,1)S(1)}, bf16[2,96,512]{2,1,0:T(8,128)(2,1)S(1)}, u32[]{:S(2)}, u32[]{:S(2)}) %collective-permute-start.7) | collective-permute-done | bytes 196640 | tf_op jit(solution)/shard_map/cond/branch_0_fun/ppermute | solution.py:21
  81.2 2.8 %collective-permute-start.9 = (bf16[2,8,96,512]{3,2,1,0:T(8,128)(2,1)S(1)}, bf16[2,8,96,512]{3,2,1,0:T(8,128)(2,1)S(1)}, u32[]{:S(2)}, u32[]{:S(2)}) collective-permute-start(bf16[2,8,96,512]{3,2,1,0:T(8,128)(2,1)S(1)} %bitcast_dynamic-update-slice_fusion.6), channel_id=1, source_target_pairs={{0,24},{24,0},{1,25},{25,1},{2,26},{26,2},{3,27},{27,3},{4,28},{28... | collective-permute-start | bytes 4718600 | tf_op jit(solution)/shard_map/cond/branch_0_fun/ppermute | solution.py:21
  84.0 2.1 %branch_0_fun.2 = (bf16[3,256,1024]{2,1,0:T(8,128)(2,1)}, bf16[3,256,768]{2,1,0:T(8,128)(2,1)S(1)}, bf16[3,256,512]{2,1,0:T(8,128)(2,1)S(1)}) custom-call(s32[4]{0:T(128)S(1)} %get-tuple-element.26.where_ref, bf16[3,256,768]{2,1,0:T(8,128)(2,1)S(1)} %copy-done.2, bf16[2,768,512]{2,1,0:T(8,128)(2,1)S(1)} %bitcast.96, bf16[3,256,1024]{2,1,0:T(8,128)(2,1)S(1)} %copy-done), custom_call_target="tpu_custom_call" | custom-call | flops 603979776 | bytes 4000000 | tf_op jit(solution)/shard_map/cond/branch_0_fun/pallas_call | solution.py:112
  86.1 0.9 %collective-permute-done.9 = bf16[2,8,96,512]{3,2,1,0:T(8,128)(2,1)S(1)} collective-permute-done((bf16[2,8,96,512]{3,2,1,0:T(8,128)(2,1)S(1)}, bf16[2,8,96,512]{3,2,1,0:T(8,128)(2,1)S(1)}, u32[]{:S(2)}, u32[]{:S(2)}) %collective-permute-start.9) | collective-permute-done | bytes 1572896 | tf_op jit(solution)/shard_map/cond/branch_0_fun/ppermute | solution.py:21
  87.0 2.0 %branch_0_fun.3 = bf16[3,256,1024]{2,1,0:T(8,128)(2,1)} custom-call(s32[4]{0:T(128)S(1)} %get-tuple-element.26.where_ref, bf16[3,256,768]{2,1,0:T(8,128)(2,1)S(1)} %get-tuple-element.30.integrals_ref, bf16[2,768,512]{2,1,0:T(8,128)(2,1)S(1)} %bitcast.98, bf16[3,256,512]{2,1,0:T(8,128)(2,1)S(1)} %get-tuple-element.31.previous_ref, ...), custom_call_target="tpu_custom_call", output_to_operand_aliasing={{}: (4, {})} | custom-call | tf_op jit(solution)/shard_map/cond/branch_0_fun/pallas_call | solution.py:130
  (24 shorter events, 1.0 us)
Async XLA Ops:
  1.6 22.7 %all-to-all-start.1 = ((bf16[32,16,128]{2,1,0:T(8,128)(2,1)}), bf16[32,16,128]{2,1,0:T(8,128)(2,1)S(1)}, u32[]{:S(2)}, u32[]{:S(2)}) async-start(bf16[32,16,128]{2,1,0:T(8,128)(2,1)} %get-tuple-element.45), calls=%async_computation.1 | async-start | bytes 262144 | tf_op jit(solution)/shard_map/all_to_all | solution.py:184
  25.4 18.8 %collective-permute-start.1 = (bf16[2,32,512]{2,1,0:T(8,128)(2,1)S(1)}, bf16[2,32,512]{2,1,0:T(8,128)(2,1)S(1)}, u32[]{:S(2)}, u32[]{:S(2)}) collective-permute-start(bf16[2,32,512]{2,1,0:T(8,128)(2,1)S(1)} %get-tuple-element.47), channel_id=1, source_target_pairs={{0,25},{1,26},{2,24},{24,2},{25,0},{26,1},{3,28},{4,29},{5,27},{27... | collective-permute-start | bytes 196616 | tf_op jit(solution)/shard_map/cond/branch_0_fun/ppermute | solution.py:158
  34.5 9.7 %collective-permute-start = (bf16[2,32,512]{2,1,0:T(8,128)(2,1)S(1)}, bf16[2,32,512]{2,1,0:T(8,128)(2,1)S(1)}, u32[]{:S(2)}, u32[]{:S(2)}) collective-permute-start(bf16[2,32,512]{2,1,0:T(8,128)(2,1)S(1)} %get-tuple-element.48), channel_id=1, source_target_pairs={{0,1},{1,2},{2,0},{24,26},{25,24},{26,25},{3,4},{4,5},{5,3},{27,29... | collective-permute-start | bytes 196616 | tf_op jit(solution)/shard_map/cond/branch_0_fun/ppermute | solution.py:156
  44.2 9.5 %collective-permute-start.3 = (bf16[2,96,512]{2,1,0:T(8,128)(2,1)S(1)}, bf16[2,96,512]{2,1,0:T(8,128)(2,1)S(1)}, u32[]{:S(2)}, u32[]{:S(2)}) collective-permute-start(bf16[2,96,512]{2,1,0:T(8,128)(2,1)S(1)} %bitcast.104), channel_id=1, source_target_pairs={{0,21},{3,0},{6,3},{9,6},{12,9},{15,12},{18,15},{21,18},{1,22},{4,... | collective-permute-start | bytes 589832 | tf_op jit(solution)/shard_map/cond/branch_0_fun/ppermute | solution.py:21
  49.3 9.7 %collective-permute-start.2 = (bf16[2,96,512]{2,1,0:T(8,128)(2,1)S(1)}, bf16[2,96,512]{2,1,0:T(8,128)(2,1)S(1)}, u32[]{:S(2)}, u32[]{:S(2)}) collective-permute-start(bf16[2,96,512]{2,1,0:T(8,128)(2,1)S(1)} %bitcast.105), channel_id=1, source_target_pairs={{0,3},{3,6},{6,9},{9,12},{12,15},{15,18},{18,21},{21,0},{1,4},{4,7... | collective-permute-start | bytes 589832 | tf_op jit(solution)/shard_map/cond/branch_0_fun/ppermute | solution.py:21
  51.5 32.6 %copy-start = (bf16[3,256,1024]{2,1,0:T(8,128)(2,1)S(1)}, bf16[3,256,1024]{2,1,0:T(8,128)(2,1)}, u32[]{:S(2)}) copy-start(bf16[3,256,1024]{2,1,0:T(8,128)(2,1)} %get-tuple-element.29.previous_ref) | copy-start | bytes 4718596 | tf_op jit(solution)/shard_map/cond
  51.5 32.5 %copy-start.2 = (bf16[3,256,768]{2,1,0:T(8,128)(2,1)S(1)}, bf16[3,256,768]{2,1,0:T(8,128)(2,1)}, u32[]{:S(2)}) copy-start(bf16[3,256,768]{2,1,0:T(8,128)(2,1)} %get-tuple-element.27.integrals_ref) | copy-start | bytes 3538948 | tf_op jit(solution)/shard_map/cond
  53.7 8.8 %collective-permute-start.5 = (bf16[2,96,512]{2,1,0:T(8,128)(2,1)S(1)}, bf16[2,96,512]{2,1,0:T(8,128)(2,1)S(1)}, u32[]{:S(2)}, u32[]{:S(2)}) collective-permute-start(bf16[2,96,512]{2,1,0:T(8,128)(2,1)S(1)} %collective-permute-done.3), channel_id=1, source_target_pairs={{0,21},{3,0},{6,3},{9,6},{12,9},{15,12},{18,15},{21,18},{1,22},{4,... | collective-permute-start | bytes 589832 | tf_op jit(solution)/shard_map/cond/branch_0_fun/ppermute | solution.py:21
  59.1 10.8 %collective-permute-start.4 = (bf16[2,96,512]{2,1,0:T(8,128)(2,1)S(1)}, bf16[2,96,512]{2,1,0:T(8,128)(2,1)S(1)}, u32[]{:S(2)}, u32[]{:S(2)}) collective-permute-start(bf16[2,96,512]{2,1,0:T(8,128)(2,1)S(1)} %collective-permute-done.2), channel_id=1, source_target_pairs={{0,3},{3,6},{6,9},{9,12},{12,15},{15,18},{18,21},{21,0},{1,4},{4,7... | collective-permute-start | bytes 589832 | tf_op jit(solution)/shard_map/cond/branch_0_fun/ppermute | solution.py:21
  62.6 18.6 %collective-permute-start.8 = (bf16[2,96,512]{2,1,0:T(8,128)(2,1)S(1)}, bf16[2,96,512]{2,1,0:T(8,128)(2,1)S(1)}, u32[]{:S(2)}, u32[]{:S(2)}) collective-permute-start(bf16[2,96,512]{2,1,0:T(8,128)(2,1)S(1)} %collective-permute-done.5), channel_id=1, source_target_pairs={{0,18},{3,21},{6,0},{9,3},{12,6},{15,9},{18,12},{21,15},{1,19},{4,... | collective-permute-start | bytes 589832 | tf_op jit(solution)/shard_map/cond/branch_0_fun/ppermute | solution.py:21
  66.6 14.6 %collective-permute-start.7 = (bf16[2,96,512]{2,1,0:T(8,128)(2,1)S(1)}, bf16[2,96,512]{2,1,0:T(8,128)(2,1)S(1)}, u32[]{:S(2)}, u32[]{:S(2)}) collective-permute-start(bf16[2,96,512]{2,1,0:T(8,128)(2,1)S(1)} %collective-permute-done.5), channel_id=1, source_target_pairs={{0,21},{3,0},{6,3},{9,6},{12,9},{15,12},{18,15},{21,18},{1,22},{4,... | collective-permute-start | bytes 589832 | tf_op jit(solution)/shard_map/cond/branch_0_fun/ppermute | solution.py:21
  69.8 7.6 %collective-permute-start.6 = (bf16[2,96,512]{2,1,0:T(8,128)(2,1)S(1)}, bf16[2,96,512]{2,1,0:T(8,128)(2,1)S(1)}, u32[]{:S(2)}, u32[]{:S(2)}) collective-permute-start(bf16[2,96,512]{2,1,0:T(8,128)(2,1)S(1)} %collective-permute-done.4), channel_id=1, source_target_pairs={{0,3},{3,6},{6,9},{9,12},{12,15},{15,18},{18,21},{21,0},{1,4},{4,7... | collective-permute-start | bytes 589832 | tf_op jit(solution)/shard_map/cond/branch_0_fun/ppermute | solution.py:21
  81.2 5.8 %collective-permute-start.9 = (bf16[2,8,96,512]{3,2,1,0:T(8,128)(2,1)S(1)}, bf16[2,8,96,512]{3,2,1,0:T(8,128)(2,1)S(1)}, u32[]{:S(2)}, u32[]{:S(2)}) collective-permute-start(bf16[2,8,96,512]{3,2,1,0:T(8,128)(2,1)S(1)} %bitcast_dynamic-update-slice_fusion.6), channel_id=1, source_target_pairs={{0,24},{24,0},{1,25},{25,1},{2,26},{26,2},{3,27},{27,3},{4,28},{28... | collective-permute-start | bytes 4718600 | tf_op jit(solution)/shard_map/cond/branch_0_fun/ppermute | solution.py:21

commit v7 on v6

--- a/solution.py
+++ b/solution.py
@@ -138,6 +138,12 @@
     )(where, integrals, block, previous, so_far)
 
 
+def turn(value, step):
+    size = lax.axis_size("bulk_0")
+    pairs = [(c * size + i, c * size + (i + (1 - 2 * c) * step) % size) for c in range(2) for i in range(size)]
+    return lax.ppermute(value, ("core", "bulk_0"), pairs)
+
+
 def put(whole, block, at):
     return lax.dynamic_update_slice_in_dim(whole, block[:, None], lax.rem(at + whole.shape[1], whole.shape[1]), 1)
 
@@ -163,13 +169,13 @@
     y_size, y = lax.axis_size("bulk_0"), lax.axis_index("bulk_0")
     whole = jnp.zeros((slots, y_size, z_size * depth, half * width), mine.dtype)
     whole = put(whole, group, y)
-    up, down = group, group
+    first, second = group, group
     for step in range(1, y_size // 2 - 1):
-        up, down = shift(up, "bulk_0", 1), shift(down, "bulk_0", -1)
-        whole = put(put(whole, up, y - step), down, y + step)
+        first, second = turn(first, -1), turn(second, 1)
+        whole = put(put(whole, second, y - way * step), first, y + way * step)
     last = y_size // 2 - 1
-    far, up, down = shift(down, "bulk_0", -2), shift(up, "bulk_0", 1), shift(down, "bulk_0", -1)
-    whole = put(put(put(whole, up, y - last), down, y + last), far, y + last + 1)
+    far, second, first = turn(first, -2), turn(second, 1), turn(first, -1)
+    whole = put(put(put(whole, second, y - way * last), first, y + way * last), far, y + last + 1)
     other = shift(whole, "core", 1)
     flat = (slots, y_size * z_size * depth, half * width)
     out, integrals, previous = own_half(where, integrals, whole.reshape(flat), residual_in)

time: 89.6 us -> 88.1 us (0.983)
  waiting for transfers between devices: 26.4 us -> 24.1 us
    ppermute x0 -> x7, starting transfers between devices: none -> 22.6 us  [turn(): return lax.ppermute(value, ('core', 'bulk_0'), pairs)]
    ppermute x8 -> x1, starting transfers between devices: 27.4 us -> 5.46 us  [shift(): lax.ppermute(value, axis, [(i, (i + step) % size) for i in range(size)])]
    ppermute x8 -> x1, waiting for transfers between devices: 12.8 us -> 0.89 us  [shift(): lax.ppermute(value, axis, [(i, (i + step) % size) for i in range(size)])]
    ppermute x0 -> x7, waiting for transfers between devices: none -> 9.65 us  [turn(): return lax.ppermute(value, ('core', 'bulk_0'), pairs)]
where the time goes in v7:
time: 88.1 us; the launch traced here: 87.6 us
  starting transfers between devices  54.6 us (62%)
  waiting for transfers between devices  24.1 us (27%)
  Pallas kernels  5.72 us (6%)
  local copies, waits for them, and re-layouts  2.06 us (2%)
    ppermute x7, starting transfers between devices, turn(): return lax.ppermute(value, ('core', 'bulk_0'), pairs)  22.6 us
    all_to_all x1, starting transfers between devices, spread(): lax.all_to_all(outgoing, CHIP_CORE, split_axis=0, concat_axis=0, tiled=True)  14 us
    ppermute x7, waiting for transfers between devices, turn(): return lax.ppermute(value, ('core', 'bulk_0'), pairs)  9.65 us
    ppermute x1, starting transfers between devices, with_slots(): opposite = lax.ppermute(theirs, ('core', 'bulk_1'), across)  9.09 us
    all_to_all x1, waiting for transfers between devices, spread(): lax.all_to_all(outgoing, CHIP_CORE, split_axis=0, concat_axis=0, tiled=True)  7.33 us
    ppermute x1, waiting for transfers between devices, with_slots(): near = lax.ppermute(mine, ('core', 'bulk_1'), same)  6.26 us
    ppermute x1, starting transfers between devices, shift(): lax.ppermute(value, axis, [(i, (i + step) % size) for i in range(size)])  5.46 us
    ppermute x1, starting transfers between devices, with_slots(): near = lax.ppermute(mine, ('core', 'bulk_1'), same)  3.36 us
  transfers between devices with their start and end apart: 11, of which 7 were waited for; matrix products, arithmetic and copies ran while one was open for 1% of the time, Pallas kernels for 2%

profile of v7, /device:TPU:1, one launch (start us, length us, event | category | flops | bytes accessed | tf_op | source)
XLA Modules:
  0.0 87.6 jit_solution(4568507319430233459)
XLA Ops:
  0.0 1.6 %shard_map.48 = (bf16[32,16,128]{2,1,0:T(8,128)(2,1)}, s32[4]{0:T(128)S(1)}) custom-call(s32[2304]{0:T(1024)} %labels_ref.1, bf16[4,32,32]{2,1,0:T(8,128)(2,1)} %amplitudes_ref.1), custom_call_target="tpu_custom_call" | custom-call | tf_op jit(solution)/shard_map/pallas_call | solution.py:56
  1.6 14.0 %all-to-all-start.1 = ((bf16[32,16,128]{2,1,0:T(8,128)(2,1)}), bf16[32,16,128]{2,1,0:T(8,128)(2,1)S(1)}, u32[]{:S(2)}, u32[]{:S(2)}) async-start(bf16[32,16,128]{2,1,0:T(8,128)(2,1)} %get-tuple-element.45), calls=%async_computation.1 | async-start | bytes 262144 | tf_op jit(solution)/shard_map/all_to_all | solution.py:190
  15.6 0.6 slice.3
  17.0 7.3 %all-to-all-done.1 = bf16[32,16,128]{2,1,0:T(8,128)(2,1)S(1)} async-done(((bf16[32,16,128]{2,1,0:T(8,128)(2,1)}), bf16[32,16,128]{2,1,0:T(8,128)(2,1)S(1)}, u32[]{:S(2)}, u32[]{:S(2)}) %all-to-all-start.1) | async-done | bytes 131104 | tf_op jit(solution)/shard_map/all_to_all | solution.py:190
  24.3 63.3 %conditional.1 = (bf16[3,256,1024]{2,1,0:T(8,128)(2,1)}) conditional(s32[]{:T(128)} %bitcast.58, (bf16[32,16,128]{2,1,0:T(8,128)(2,1)S(1)}, s32[4]{0:T(128)S(1)}, bf16[3,256,768]{2,1,0:T(8,128)(2,1)}, bf16[3,256,1024]{2,1,0:T(8,128)(2,1)}) %tuple.11, (s32[2304]{0:T(1024)}, bf16[4,32,32]{2,1,0:T(8,128)(2,1)}, s32[4]{0:T(128)S(1)}, ...), branch_computations={%region_0.1_spmd, %region_1.2_spmd} | conditional | flops 603979904 | bytes 43618404 | solution.py:202
  24.5 0.3 copy.37
  24.9 0.4 reshape.31
  25.4 9.1 %collective-permute-start.1 = (bf16[2,32,512]{2,1,0:T(8,128)(2,1)S(1)}, bf16[2,32,512]{2,1,0:T(8,128)(2,1)S(1)}, u32[]{:S(2)}, u32[]{:S(2)}) collective-permute-start(bf16[2,32,512]{2,1,0:T(8,128)(2,1)S(1)} %get-tuple-element.47), channel_id=1, source_target_pairs={{0,25},{1,26},{2,24},{24,2},{25,0},{26,1},{3,28},{4,29},{5,27},{27... | collective-permute-start | bytes 196616 | tf_op jit(solution)/shard_map/cond/branch_0_fun/ppermute | solution.py:164
  34.5 3.4 %collective-permute-start = (bf16[2,32,512]{2,1,0:T(8,128)(2,1)S(1)}, bf16[2,32,512]{2,1,0:T(8,128)(2,1)S(1)}, u32[]{:S(2)}, u32[]{:S(2)}) collective-permute-start(bf16[2,32,512]{2,1,0:T(8,128)(2,1)S(1)} %get-tuple-element.48), channel_id=1, source_target_pairs={{0,1},{1,2},{2,0},{24,26},{25,24},{26,25},{3,4},{4,5},{5,3},{27,29... | collective-permute-start | bytes 196616 | tf_op jit(solution)/shard_map/cond/branch_0_fun/ppermute | solution.py:162
  37.9 6.3 %collective-permute-done = bf16[2,32,512]{2,1,0:T(8,128)(2,1)S(1)} collective-permute-done((bf16[2,32,512]{2,1,0:T(8,128)(2,1)S(1)}, bf16[2,32,512]{2,1,0:T(8,128)(2,1)S(1)}, u32[]{:S(2)}, u32[]{:S(2)}) %collective-permute-start) | collective-permute-done | bytes 65568 | tf_op jit(solution)/shard_map/cond/branch_0_fun/ppermute | solution.py:162
  44.2 3.2 %collective-permute-start.3 = (bf16[2,96,512]{2,1,0:T(8,128)(2,1)S(1)}, bf16[2,96,512]{2,1,0:T(8,128)(2,1)S(1)}, u32[]{:S(2)}, u32[]{:S(2)}) collective-permute-start(bf16[2,96,512]{2,1,0:T(8,128)(2,1)S(1)} %bitcast.104), channel_id=1, source_target_pairs={{0,21},{3,0},{6,3},{9,6},{12,9},{15,12},{18,15},{21,18},{24,27},{2... | collective-permute-start | bytes 589832 | tf_op jit(solution)/shard_map/cond/branch_0_fun/ppermute | solution.py:144
  47.4 3.8 %collective-permute-start.2 = (bf16[2,96,512]{2,1,0:T(8,128)(2,1)S(1)}, bf16[2,96,512]{2,1,0:T(8,128)(2,1)S(1)}, u32[]{:S(2)}, u32[]{:S(2)}) collective-permute-start(bf16[2,96,512]{2,1,0:T(8,128)(2,1)S(1)} %bitcast.105), channel_id=1, source_target_pairs={{0,3},{3,6},{6,9},{9,12},{12,15},{15,18},{18,21},{21,0},{24,45},{2... | collective-permute-start | bytes 589832 | tf_op jit(solution)/shard_map/cond/branch_0_fun/ppermute | solution.py:144
  51.5 0.8 collective-permute-done.3
  52.4 1.9 %collective-permute-start.5 = (bf16[2,96,512]{2,1,0:T(8,128)(2,1)S(1)}, bf16[2,96,512]{2,1,0:T(8,128)(2,1)S(1)}, u32[]{:S(2)}, u32[]{:S(2)}) collective-permute-start(bf16[2,96,512]{2,1,0:T(8,128)(2,1)S(1)} %collective-permute-done.3), channel_id=1, source_target_pairs={{0,21},{3,0},{6,3},{9,6},{12,9},{15,12},{18,15},{21,18},{24,27},{2... | collective-permute-start | bytes 589832 | tf_op jit(solution)/shard_map/cond/branch_0_fun/ppermute | solution.py:144
  54.4 5.0 %collective-permute-start.4 = (bf16[2,96,512]{2,1,0:T(8,128)(2,1)S(1)}, bf16[2,96,512]{2,1,0:T(8,128)(2,1)S(1)}, u32[]{:S(2)}, u32[]{:S(2)}) collective-permute-start(bf16[2,96,512]{2,1,0:T(8,128)(2,1)S(1)} %collective-permute-done.2), channel_id=1, source_target_pairs={{0,3},{3,6},{6,9},{9,12},{12,15},{15,18},{18,21},{21,0},{24,45},{2... | collective-permute-start | bytes 589832 | tf_op jit(solution)/shard_map/cond/branch_0_fun/ppermute | solution.py:144
  59.5 0.5 collective-permute-done.5
  60.0 1.9 %collective-permute-start.8 = (bf16[2,96,512]{2,1,0:T(8,128)(2,1)S(1)}, bf16[2,96,512]{2,1,0:T(8,128)(2,1)S(1)}, u32[]{:S(2)}, u32[]{:S(2)}) collective-permute-start(bf16[2,96,512]{2,1,0:T(8,128)(2,1)S(1)} %collective-permute-done.5), channel_id=1, source_target_pairs={{0,18},{3,21},{6,0},{9,3},{12,6},{15,9},{18,12},{21,15},{24,30},{2... | collective-permute-start | bytes 589832 | tf_op jit(solution)/shard_map/cond/branch_0_fun/ppermute | solution.py:144
  61.9 4.4 %collective-permute-start.7 = (bf16[2,96,512]{2,1,0:T(8,128)(2,1)S(1)}, bf16[2,96,512]{2,1,0:T(8,128)(2,1)S(1)}, u32[]{:S(2)}, u32[]{:S(2)}) collective-permute-start(bf16[2,96,512]{2,1,0:T(8,128)(2,1)S(1)} %collective-permute-done.5), channel_id=1, source_target_pairs={{0,21},{3,0},{6,3},{9,6},{12,9},{15,12},{18,15},{21,18},{24,27},{2... | collective-permute-start | bytes 589832 | tf_op jit(solution)/shard_map/cond/branch_0_fun/ppermute | solution.py:144
  66.3 2.4 %collective-permute-start.6 = (bf16[2,96,512]{2,1,0:T(8,128)(2,1)S(1)}, bf16[2,96,512]{2,1,0:T(8,128)(2,1)S(1)}, u32[]{:S(2)}, u32[]{:S(2)}) collective-permute-start(bf16[2,96,512]{2,1,0:T(8,128)(2,1)S(1)} %collective-permute-done.4), channel_id=1, source_target_pairs={{0,3},{3,6},{6,9},{9,12},{12,15},{15,18},{18,21},{21,0},{24,45},{2... | collective-permute-start | bytes 589832 | tf_op jit(solution)/shard_map/cond/branch_0_fun/ppermute | solution.py:144
  68.8 8.2 %collective-permute-done.6 = bf16[2,96,512]{2,1,0:T(8,128)(2,1)S(1)} collective-permute-done((bf16[2,96,512]{2,1,0:T(8,128)(2,1)S(1)}, bf16[2,96,512]{2,1,0:T(8,128)(2,1)S(1)}, u32[]{:S(2)}, u32[]{:S(2)}) %collective-permute-start.6) | collective-permute-done | bytes 196640 | tf_op jit(solution)/shard_map/cond/branch_0_fun/ppermute | solution.py:144
  77.0 5.5 %collective-permute-start.9 = (bf16[2,8,96,512]{3,2,1,0:T(8,128)(2,1)S(1)}, bf16[2,8,96,512]{3,2,1,0:T(8,128)(2,1)S(1)}, u32[]{:S(2)}, u32[]{:S(2)}) collective-permute-start(bf16[2,8,96,512]{3,2,1,0:T(8,128)(2,1)S(1)} %bitcast_dynamic-update-slice_fusion.6), channel_id=1, source_target_pairs={{0,24},{24,0},{1,25},{25,1},{2,26},{26,2},{3,27},{27,3},{4,28},{28... | collective-permute-start | bytes 4718600 | tf_op jit(solution)/shard_map/cond/branch_0_fun/ppermute | solution.py:21
  82.5 2.1 %branch_0_fun.2 = (bf16[3,256,1024]{2,1,0:T(8,128)(2,1)}, bf16[3,256,768]{2,1,0:T(8,128)(2,1)S(1)}, bf16[3,256,512]{2,1,0:T(8,128)(2,1)S(1)}) custom-call(s32[4]{0:T(128)S(1)} %get-tuple-element.26.where_ref, bf16[3,256,768]{2,1,0:T(8,128)(2,1)S(1)} %copy-done.2, bf16[2,768,512]{2,1,0:T(8,128)(2,1)S(1)} %bitcast.96, bf16[3,256,1024]{2,1,0:T(8,128)(2,1)S(1)} %copy-done), custom_call_target="tpu_custom_call" | custom-call | flops 603979776 | bytes 4000000 | tf_op jit(solution)/shard_map/cond/branch_0_fun/pallas_call | solution.py:112
  84.6 0.9 %collective-permute-done.9 = bf16[2,8,96,512]{3,2,1,0:T(8,128)(2,1)S(1)} collective-permute-done((bf16[2,8,96,512]{3,2,1,0:T(8,128)(2,1)S(1)}, bf16[2,8,96,512]{3,2,1,0:T(8,128)(2,1)S(1)}, u32[]{:S(2)}, u32[]{:S(2)}) %collective-permute-start.9) | collective-permute-done | bytes 1572896 | tf_op jit(solution)/shard_map/cond/branch_0_fun/ppermute | solution.py:21
  85.5 2.0 %branch_0_fun.3 = bf16[3,256,1024]{2,1,0:T(8,128)(2,1)} custom-call(s32[4]{0:T(128)S(1)} %get-tuple-element.26.where_ref, bf16[3,256,768]{2,1,0:T(8,128)(2,1)S(1)} %get-tuple-element.30.integrals_ref, bf16[2,768,512]{2,1,0:T(8,128)(2,1)S(1)} %bitcast.98, bf16[3,256,512]{2,1,0:T(8,128)(2,1)S(1)} %get-tuple-element.31.previous_ref, ...), custom_call_target="tpu_custom_call", output_to_operand_aliasing={{}: (4, {})} | custom-call | tf_op jit(solution)/shard_map/cond/branch_0_fun/pallas_call | solution.py:130
  (24 shorter events, 0.8 us)
Async XLA Ops:
  1.6 22.7 %all-to-all-start.1 = ((bf16[32,16,128]{2,1,0:T(8,128)(2,1)}), bf16[32,16,128]{2,1,0:T(8,128)(2,1)S(1)}, u32[]{:S(2)}, u32[]{:S(2)}) async-start(bf16[32,16,128]{2,1,0:T(8,128)(2,1)} %get-tuple-element.45), calls=%async_computation.1 | async-start | bytes 262144 | tf_op jit(solution)/shard_map/all_to_all | solution.py:190
  25.4 18.8 %collective-permute-start.1 = (bf16[2,32,512]{2,1,0:T(8,128)(2,1)S(1)}, bf16[2,32,512]{2,1,0:T(8,128)(2,1)S(1)}, u32[]{:S(2)}, u32[]{:S(2)}) collective-permute-start(bf16[2,32,512]{2,1,0:T(8,128)(2,1)S(1)} %get-tuple-element.47), channel_id=1, source_target_pairs={{0,25},{1,26},{2,24},{24,2},{25,0},{26,1},{3,28},{4,29},{5,27},{27... | collective-permute-start | bytes 196616 | tf_op jit(solution)/shard_map/cond/branch_0_fun/ppermute | solution.py:164
  34.5 9.7 %collective-permute-start = (bf16[2,32,512]{2,1,0:T(8,128)(2,1)S(1)}, bf16[2,32,512]{2,1,0:T(8,128)(2,1)S(1)}, u32[]{:S(2)}, u32[]{:S(2)}) collective-permute-start(bf16[2,32,512]{2,1,0:T(8,128)(2,1)S(1)} %get-tuple-element.48), channel_id=1, source_target_pairs={{0,1},{1,2},{2,0},{24,26},{25,24},{26,25},{3,4},{4,5},{5,3},{27,29... | collective-permute-start | bytes 196616 | tf_op jit(solution)/shard_map/cond/branch_0_fun/ppermute | solution.py:162
  44.2 8.1 %collective-permute-start.3 = (bf16[2,96,512]{2,1,0:T(8,128)(2,1)S(1)}, bf16[2,96,512]{2,1,0:T(8,128)(2,1)S(1)}, u32[]{:S(2)}, u32[]{:S(2)}) collective-permute-start(bf16[2,96,512]{2,1,0:T(8,128)(2,1)S(1)} %bitcast.104), channel_id=1, source_target_pairs={{0,21},{3,0},{6,3},{9,6},{12,9},{15,12},{18,15},{21,18},{24,27},{2... | collective-permute-start | bytes 589832 | tf_op jit(solution)/shard_map/cond/branch_0_fun/ppermute | solution.py:144
  47.4 7.0 %collective-permute-start.2 = (bf16[2,96,512]{2,1,0:T(8,128)(2,1)S(1)}, bf16[2,96,512]{2,1,0:T(8,128)(2,1)S(1)}, u32[]{:S(2)}, u32[]{:S(2)}) collective-permute-start(bf16[2,96,512]{2,1,0:T(8,128)(2,1)S(1)} %bitcast.105), channel_id=1, source_target_pairs={{0,3},{3,6},{6,9},{9,12},{12,15},{15,18},{18,21},{21,0},{24,45},{2... | collective-permute-start | bytes 589832 | tf_op jit(solution)/shard_map/cond/branch_0_fun/ppermute | solution.py:144
  51.5 31.0 %copy-start = (bf16[3,256,1024]{2,1,0:T(8,128)(2,1)S(1)}, bf16[3,256,1024]{2,1,0:T(8,128)(2,1)}, u32[]{:S(2)}) copy-start(bf16[3,256,1024]{2,1,0:T(8,128)(2,1)} %get-tuple-element.29.previous_ref) | copy-start | bytes 4718596 | tf_op jit(solution)/shard_map/cond
  51.5 31.0 %copy-start.2 = (bf16[3,256,768]{2,1,0:T(8,128)(2,1)S(1)}, bf16[3,256,768]{2,1,0:T(8,128)(2,1)}, u32[]{:S(2)}) copy-start(bf16[3,256,768]{2,1,0:T(8,128)(2,1)} %get-tuple-element.27.integrals_ref) | copy-start | bytes 3538948 | tf_op jit(solution)/shard_map/cond
  52.4 7.6 %collective-permute-start.5 = (bf16[2,96,512]{2,1,0:T(8,128)(2,1)S(1)}, bf16[2,96,512]{2,1,0:T(8,128)(2,1)S(1)}, u32[]{:S(2)}, u32[]{:S(2)}) collective-permute-start(bf16[2,96,512]{2,1,0:T(8,128)(2,1)S(1)} %collective-permute-done.3), channel_id=1, source_target_pairs={{0,21},{3,0},{6,3},{9,6},{12,9},{15,12},{18,15},{21,18},{24,27},{2... | collective-permute-start | bytes 589832 | tf_op jit(solution)/shard_map/cond/branch_0_fun/ppermute | solution.py:144
  54.4 11.9 %collective-permute-start.4 = (bf16[2,96,512]{2,1,0:T(8,128)(2,1)S(1)}, bf16[2,96,512]{2,1,0:T(8,128)(2,1)S(1)}, u32[]{:S(2)}, u32[]{:S(2)}) collective-permute-start(bf16[2,96,512]{2,1,0:T(8,128)(2,1)S(1)} %collective-permute-done.2), channel_id=1, source_target_pairs={{0,3},{3,6},{6,9},{9,12},{12,15},{15,18},{18,21},{21,0},{24,45},{2... | collective-permute-start | bytes 589832 | tf_op jit(solution)/shard_map/cond/branch_0_fun/ppermute | solution.py:144
  60.0 17.0 %collective-permute-start.8 = (bf16[2,96,512]{2,1,0:T(8,128)(2,1)S(1)}, bf16[2,96,512]{2,1,0:T(8,128)(2,1)S(1)}, u32[]{:S(2)}, u32[]{:S(2)}) collective-permute-start(bf16[2,96,512]{2,1,0:T(8,128)(2,1)S(1)} %collective-permute-done.5), channel_id=1, source_target_pairs={{0,18},{3,21},{6,0},{9,3},{12,6},{15,9},{18,12},{21,15},{24,30},{2... | collective-permute-start | bytes 589832 | tf_op jit(solution)/shard_map/cond/branch_0_fun/ppermute | solution.py:144
  61.9 15.0 %collective-permute-start.7 = (bf16[2,96,512]{2,1,0:T(8,128)(2,1)S(1)}, bf16[2,96,512]{2,1,0:T(8,128)(2,1)S(1)}, u32[]{:S(2)}, u32[]{:S(2)}) collective-permute-start(bf16[2,96,512]{2,1,0:T(8,128)(2,1)S(1)} %collective-permute-done.5), channel_id=1, source_target_pairs={{0,21},{3,0},{6,3},{9,6},{12,9},{15,12},{18,15},{21,18},{24,27},{2... | collective-permute-start | bytes 589832 | tf_op jit(solution)/shard_map/cond/branch_0_fun/ppermute | solution.py:144
  66.3 10.6 %collective-permute-start.6 = (bf16[2,96,512]{2,1,0:T(8,128)(2,1)S(1)}, bf16[2,96,512]{2,1,0:T(8,128)(2,1)S(1)}, u32[]{:S(2)}, u32[]{:S(2)}) collective-permute-start(bf16[2,96,512]{2,1,0:T(8,128)(2,1)S(1)} %collective-permute-done.4), channel_id=1, source_target_pairs={{0,3},{3,6},{6,9},{9,12},{12,15},{15,18},{18,21},{21,0},{24,45},{2... | collective-permute-start | bytes 589832 | tf_op jit(solution)/shard_map/cond/branch_0_fun/ppermute | solution.py:144
  77.0 8.5 %collective-permute-start.9 = (bf16[2,8,96,512]{3,2,1,0:T(8,128)(2,1)S(1)}, bf16[2,8,96,512]{3,2,1,0:T(8,128)(2,1)S(1)}, u32[]{:S(2)}, u32[]{:S(2)}) collective-permute-start(bf16[2,8,96,512]{3,2,1,0:T(8,128)(2,1)S(1)} %bitcast_dynamic-update-slice_fusion.6), channel_id=1, source_target_pairs={{0,24},{24,0},{1,25},{25,1},{2,26},{26,2},{3,27},{27,3},{4,28},{28... | collective-permute-start | bytes 4718600 | tf_op jit(solution)/shard_map/cond/branch_0_fun/ppermute | solution.py:21

commit v8 on v7

--- a/solution.py
+++ b/solution.py
@@ -173,8 +173,10 @@
     for step in range(1, y_size // 2 - 1):
         first, second = turn(first, -1), turn(second, 1)
         whole = put(put(whole, second, y - way * step), first, y + way * step)
+        if step == 1:
+            far = turn(first, step - y_size // 2)
     last = y_size // 2 - 1
-    far, second, first = turn(first, -2), turn(second, 1), turn(first, -1)
+    second, first = turn(second, 1), turn(first, -1)
     whole = put(put(put(whole, second, y - way * last), first, y + way * last), far, y + last + 1)
     other = shift(whole, "core", 1)
     flat = (slots, y_size * z_size * depth, half * width)

time: 88.1 us -> 92.4 us (1.049)
  starting transfers between devices: 54.6 us -> 58.2 us
    ppermute x7, starting transfers between devices: 22.6 us -> 24.6 us  [turn(): return lax.ppermute(value, ('core', 'bulk_0'), pairs)]
    ppermute x1, starting transfers between devices: 5.46 us -> 7.1 us  [shift(): lax.ppermute(value, axis, [(i, (i + step) % size) for i in range(size)])]
  transfers between devices with their start and end apart: 11 -> 11, of which waited for: 7 -> 6; matrix products, arithmetic and copies ran while one was open for 1% -> 1% of each run, Pallas kernels for 2% -> 2%
where the time goes in v8:
time: 92.4 us; the launch traced here: 91.8 us
  starting transfers between devices  58.2 us (63%)
  waiting for transfers between devices  24.7 us (27%)
  Pallas kernels  5.72 us (6%)
  local copies, waits for them, and re-layouts  2.06 us (2%)
    ppermute x7, starting transfers between devices, turn(): return lax.ppermute(value, ('core', 'bulk_0'), pairs)  24.6 us
    all_to_all x1, starting transfers between devices, spread(): lax.all_to_all(outgoing, CHIP_CORE, split_axis=0, concat_axis=0, tiled=True)  14 us
    ppermute x7, waiting for transfers between devices, turn(): return lax.ppermute(value, ('core', 'bulk_0'), pairs)  10.2 us
    ppermute x1, starting transfers between devices, with_slots(): opposite = lax.ppermute(theirs, ('core', 'bulk_1'), across)  9.09 us
    all_to_all x1, waiting for transfers between devices, spread(): lax.all_to_all(outgoing, CHIP_CORE, split_axis=0, concat_axis=0, tiled=True)  7.33 us
    ppermute x1, starting transfers between devices, shift(): lax.ppermute(value, axis, [(i, (i + step) % size) for i in range(size)])  7.1 us
    ppermute x1, waiting for transfers between devices, with_slots(): near = lax.ppermute(mine, ('core', 'bulk_1'), same)  6.26 us
    ppermute x1, starting transfers between devices, with_slots(): near = lax.ppermute(mine, ('core', 'bulk_1'), same)  3.36 us
  transfers between devices with their start and end apart: 11, of which 6 were waited for; matrix products, arithmetic and copies ran while one was open for 1% of the time, Pallas kernels for 2%

profile of v8, /device:TPU:1, one launch (start us, length us, event | category | flops | bytes accessed | tf_op | source)
XLA Modules:
  0.0 91.8 jit_solution(869103413225291263)
XLA Ops:
  0.0 1.6 %shard_map.48 = (bf16[32,16,128]{2,1,0:T(8,128)(2,1)}, s32[4]{0:T(128)S(1)}) custom-call(s32[2304]{0:T(1024)} %labels_ref.1, bf16[4,32,32]{2,1,0:T(8,128)(2,1)} %amplitudes_ref.1), custom_call_target="tpu_custom_call" | custom-call | tf_op jit(solution)/shard_map/pallas_call | solution.py:56
  1.6 14.0 %all-to-all-start.1 = ((bf16[32,16,128]{2,1,0:T(8,128)(2,1)}), bf16[32,16,128]{2,1,0:T(8,128)(2,1)S(1)}, u32[]{:S(2)}, u32[]{:S(2)}) async-start(bf16[32,16,128]{2,1,0:T(8,128)(2,1)} %get-tuple-element.45), calls=%async_computation.1 | async-start | bytes 262144 | tf_op jit(solution)/shard_map/all_to_all | solution.py:192
  15.6 0.6 slice.3
  17.0 7.3 %all-to-all-done.1 = bf16[32,16,128]{2,1,0:T(8,128)(2,1)S(1)} async-done(((bf16[32,16,128]{2,1,0:T(8,128)(2,1)}), bf16[32,16,128]{2,1,0:T(8,128)(2,1)S(1)}, u32[]{:S(2)}, u32[]{:S(2)}) %all-to-all-start.1) | async-done | bytes 131104 | tf_op jit(solution)/shard_map/all_to_all | solution.py:192
  24.3 67.5 %conditional.1 = (bf16[3,256,1024]{2,1,0:T(8,128)(2,1)}) conditional(s32[]{:T(128)} %bitcast.58, (bf16[32,16,128]{2,1,0:T(8,128)(2,1)S(1)}, s32[4]{0:T(128)S(1)}, bf16[3,256,768]{2,1,0:T(8,128)(2,1)}, bf16[3,256,1024]{2,1,0:T(8,128)(2,1)}) %tuple.11, (s32[2304]{0:T(1024)}, bf16[4,32,32]{2,1,0:T(8,128)(2,1)}, s32[4]{0:T(128)S(1)}, ...), branch_computations={%region_0.1_spmd, %region_1.2_spmd} | conditional | flops 603979904 | bytes 43618404 | solution.py:204
  24.5 0.3 copy.37
  24.9 0.4 reshape.31
  25.4 9.1 %collective-permute-start.1 = (bf16[2,32,512]{2,1,0:T(8,128)(2,1)S(1)}, bf16[2,32,512]{2,1,0:T(8,128)(2,1)S(1)}, u32[]{:S(2)}, u32[]{:S(2)}) collective-permute-start(bf16[2,32,512]{2,1,0:T(8,128)(2,1)S(1)} %get-tuple-element.47), channel_id=1, source_target_pairs={{0,25},{1,26},{2,24},{24,2},{25,0},{26,1},{3,28},{4,29},{5,27},{27... | collective-permute-start | bytes 196616 | tf_op jit(solution)/shard_map/cond/branch_0_fun/ppermute | solution.py:164
  34.5 3.4 %collective-permute-start = (bf16[2,32,512]{2,1,0:T(8,128)(2,1)S(1)}, bf16[2,32,512]{2,1,0:T(8,128)(2,1)S(1)}, u32[]{:S(2)}, u32[]{:S(2)}) collective-permute-start(bf16[2,32,512]{2,1,0:T(8,128)(2,1)S(1)} %get-tuple-element.48), channel_id=1, source_target_pairs={{0,1},{1,2},{2,0},{24,26},{25,24},{26,25},{3,4},{4,5},{5,3},{27,29... | collective-permute-start | bytes 196616 | tf_op jit(solution)/shard_map/cond/branch_0_fun/ppermute | solution.py:162
  37.9 6.3 %collective-permute-done = bf16[2,32,512]{2,1,0:T(8,128)(2,1)S(1)} collective-permute-done((bf16[2,32,512]{2,1,0:T(8,128)(2,1)S(1)}, bf16[2,32,512]{2,1,0:T(8,128)(2,1)S(1)}, u32[]{:S(2)}, u32[]{:S(2)}) %collective-permute-start) | collective-permute-done | bytes 65568 | tf_op jit(solution)/shard_map/cond/branch_0_fun/ppermute | solution.py:162
  44.2 3.2 %collective-permute-start.3 = (bf16[2,96,512]{2,1,0:T(8,128)(2,1)S(1)}, bf16[2,96,512]{2,1,0:T(8,128)(2,1)S(1)}, u32[]{:S(2)}, u32[]{:S(2)}) collective-permute-start(bf16[2,96,512]{2,1,0:T(8,128)(2,1)S(1)} %bitcast.104), channel_id=1, source_target_pairs={{0,21},{3,0},{6,3},{9,6},{12,9},{15,12},{18,15},{21,18},{24,27},{2... | collective-permute-start | bytes 589832 | tf_op jit(solution)/shard_map/cond/branch_0_fun/ppermute | solution.py:144
  47.4 3.8 %collective-permute-start.2 = (bf16[2,96,512]{2,1,0:T(8,128)(2,1)S(1)}, bf16[2,96,512]{2,1,0:T(8,128)(2,1)S(1)}, u32[]{:S(2)}, u32[]{:S(2)}) collective-permute-start(bf16[2,96,512]{2,1,0:T(8,128)(2,1)S(1)} %bitcast.105), channel_id=1, source_target_pairs={{0,3},{3,6},{6,9},{9,12},{12,15},{15,18},{18,21},{21,0},{24,45},{2... | collective-permute-start | bytes 589832 | tf_op jit(solution)/shard_map/cond/branch_0_fun/ppermute | solution.py:144
  51.5 0.8 collective-permute-done.3
  52.4 4.2 %collective-permute-start.8 = (bf16[2,96,512]{2,1,0:T(8,128)(2,1)S(1)}, bf16[2,96,512]{2,1,0:T(8,128)(2,1)S(1)}, u32[]{:S(2)}, u32[]{:S(2)}) collective-permute-start(bf16[2,96,512]{2,1,0:T(8,128)(2,1)S(1)} %collective-permute-done.3), channel_id=1, source_target_pairs={{0,15},{3,18},{6,21},{9,0},{12,3},{15,6},{18,9},{21,12},{24,33},{2... | collective-permute-start | bytes 589832 | tf_op jit(solution)/shard_map/cond/branch_0_fun/ppermute | solution.py:144
  56.6 4.9 %collective-permute-start.5 = (bf16[2,96,512]{2,1,0:T(8,128)(2,1)S(1)}, bf16[2,96,512]{2,1,0:T(8,128)(2,1)S(1)}, u32[]{:S(2)}, u32[]{:S(2)}) collective-permute-start(bf16[2,96,512]{2,1,0:T(8,128)(2,1)S(1)} %collective-permute-done.3), channel_id=1, source_target_pairs={{0,21},{3,0},{6,3},{9,6},{12,9},{15,12},{18,15},{21,18},{24,27},{2... | collective-permute-start | bytes 589832 | tf_op jit(solution)/shard_map/cond/branch_0_fun/ppermute | solution.py:144
  61.5 1.9 %collective-permute-start.4 = (bf16[2,96,512]{2,1,0:T(8,128)(2,1)S(1)}, bf16[2,96,512]{2,1,0:T(8,128)(2,1)S(1)}, u32[]{:S(2)}, u32[]{:S(2)}) collective-permute-start(bf16[2,96,512]{2,1,0:T(8,128)(2,1)S(1)} %collective-permute-done.2), channel_id=1, source_target_pairs={{0,3},{3,6},{6,9},{9,12},{12,15},{15,18},{18,21},{21,0},{24,45},{2... | collective-permute-start | bytes 589832 | tf_op jit(solution)/shard_map/cond/branch_0_fun/ppermute | solution.py:144
  63.5 3.7 %collective-permute-done.5 = bf16[2,96,512]{2,1,0:T(8,128)(2,1)S(1)} collective-permute-done((bf16[2,96,512]{2,1,0:T(8,128)(2,1)S(1)}, bf16[2,96,512]{2,1,0:T(8,128)(2,1)S(1)}, u32[]{:S(2)}, u32[]{:S(2)}) %collective-permute-start.5) | collective-permute-done | bytes 196640 | tf_op jit(solution)/shard_map/cond/branch_0_fun/ppermute | solution.py:144
  67.2 4.3 %collective-permute-start.7 = (bf16[2,96,512]{2,1,0:T(8,128)(2,1)S(1)}, bf16[2,96,512]{2,1,0:T(8,128)(2,1)S(1)}, u32[]{:S(2)}, u32[]{:S(2)}) collective-permute-start(bf16[2,96,512]{2,1,0:T(8,128)(2,1)S(1)} %collective-permute-done.5), channel_id=1, source_target_pairs={{0,21},{3,0},{6,3},{9,6},{12,9},{15,12},{18,15},{21,18},{24,27},{2... | collective-permute-start | bytes 589832 | tf_op jit(solution)/shard_map/cond/branch_0_fun/ppermute | solution.py:144
  71.5 2.3 %collective-permute-start.6 = (bf16[2,96,512]{2,1,0:T(8,128)(2,1)S(1)}, bf16[2,96,512]{2,1,0:T(8,128)(2,1)S(1)}, u32[]{:S(2)}, u32[]{:S(2)}) collective-permute-start(bf16[2,96,512]{2,1,0:T(8,128)(2,1)S(1)} %collective-permute-done.4), channel_id=1, source_target_pairs={{0,3},{3,6},{6,9},{9,12},{12,15},{15,18},{18,21},{21,0},{24,45},{2... | collective-permute-start | bytes 589832 | tf_op jit(solution)/shard_map/cond/branch_0_fun/ppermute | solution.py:144
  73.8 5.7 %collective-permute-done.6 = bf16[2,96,512]{2,1,0:T(8,128)(2,1)S(1)} collective-permute-done((bf16[2,96,512]{2,1,0:T(8,128)(2,1)S(1)}, bf16[2,96,512]{2,1,0:T(8,128)(2,1)S(1)}, u32[]{:S(2)}, u32[]{:S(2)}) %collective-permute-start.6) | collective-permute-done | bytes 196640 | tf_op jit(solution)/shard_map/cond/branch_0_fun/ppermute | solution.py:144
  79.7 7.1 %collective-permute-start.9 = (bf16[2,8,96,512]{3,2,1,0:T(8,128)(2,1)S(1)}, bf16[2,8,96,512]{3,2,1,0:T(8,128)(2,1)S(1)}, u32[]{:S(2)}, u32[]{:S(2)}) collective-permute-start(bf16[2,8,96,512]{3,2,1,0:T(8,128)(2,1)S(1)} %bitcast_dynamic-update-slice_fusion.6), channel_id=1, source_target_pairs={{0,24},{24,0},{1,25},{25,1},{2,26},{26,2},{3,27},{27,3},{4,28},{28... | collective-permute-start | bytes 4718600 | tf_op jit(solution)/shard_map/cond/branch_0_fun/ppermute | solution.py:21
  86.8 2.1 %branch_0_fun.2 = (bf16[3,256,1024]{2,1,0:T(8,128)(2,1)}, bf16[3,256,768]{2,1,0:T(8,128)(2,1)S(1)}, bf16[3,256,512]{2,1,0:T(8,128)(2,1)S(1)}) custom-call(s32[4]{0:T(128)S(1)} %get-tuple-element.26.where_ref, bf16[3,256,768]{2,1,0:T(8,128)(2,1)S(1)} %copy-done.2, bf16[2,768,512]{2,1,0:T(8,128)(2,1)S(1)} %bitcast.96, bf16[3,256,1024]{2,1,0:T(8,128)(2,1)S(1)} %copy-done), custom_call_target="tpu_custom_call" | custom-call | flops 603979776 | bytes 4000000 | tf_op jit(solution)/shard_map/cond/branch_0_fun/pallas_call | solution.py:112
  88.9 0.9 collective-permute-done.9
  89.8 2.0 %branch_0_fun.3 = bf16[3,256,1024]{2,1,0:T(8,128)(2,1)} custom-call(s32[4]{0:T(128)S(1)} %get-tuple-element.26.where_ref, bf16[3,256,768]{2,1,0:T(8,128)(2,1)S(1)} %get-tuple-element.30.integrals_ref, bf16[2,768,512]{2,1,0:T(8,128)(2,1)S(1)} %bitcast.98, bf16[3,256,512]{2,1,0:T(8,128)(2,1)S(1)} %get-tuple-element.31.previous_ref, ...), custom_call_target="tpu_custom_call", output_to_operand_aliasing={{}: (4, {})} | custom-call | tf_op jit(solution)/shard_map/cond/branch_0_fun/pallas_call | solution.py:130
  (24 shorter events, 0.6 us)
Async XLA Ops:
  1.6 22.7 %all-to-all-start.1 = ((bf16[32,16,128]{2,1,0:T(8,128)(2,1)}), bf16[32,16,128]{2,1,0:T(8,128)(2,1)S(1)}, u32[]{:S(2)}, u32[]{:S(2)}) async-start(bf16[32,16,128]{2,1,0:T(8,128)(2,1)} %get-tuple-element.45), calls=%async_computation.1 | async-start | bytes 262144 | tf_op jit(solution)/shard_map/all_to_all | solution.py:192
  25.4 18.8 %collective-permute-start.1 = (bf16[2,32,512]{2,1,0:T(8,128)(2,1)S(1)}, bf16[2,32,512]{2,1,0:T(8,128)(2,1)S(1)}, u32[]{:S(2)}, u32[]{:S(2)}) collective-permute-start(bf16[2,32,512]{2,1,0:T(8,128)(2,1)S(1)} %get-tuple-element.47), channel_id=1, source_target_pairs={{0,25},{1,26},{2,24},{24,2},{25,0},{26,1},{3,28},{4,29},{5,27},{27... | collective-permute-start | bytes 196616 | tf_op jit(solution)/shard_map/cond/branch_0_fun/ppermute | solution.py:164
  34.5 9.7 %collective-permute-start = (bf16[2,32,512]{2,1,0:T(8,128)(2,1)S(1)}, bf16[2,32,512]{2,1,0:T(8,128)(2,1)S(1)}, u32[]{:S(2)}, u32[]{:S(2)}) collective-permute-start(bf16[2,32,512]{2,1,0:T(8,128)(2,1)S(1)} %get-tuple-element.48), channel_id=1, source_target_pairs={{0,1},{1,2},{2,0},{24,26},{25,24},{26,25},{3,4},{4,5},{5,3},{27,29... | collective-permute-start | bytes 196616 | tf_op jit(solution)/shard_map/cond/branch_0_fun/ppermute | solution.py:162
  44.2 8.1 %collective-permute-start.3 = (bf16[2,96,512]{2,1,0:T(8,128)(2,1)S(1)}, bf16[2,96,512]{2,1,0:T(8,128)(2,1)S(1)}, u32[]{:S(2)}, u32[]{:S(2)}) collective-permute-start(bf16[2,96,512]{2,1,0:T(8,128)(2,1)S(1)} %bitcast.104), channel_id=1, source_target_pairs={{0,21},{3,0},{6,3},{9,6},{12,9},{15,12},{18,15},{21,18},{24,27},{2... | collective-permute-start | bytes 589832 | tf_op jit(solution)/shard_map/cond/branch_0_fun/ppermute | solution.py:144
  47.4 14.1 %collective-permute-start.2 = (bf16[2,96,512]{2,1,0:T(8,128)(2,1)S(1)}, bf16[2,96,512]{2,1,0:T(8,128)(2,1)S(1)}, u32[]{:S(2)}, u32[]{:S(2)}) collective-permute-start(bf16[2,96,512]{2,1,0:T(8,128)(2,1)S(1)} %bitcast.105), channel_id=1, source_target_pairs={{0,3},{3,6},{6,9},{9,12},{12,15},{15,18},{18,21},{21,0},{24,45},{2... | collective-permute-start | bytes 589832 | tf_op jit(solution)/shard_map/cond/branch_0_fun/ppermute | solution.py:144
  51.5 35.3 %copy-start = (bf16[3,256,1024]{2,1,0:T(8,128)(2,1)S(1)}, bf16[3,256,1024]{2,1,0:T(8,128)(2,1)}, u32[]{:S(2)}) copy-start(bf16[3,256,1024]{2,1,0:T(8,128)(2,1)} %get-tuple-element.29.previous_ref) | copy-start | bytes 4718596 | tf_op jit(solution)/shard_map/cond
  51.5 35.3 %copy-start.2 = (bf16[3,256,768]{2,1,0:T(8,128)(2,1)S(1)}, bf16[3,256,768]{2,1,0:T(8,128)(2,1)}, u32[]{:S(2)}) copy-start(bf16[3,256,768]{2,1,0:T(8,128)(2,1)} %get-tuple-element.27.integrals_ref) | copy-start | bytes 3538948 | tf_op jit(solution)/shard_map/cond
  52.4 27.2 %collective-permute-start.8 = (bf16[2,96,512]{2,1,0:T(8,128)(2,1)S(1)}, bf16[2,96,512]{2,1,0:T(8,128)(2,1)S(1)}, u32[]{:S(2)}, u32[]{:S(2)}) collective-permute-start(bf16[2,96,512]{2,1,0:T(8,128)(2,1)S(1)} %collective-permute-done.3), channel_id=1, source_target_pairs={{0,15},{3,18},{6,21},{9,0},{12,3},{15,6},{18,9},{21,12},{24,33},{2... | collective-permute-start | bytes 589832 | tf_op jit(solution)/shard_map/cond/branch_0_fun/ppermute | solution.py:144
  56.6 10.6 %collective-permute-start.5 = (bf16[2,96,512]{2,1,0:T(8,128)(2,1)S(1)}, bf16[2,96,512]{2,1,0:T(8,128)(2,1)S(1)}, u32[]{:S(2)}, u32[]{:S(2)}) collective-permute-start(bf16[2,96,512]{2,1,0:T(8,128)(2,1)S(1)} %collective-permute-done.3), channel_id=1, source_target_pairs={{0,21},{3,0},{6,3},{9,6},{12,9},{15,12},{18,15},{21,18},{24,27},{2... | collective-permute-start | bytes 589832 | tf_op jit(solution)/shard_map/cond/branch_0_fun/ppermute | solution.py:144
  61.5 10.0 %collective-permute-start.4 = (bf16[2,96,512]{2,1,0:T(8,128)(2,1)S(1)}, bf16[2,96,512]{2,1,0:T(8,128)(2,1)S(1)}, u32[]{:S(2)}, u32[]{:S(2)}) collective-permute-start(bf16[2,96,512]{2,1,0:T(8,128)(2,1)S(1)} %collective-permute-done.2), channel_id=1, source_target_pairs={{0,3},{3,6},{6,9},{9,12},{12,15},{15,18},{18,21},{21,0},{24,45},{2... | collective-permute-start | bytes 589832 | tf_op jit(solution)/shard_map/cond/branch_0_fun/ppermute | solution.py:144
  67.2 12.4 %collective-permute-start.7 = (bf16[2,96,512]{2,1,0:T(8,128)(2,1)S(1)}, bf16[2,96,512]{2,1,0:T(8,128)(2,1)S(1)}, u32[]{:S(2)}, u32[]{:S(2)}) collective-permute-start(bf16[2,96,512]{2,1,0:T(8,128)(2,1)S(1)} %collective-permute-done.5), channel_id=1, source_target_pairs={{0,21},{3,0},{6,3},{9,6},{12,9},{15,12},{18,15},{21,18},{24,27},{2... | collective-permute-start | bytes 589832 | tf_op jit(solution)/shard_map/cond/branch_0_fun/ppermute | solution.py:144
  71.5 8.1 %collective-permute-start.6 = (bf16[2,96,512]{2,1,0:T(8,128)(2,1)S(1)}, bf16[2,96,512]{2,1,0:T(8,128)(2,1)S(1)}, u32[]{:S(2)}, u32[]{:S(2)}) collective-permute-start(bf16[2,96,512]{2,1,0:T(8,128)(2,1)S(1)} %collective-permute-done.4), channel_id=1, source_target_pairs={{0,3},{3,6},{6,9},{9,12},{12,15},{15,18},{18,21},{21,0},{24,45},{2... | collective-permute-start | bytes 589832 | tf_op jit(solution)/shard_map/cond/branch_0_fun/ppermute | solution.py:144
  79.7 10.1 %collective-permute-start.9 = (bf16[2,8,96,512]{3,2,1,0:T(8,128)(2,1)S(1)}, bf16[2,8,96,512]{3,2,1,0:T(8,128)(2,1)S(1)}, u32[]{:S(2)}, u32[]{:S(2)}) collective-permute-start(bf16[2,8,96,512]{3,2,1,0:T(8,128)(2,1)S(1)} %bitcast_dynamic-update-slice_fusion.6), channel_id=1, source_target_pairs={{0,24},{24,0},{1,25},{25,1},{2,26},{26,2},{3,27},{27,3},{4,28},{28... | collective-permute-start | bytes 4718600 | tf_op jit(solution)/shard_map/cond/branch_0_fun/ppermute | solution.py:21

commit v9 on v5

--- a/solution.py
+++ b/solution.py
@@ -138,6 +138,12 @@
     )(where, integrals, block, previous, so_far)
 
 
+def turn(value, step):
+    size = lax.axis_size("bulk_0")
+    pairs = [(c * size + i, c * size + (i + (1 - 2 * c) * step) % size) for c in range(2) for i in range(size)]
+    return lax.ppermute(value, ("core", "bulk_0"), pairs)
+
+
 def put(whole, block, at):
     return lax.dynamic_update_slice_in_dim(whole, block[:, None], lax.rem(at + whole.shape[1], whole.shape[1]), 1)
 
@@ -156,16 +162,17 @@
         got = shift(mine, "bulk_1", step)
         group = lax.dynamic_update_slice_in_dim(group, got[:, None], lax.rem(z - step + z_size, z_size), 1)
     group = group.reshape(slots, z_size * depth, half * width)
+    way = 1 - 2 * core
     y_size, y = lax.axis_size("bulk_0"), lax.axis_index("bulk_0")
     whole = jnp.zeros((slots, y_size, z_size * depth, half * width), mine.dtype)
     whole = put(whole, group, y)
-    up, down = group, group
+    first, second = group, group
     for step in range(1, y_size // 2 - 1):
-        up, down = shift(up, "bulk_0", 1), shift(down, "bulk_0", -1)
-        whole = put(put(whole, up, y - step), down, y + step)
+        first, second = turn(first, -1), turn(second, 1)
+        whole = put(put(whole, second, y - way * step), first, y + way * step)
     last = y_size // 2 - 1
-    far, up, down = shift(down, "bulk_0", -2), shift(up, "bulk_0", 1), shift(down, "bulk_0", -1)
-    whole = put(put(put(whole, up, y - last), down, y + last), far, y + last + 1)
+    far, second, first = turn(first, -2), turn(second, 1), turn(first, -1)
+    whole = put(put(put(whole, second, y - way * last), first, y + way * last), far, y + last + 1)
     other = shift(whole, "core", 1)
     flat = (slots, y_size * z_size * depth, half * width)
     out, integrals, previous = own_half(where, integrals, whole.reshape(flat), residual_in)

time: 90 us -> 90.8 us (level)
  starting transfers between devices: 52.3 us -> 54.6 us
  waiting for transfers between devices: 28.7 us -> 27.2 us
    ppermute x0 -> x7, starting transfers between devices: none -> 23.4 us  [turn(): return lax.ppermute(value, ('core', 'bulk_0'), pairs)]
    ppermute x10 -> x3, starting transfers between devices: 38.3 us -> 17.1 us  [shift(): lax.ppermute(value, axis, [(i, (i + step) % size) for i in range(size)])]
    ppermute x10 -> x3, waiting for transfers between devices: 21.2 us -> 10.9 us  [shift(): lax.ppermute(value, axis, [(i, (i + step) % size) for i in range(size)])]
    ppermute x0 -> x7, waiting for transfers between devices: none -> 8.85 us  [turn(): return lax.ppermute(value, ('core', 'bulk_0'), pairs)]
where the time goes in v9:
time: 90.8 us; the launch traced here: 90.3 us
  starting transfers between devices  54.6 us (60%)
  waiting for transfers between devices  27.2 us (30%)
  Pallas kernels  5.72 us (6%)
  local copies, waits for them, and re-layouts  1.78 us (2%)
    ppermute x7, starting transfers between devices, turn(): return lax.ppermute(value, ('core', 'bulk_0'), pairs)  23.4 us
    ppermute x3, starting transfers between devices, shift(): lax.ppermute(value, axis, [(i, (i + step) % size) for i in range(size)])  17.1 us
    all_to_all x1, starting transfers between devices, spread(): lax.all_to_all(outgoing, CHIP_CORE, split_axis=0, concat_axis=0, tiled=True)  14 us
    ppermute x3, waiting for transfers between devices, shift(): lax.ppermute(value, axis, [(i, (i + step) % size) for i in range(size)])  10.9 us
    ppermute x7, waiting for transfers between devices, turn(): return lax.ppermute(value, ('core', 'bulk_0'), pairs)  8.85 us
    all_to_all x1, waiting for transfers between devices, spread(): lax.all_to_all(outgoing, CHIP_CORE, split_axis=0, concat_axis=0, tiled=True)  7.43 us
    pallas_call x1, Pallas kernels, own_half(): pl.pallas_call(own_kernel, in_specs=[SMEM, VMEM, VMEM, VMEM], out_specs=(...  2.09 us
    pallas_call x1, Pallas kernels, other_half(): pl.pallas_call(other_kernel, in_specs=[SMEM, VMEM, VMEM, VMEM, ANY], out_...  2.05 us
  transfers between devices with their start and end apart: 11, of which 7 were waited for; matrix products, arithmetic and copies ran while one was open for 1% of the time, Pallas kernels for 2%

profile of v9, /device:TPU:1, one launch (start us, length us, event | category | flops | bytes accessed | tf_op | source)
XLA Modules:
  0.0 90.3 jit_solution(600417391885443914)
XLA Ops:
  0.0 1.6 %shard_map.48 = (bf16[32,16,128]{2,1,0:T(8,128)(2,1)}, s32[4]{0:T(128)S(1)}) custom-call(s32[2304]{0:T(1024)} %labels_ref.1, bf16[4,32,32]{2,1,0:T(8,128)(2,1)} %amplitudes_ref.1), custom_call_target="tpu_custom_call" | custom-call | tf_op jit(solution)/shard_map/pallas_call | solution.py:56
  1.6 14.0 %all-to-all-start.1 = ((bf16[32,16,128]{2,1,0:T(8,128)(2,1)}), bf16[32,16,128]{2,1,0:T(8,128)(2,1)S(1)}, u32[]{:S(2)}, u32[]{:S(2)}) async-start(bf16[32,16,128]{2,1,0:T(8,128)(2,1)} %get-tuple-element.45), calls=%async_computation.1 | async-start | bytes 262144 | tf_op jit(solution)/shard_map/all_to_all | solution.py:187
  15.6 0.6 slice.3
  16.9 7.4 %all-to-all-done.1 = bf16[32,16,128]{2,1,0:T(8,128)(2,1)S(1)} async-done(((bf16[32,16,128]{2,1,0:T(8,128)(2,1)}), bf16[32,16,128]{2,1,0:T(8,128)(2,1)S(1)}, u32[]{:S(2)}, u32[]{:S(2)}) %all-to-all-start.1) | async-done | bytes 131104 | tf_op jit(solution)/shard_map/all_to_all | solution.py:187
  24.3 66.0 %conditional.1 = (bf16[3,256,1024]{2,1,0:T(8,128)(2,1)}) conditional(s32[]{:T(128)} %bitcast.62, (bf16[32,16,128]{2,1,0:T(8,128)(2,1)S(1)}, s32[4]{0:T(128)S(1)}, bf16[3,256,768]{2,1,0:T(8,128)(2,1)}, bf16[3,256,1024]{2,1,0:T(8,128)(2,1)}) %tuple.11, (s32[2304]{0:T(1024)}, bf16[4,32,32]{2,1,0:T(8,128)(2,1)}, s32[4]{0:T(128)S(1)}, ...), branch_computations={%region_0.0_spmd, %region_1.0_spmd} | conditional | flops 603979904 | bytes 43028492 | solution.py:199
  24.6 0.2 reshape.34
  24.9 8.8 %collective-permute-start.1 = (bf16[2,32,512]{2,1,0:T(8,128)(2,1)S(1)}, bf16[2,32,512]{2,1,0:T(8,128)(2,1)S(1)}, u32[]{:S(2)}, u32[]{:S(2)}) collective-permute-start(bf16[2,32,512]{2,1,0:T(8,128)(2,1)S(1)} %reshape.34), channel_id=1, source_target_pairs={{0,2},{1,0},{2,1},{3,5},{4,3},{5,4},{6,8},{7,6},{8,7},{9,11},{10,9... | collective-permute-start | bytes 196616 | tf_op jit(solution)/shard_map/cond/branch_0_fun/ppermute | solution.py:21
  33.7 1.9 %collective-permute-start = (bf16[2,32,512]{2,1,0:T(8,128)(2,1)S(1)}, bf16[2,32,512]{2,1,0:T(8,128)(2,1)S(1)}, u32[]{:S(2)}, u32[]{:S(2)}) collective-permute-start(bf16[2,32,512]{2,1,0:T(8,128)(2,1)S(1)} %reshape.34), channel_id=1, source_target_pairs={{0,1},{1,2},{2,0},{3,4},{4,5},{5,3},{6,7},{7,8},{8,6},{9,10},{10,1... | collective-permute-start | bytes 196616 | tf_op jit(solution)/shard_map/cond/branch_0_fun/ppermute | solution.py:21
  35.9 10.0 %collective-permute-done = bf16[2,32,512]{2,1,0:T(8,128)(2,1)S(1)} collective-permute-done((bf16[2,32,512]{2,1,0:T(8,128)(2,1)S(1)}, bf16[2,32,512]{2,1,0:T(8,128)(2,1)S(1)}, u32[]{:S(2)}, u32[]{:S(2)}) %collective-permute-start) | collective-permute-done | bytes 65568 | tf_op jit(solution)/shard_map/cond/branch_0_fun/ppermute | solution.py:21
  46.0 3.2 %collective-permute-start.3 = (bf16[2,96,512]{2,1,0:T(8,128)(2,1)S(1)}, bf16[2,96,512]{2,1,0:T(8,128)(2,1)S(1)}, u32[]{:S(2)}, u32[]{:S(2)}) collective-permute-start(bf16[2,96,512]{2,1,0:T(8,128)(2,1)S(1)} %bitcast.104), channel_id=1, source_target_pairs={{0,21},{3,0},{6,3},{9,6},{12,9},{15,12},{18,15},{21,18},{24,27},{2... | collective-permute-start | bytes 589832 | tf_op jit(solution)/shard_map/cond/branch_0_fun/ppermute | solution.py:144
  49.2 3.8 %collective-permute-start.2 = (bf16[2,96,512]{2,1,0:T(8,128)(2,1)S(1)}, bf16[2,96,512]{2,1,0:T(8,128)(2,1)S(1)}, u32[]{:S(2)}, u32[]{:S(2)}) collective-permute-start(bf16[2,96,512]{2,1,0:T(8,128)(2,1)S(1)} %bitcast.105), channel_id=1, source_target_pairs={{0,3},{3,6},{6,9},{9,12},{12,15},{15,18},{18,21},{21,0},{24,45},{2... | collective-permute-start | bytes 589832 | tf_op jit(solution)/shard_map/cond/branch_0_fun/ppermute | solution.py:144
  53.3 0.8 collective-permute-done.3
  54.2 1.9 %collective-permute-start.5 = (bf16[2,96,512]{2,1,0:T(8,128)(2,1)S(1)}, bf16[2,96,512]{2,1,0:T(8,128)(2,1)S(1)}, u32[]{:S(2)}, u32[]{:S(2)}) collective-permute-start(bf16[2,96,512]{2,1,0:T(8,128)(2,1)S(1)} %collective-permute-done.3), channel_id=1, source_target_pairs={{0,21},{3,0},{6,3},{9,6},{12,9},{15,12},{18,15},{21,18},{24,27},{2... | collective-permute-start | bytes 589832 | tf_op jit(solution)/shard_map/cond/branch_0_fun/ppermute | solution.py:144
  56.1 0.7 collective-permute-done.2
  56.8 5.0 %collective-permute-start.4 = (bf16[2,96,512]{2,1,0:T(8,128)(2,1)S(1)}, bf16[2,96,512]{2,1,0:T(8,128)(2,1)S(1)}, u32[]{:S(2)}, u32[]{:S(2)}) collective-permute-start(bf16[2,96,512]{2,1,0:T(8,128)(2,1)S(1)} %collective-permute-done.2), channel_id=1, source_target_pairs={{0,3},{3,6},{6,9},{9,12},{12,15},{15,18},{18,21},{21,0},{24,45},{2... | collective-permute-start | bytes 589832 | tf_op jit(solution)/shard_map/cond/branch_0_fun/ppermute | solution.py:144
  61.8 0.2 collective-permute-done.5
  62.1 1.9 %collective-permute-start.8 = (bf16[2,96,512]{2,1,0:T(8,128)(2,1)S(1)}, bf16[2,96,512]{2,1,0:T(8,128)(2,1)S(1)}, u32[]{:S(2)}, u32[]{:S(2)}) collective-permute-start(bf16[2,96,512]{2,1,0:T(8,128)(2,1)S(1)} %collective-permute-done.5), channel_id=1, source_target_pairs={{0,18},{3,21},{6,0},{9,3},{12,6},{15,9},{18,12},{21,15},{24,30},{2... | collective-permute-start | bytes 589832 | tf_op jit(solution)/shard_map/cond/branch_0_fun/ppermute | solution.py:144
  64.0 4.0 %collective-permute-start.7 = (bf16[2,96,512]{2,1,0:T(8,128)(2,1)S(1)}, bf16[2,96,512]{2,1,0:T(8,128)(2,1)S(1)}, u32[]{:S(2)}, u32[]{:S(2)}) collective-permute-start(bf16[2,96,512]{2,1,0:T(8,128)(2,1)S(1)} %collective-permute-done.5), channel_id=1, source_target_pairs={{0,21},{3,0},{6,3},{9,6},{12,9},{15,12},{18,15},{21,18},{24,27},{2... | collective-permute-start | bytes 589832 | tf_op jit(solution)/shard_map/cond/branch_0_fun/ppermute | solution.py:144
  68.1 3.5 %collective-permute-start.6 = (bf16[2,96,512]{2,1,0:T(8,128)(2,1)S(1)}, bf16[2,96,512]{2,1,0:T(8,128)(2,1)S(1)}, u32[]{:S(2)}, u32[]{:S(2)}) collective-permute-start(bf16[2,96,512]{2,1,0:T(8,128)(2,1)S(1)} %collective-permute-done.4), channel_id=1, source_target_pairs={{0,3},{3,6},{6,9},{9,12},{12,15},{15,18},{18,21},{21,0},{24,45},{2... | collective-permute-start | bytes 589832 | tf_op jit(solution)/shard_map/cond/branch_0_fun/ppermute | solution.py:144
  71.7 7.1 %collective-permute-done.6 = bf16[2,96,512]{2,1,0:T(8,128)(2,1)S(1)} collective-permute-done((bf16[2,96,512]{2,1,0:T(8,128)(2,1)S(1)}, bf16[2,96,512]{2,1,0:T(8,128)(2,1)S(1)}, u32[]{:S(2)}, u32[]{:S(2)}) %collective-permute-start.6) | collective-permute-done | bytes 196640 | tf_op jit(solution)/shard_map/cond/branch_0_fun/ppermute | solution.py:144
  78.8 6.4 %collective-permute-start.9 = (bf16[2,8,96,512]{3,2,1,0:T(8,128)(2,1)S(1)}, bf16[2,8,96,512]{3,2,1,0:T(8,128)(2,1)S(1)}, u32[]{:S(2)}, u32[]{:S(2)}) collective-permute-start(bf16[2,8,96,512]{3,2,1,0:T(8,128)(2,1)S(1)} %bitcast_dynamic-update-slice_fusion.6), channel_id=1, source_target_pairs={{0,24},{24,0},{1,25},{25,1},{2,26},{26,2},{3,27},{27,3},{4,28},{28... | collective-permute-start | bytes 4718600 | tf_op jit(solution)/shard_map/cond/branch_0_fun/ppermute | solution.py:21
  85.2 2.1 %branch_0_fun.2 = (bf16[3,256,1024]{2,1,0:T(8,128)(2,1)}, bf16[3,256,768]{2,1,0:T(8,128)(2,1)S(1)}, bf16[3,256,512]{2,1,0:T(8,128)(2,1)S(1)}) custom-call(s32[4]{0:T(128)S(1)} %get-tuple-element.26.where_ref, bf16[3,256,768]{2,1,0:T(8,128)(2,1)S(1)} %copy-done.2, bf16[2,768,512]{2,1,0:T(8,128)(2,1)S(1)} %bitcast.96, bf16[3,256,1024]{2,1,0:T(8,128)(2,1)S(1)} %copy-done), custom_call_target="tpu_custom_call" | custom-call | flops 603979776 | bytes 4000000 | tf_op jit(solution)/shard_map/cond/branch_0_fun/pallas_call | solution.py:112
  87.3 0.9 collective-permute-done.9
  88.2 2.0 %branch_0_fun.3 = bf16[3,256,1024]{2,1,0:T(8,128)(2,1)} custom-call(s32[4]{0:T(128)S(1)} %get-tuple-element.26.where_ref, bf16[3,256,768]{2,1,0:T(8,128)(2,1)S(1)} %get-tuple-element.30.integrals_ref, bf16[2,768,512]{2,1,0:T(8,128)(2,1)S(1)} %bitcast.98, bf16[3,256,512]{2,1,0:T(8,128)(2,1)S(1)} %get-tuple-element.31.previous_ref, ...), custom_call_target="tpu_custom_call", output_to_operand_aliasing={{}: (4, {})} | custom-call | tf_op jit(solution)/shard_map/cond/branch_0_fun/pallas_call | solution.py:130
  (25 shorter events, 0.9 us)
Async XLA Ops:
  1.6 22.7 %all-to-all-start.1 = ((bf16[32,16,128]{2,1,0:T(8,128)(2,1)}), bf16[32,16,128]{2,1,0:T(8,128)(2,1)S(1)}, u32[]{:S(2)}, u32[]{:S(2)}) async-start(bf16[32,16,128]{2,1,0:T(8,128)(2,1)} %get-tuple-element.45), calls=%async_computation.1 | async-start | bytes 262144 | tf_op jit(solution)/shard_map/all_to_all | solution.py:187
  24.9 21.1 %collective-permute-start.1 = (bf16[2,32,512]{2,1,0:T(8,128)(2,1)S(1)}, bf16[2,32,512]{2,1,0:T(8,128)(2,1)S(1)}, u32[]{:S(2)}, u32[]{:S(2)}) collective-permute-start(bf16[2,32,512]{2,1,0:T(8,128)(2,1)S(1)} %reshape.34), channel_id=1, source_target_pairs={{0,2},{1,0},{2,1},{3,5},{4,3},{5,4},{6,8},{7,6},{8,7},{9,11},{10,9... | collective-permute-start | bytes 196616 | tf_op jit(solution)/shard_map/cond/branch_0_fun/ppermute | solution.py:21
  33.7 12.3 %collective-permute-start = (bf16[2,32,512]{2,1,0:T(8,128)(2,1)S(1)}, bf16[2,32,512]{2,1,0:T(8,128)(2,1)S(1)}, u32[]{:S(2)}, u32[]{:S(2)}) collective-permute-start(bf16[2,32,512]{2,1,0:T(8,128)(2,1)S(1)} %reshape.34), channel_id=1, source_target_pairs={{0,1},{1,2},{2,0},{3,4},{4,5},{5,3},{6,7},{7,8},{8,6},{9,10},{10,1... | collective-permute-start | bytes 196616 | tf_op jit(solution)/shard_map/cond/branch_0_fun/ppermute | solution.py:21
  46.0 8.1 %collective-permute-start.3 = (bf16[2,96,512]{2,1,0:T(8,128)(2,1)S(1)}, bf16[2,96,512]{2,1,0:T(8,128)(2,1)S(1)}, u32[]{:S(2)}, u32[]{:S(2)}) collective-permute-start(bf16[2,96,512]{2,1,0:T(8,128)(2,1)S(1)} %bitcast.104), channel_id=1, source_target_pairs={{0,21},{3,0},{6,3},{9,6},{12,9},{15,12},{18,15},{21,18},{24,27},{2... | collective-permute-start | bytes 589832 | tf_op jit(solution)/shard_map/cond/branch_0_fun/ppermute | solution.py:144
  49.2 7.6 %collective-permute-start.2 = (bf16[2,96,512]{2,1,0:T(8,128)(2,1)S(1)}, bf16[2,96,512]{2,1,0:T(8,128)(2,1)S(1)}, u32[]{:S(2)}, u32[]{:S(2)}) collective-permute-start(bf16[2,96,512]{2,1,0:T(8,128)(2,1)S(1)} %bitcast.105), channel_id=1, source_target_pairs={{0,3},{3,6},{6,9},{9,12},{12,15},{15,18},{18,21},{21,0},{24,45},{2... | collective-permute-start | bytes 589832 | tf_op jit(solution)/shard_map/cond/branch_0_fun/ppermute | solution.py:144
  53.2 32.0 %copy-start = (bf16[3,256,1024]{2,1,0:T(8,128)(2,1)S(1)}, bf16[3,256,1024]{2,1,0:T(8,128)(2,1)}, u32[]{:S(2)}) copy-start(bf16[3,256,1024]{2,1,0:T(8,128)(2,1)} %get-tuple-element.29.previous_ref) | copy-start | bytes 4718596 | tf_op jit(solution)/shard_map/cond
  53.3 32.0 %copy-start.2 = (bf16[3,256,768]{2,1,0:T(8,128)(2,1)S(1)}, bf16[3,256,768]{2,1,0:T(8,128)(2,1)}, u32[]{:S(2)}) copy-start(bf16[3,256,768]{2,1,0:T(8,128)(2,1)} %get-tuple-element.27.integrals_ref) | copy-start | bytes 3538948 | tf_op jit(solution)/shard_map/cond
  54.2 7.9 %collective-permute-start.5 = (bf16[2,96,512]{2,1,0:T(8,128)(2,1)S(1)}, bf16[2,96,512]{2,1,0:T(8,128)(2,1)S(1)}, u32[]{:S(2)}, u32[]{:S(2)}) collective-permute-start(bf16[2,96,512]{2,1,0:T(8,128)(2,1)S(1)} %collective-permute-done.3), channel_id=1, source_target_pairs={{0,21},{3,0},{6,3},{9,6},{12,9},{15,12},{18,15},{21,18},{24,27},{2... | collective-permute-start | bytes 589832 | tf_op jit(solution)/shard_map/cond/branch_0_fun/ppermute | solution.py:144
  56.8 11.3 %collective-permute-start.4 = (bf16[2,96,512]{2,1,0:T(8,128)(2,1)S(1)}, bf16[2,96,512]{2,1,0:T(8,128)(2,1)S(1)}, u32[]{:S(2)}, u32[]{:S(2)}) collective-permute-start(bf16[2,96,512]{2,1,0:T(8,128)(2,1)S(1)} %collective-permute-done.2), channel_id=1, source_target_pairs={{0,3},{3,6},{6,9},{9,12},{12,15},{15,18},{18,21},{21,0},{24,45},{2... | collective-permute-start | bytes 589832 | tf_op jit(solution)/shard_map/cond/branch_0_fun/ppermute | solution.py:144
  62.1 16.7 %collective-permute-start.8 = (bf16[2,96,512]{2,1,0:T(8,128)(2,1)S(1)}, bf16[2,96,512]{2,1,0:T(8,128)(2,1)S(1)}, u32[]{:S(2)}, u32[]{:S(2)}) collective-permute-start(bf16[2,96,512]{2,1,0:T(8,128)(2,1)S(1)} %collective-permute-done.5), channel_id=1, source_target_pairs={{0,18},{3,21},{6,0},{9,3},{12,6},{15,9},{18,12},{21,15},{24,30},{2... | collective-permute-start | bytes 589832 | tf_op jit(solution)/shard_map/cond/branch_0_fun/ppermute | solution.py:144
  64.0 14.8 %collective-permute-start.7 = (bf16[2,96,512]{2,1,0:T(8,128)(2,1)S(1)}, bf16[2,96,512]{2,1,0:T(8,128)(2,1)S(1)}, u32[]{:S(2)}, u32[]{:S(2)}) collective-permute-start(bf16[2,96,512]{2,1,0:T(8,128)(2,1)S(1)} %collective-permute-done.5), channel_id=1, source_target_pairs={{0,21},{3,0},{6,3},{9,6},{12,9},{15,12},{18,15},{21,18},{24,27},{2... | collective-permute-start | bytes 589832 | tf_op jit(solution)/shard_map/cond/branch_0_fun/ppermute | solution.py:144
  68.1 10.7 %collective-permute-start.6 = (bf16[2,96,512]{2,1,0:T(8,128)(2,1)S(1)}, bf16[2,96,512]{2,1,0:T(8,128)(2,1)S(1)}, u32[]{:S(2)}, u32[]{:S(2)}) collective-permute-start(bf16[2,96,512]{2,1,0:T(8,128)(2,1)S(1)} %collective-permute-done.4), channel_id=1, source_target_pairs={{0,3},{3,6},{6,9},{9,12},{12,15},{15,18},{18,21},{21,0},{24,45},{2... | collective-permute-start | bytes 589832 | tf_op jit(solution)/shard_map/cond/branch_0_fun/ppermute | solution.py:144
  78.8 9.4 %collective-permute-start.9 = (bf16[2,8,96,512]{3,2,1,0:T(8,128)(2,1)S(1)}, bf16[2,8,96,512]{3,2,1,0:T(8,128)(2,1)S(1)}, u32[]{:S(2)}, u32[]{:S(2)}) collective-permute-start(bf16[2,8,96,512]{3,2,1,0:T(8,128)(2,1)S(1)} %bitcast_dynamic-update-slice_fusion.6), channel_id=1, source_target_pairs={{0,24},{24,0},{1,25},{25,1},{2,26},{26,2},{3,27},{27,3},{4,28},{28... | collective-permute-start | bytes 4718600 | tf_op jit(solution)/shard_map/cond/branch_0_fun/ppermute | solution.py:21
